TPU v7x, 32 devices: a whole 2x2x4 slice. The times are simulated.
32 devices in a mesh: blk: 8 (over z, x), narrow: 4 (over y, core).
Axes of the slice: x: 2, y: 2, z: 4, core: 2. Of those that a mesh axis runs over, the one named last changes fastest.
Arguments:
- query_ids: int32 [2, 32, 32], P(None, ('blk', 'narrow')), may hold values from 0 to 30719, as said below
- passage_ids: int32 [2, 32, 512], P(None, ('blk', 'narrow')), may hold values from 0 to 30719, as said below
- passage_len: int32 [2, 32], P(None, ('blk', 'narrow')), may hold values from 1 to 512, 8192 in all within a row
- positives: int32 [2, 4, 8], P(None, 'narrow'), may hold values from 0 to 7
- domains: int32 [2, 4, 8], P(None, 'narrow'), may hold values from 0 to 3
- table: float32 [30720, 768], P(('blk', 'narrow')), may hold values from -0.3125 to 0.3125
- table_m: float32 [30720, 768], P(('blk', 'narrow')), may hold values from -5.722046e-06 to 5.722046e-06
- table_v: float32 [30720, 768], P(('blk', 'narrow')), may hold values from 4.1702596e-12 to 1.6681038e-11
- pos_table: float32 [512, 768], P(None, 'narrow'), may hold values from -0.3125 to 0.3125
- pos_m: float32 [512, 768], P(None, 'narrow'), may hold values from -5.722046e-06 to 5.722046e-06
- pos_v: float32 [512, 768], P(None, 'narrow'), may hold values from 4.1702596e-12 to 1.6681038e-11
- vector: float32 [1, 10752], P(None, 'narrow')
- vector_m: float32 [1, 10752], P(None, 'narrow'), may hold values from -2.2888184e-05 to 2.2888184e-05
- vector_v: float32 [1, 10752], P(None, 'narrow'), may hold values from 6.736573e-11 to 2.6946292e-10
- w_qkv: float32 [768, 2304], P(None, 'narrow'), may hold values from -0.21875 to 0.21875
- m_qkv: float32 [768, 2304], P(None, 'narrow'), may hold values from -5.340576e-05 to 5.340576e-05
- w_attn: float32 [768, 768], P(None, 'narrow'), may hold values from -3.5 to 3.5
- m_attn: float32 [768, 768], P(None, 'narrow'), may hold values from -5.340576e-05 to 5.340576e-05
- w_in: float32 [768, 3072], P(None, 'narrow'), may hold values from -0.21875 to 0.21875
- m_in: float32 [768, 3072], P(None, 'narrow'), may hold values from -5.340576e-05 to 5.340576e-05
- w_out: float32 [768, 3072], P(None, 'narrow'), may hold values from -0.109375 to 0.109375
- m_out: float32 [768, 3072], P(None, 'narrow'), may hold values from -5.340576e-05 to 5.340576e-05
- w_proj: float32 [128, 768], P(None, 'narrow'), may hold values from -0.21875 to 0.21875
- m_proj: float32 [128, 768], P(None, 'narrow'), may hold values from -5.340576e-05 to 5.340576e-05
Outputs:
- loss: float32 [], replicated
- grad_norm: float32 [], replicated
- table_new: float32 [30720, 768], P(('blk', 'narrow'))
- table_m_new: float32 [30720, 768], P(('blk', 'narrow'))
- table_v_new: float32 [30720, 768], P(('blk', 'narrow'))
- pos_new: float32 [512, 768], P(None, 'narrow')
- pos_m_new: float32 [512, 768], P(None, 'narrow')
- pos_v_new: float32 [512, 768], P(None, 'narrow')
- vector_new: float32 [1, 10752], P(None, 'narrow')
- vector_m_new: float32 [1, 10752], P(None, 'narrow')
- vector_v_new: float32 [1, 10752], P(None, 'narrow')
- qkv_new: float32 [768, 2304], P(None, 'narrow')
- qkv_mom: float32 [768, 2304], P(None, 'narrow')
- attn_new: float32 [768, 768], P(None, 'narrow')
- attn_mom: float32 [768, 768], P(None, 'narrow')
- in_new: float32 [768, 3072], P(None, 'narrow')
- in_mom: float32 [768, 3072], P(None, 'narrow')
- out_new: float32 [768, 3072], P(None, 'narrow')
- out_mom: float32 [768, 3072], P(None, 'narrow')
- proj_new: float32 [128, 768], P(None, 'narrow')
- proj_mom: float32 [128, 768], P(None, 'narrow')
- attn_bias_grad: float32 [1, 768], P(None, 'narrow')
Inputs may be any that keep to these rules, and one draw needn't show every extreme that they name: `query_ids`: counting all token slots of one device together (its query and passage of every micro-batch, unused slots too), at most 36 have ids in any one block of 960 consecutive ids starting at a multiple of 960, and exactly 36 in some block. `passage_ids`: the same bound of 36 holds for these slots together with the query slots of the same device. `passage_len`: in each micro-batch the longest passage has exactly 512 tokens.
All inputs are finite; a program needn't handle non-finite values. No bound on the sum of `passage_len` on one device may be relied on, other than what follows from the above.
Results may differ from a plain program's by a relative error of at most 0.015.
Values may be sent and summed in bfloat16 or wider, within the bound.
No kernel may reach another device: no remote copies, remote signals or barrier semaphores. Data moves between devices by JAX's collectives and lax.ppermute only.
A program may use at most 384 MiB of HBM per device.

v0:
```python
import jax
import jax.numpy as jnp
from jax import lax
from jax.sharding import PartitionSpec as P

D = 768
HEADS = 12
HDIM = 64
FF = 3072
STEP = 10


highest = lax.Precision.HIGHEST
norm_eps = 1e-12
smoothing = 0.1
masked = -1e30
newton_one = 3.4445
newton_two = -4.775
newton_three = 2.0315
muon_rate = 0.1
attn_rate = 1.0
muon_moment = 0.95
weight_decay = 0.01
adam_rate = 0.02
vector_rate = 0.25
beta_one = 0.9
beta_two = 0.95
adam_eps = 1e-08
clip_limit = 0.05


def combined_all(value, axis, join):
    pieces = jax.tree.map(lambda part: lax.all_gather(part, axis), value)
    head = jax.tree.map(lambda part: part[0], pieces)
    tail = jax.tree.map(lambda part: part[1:], pieces)
    running, _ = lax.scan(lambda running, slab: (join(running, slab), None), head, tail)
    return running


def to_bfloat(values):
    return lax.optimization_barrier(values.astype(jnp.bfloat16)).astype(jnp.float32)


def build_rounders():

    def value_plain(values):
        return to_bfloat(values)

    def grad_plain(values):
        return values

    def value_keep(values):
        return (to_bfloat(values), None)

    def value_pass(kept, grad):
        return (grad,)

    def grad_keep(values):
        return (values, None)

    def grad_lower(kept, grad):
        return (to_bfloat(grad),)

    value_round = jax.custom_vjp(value_plain)
    grad_round = jax.custom_vjp(grad_plain)
    value_round.defvjp(value_keep, value_pass)
    grad_round.defvjp(grad_keep, grad_lower)
    return (value_round, grad_round)


def low_value(values):
    return build_rounders()[0](values)


def low_grad(values):
    return build_rounders()[1](values)


def product(operand, other):
    return jnp.dot(operand, other, precision=highest, preferred_element_type=jnp.float32)


def single_pass(operand, other):
    return jnp.dot(operand, other, preferred_element_type=jnp.float32)


def rounded(values):
    return low_value(low_grad(values))


def layer_norm(values, norm_gain, norm_shift):
    centred = values - jnp.mean(values, axis=-1, keepdims=True)
    spread = jnp.mean(centred * centred, axis=-1, keepdims=True)
    return centred * lax.rsqrt(spread + norm_eps) * norm_gain + norm_shift


def encode(token_rows, positions, weights, vector, usable):
    w_qkv, w_attn, w_in, w_out, w_proj = weights
    length = token_rows.shape[0]
    bounds = [
        0,
        D,
        2 * D,
        3 * D,
        4 * D,
        5 * D,
        6 * D,
        7 * D,
        7 * D + FF,
        8 * D + FF,
        9 * D + FF,
        10 * D + FF,
    ]
    pieces = [vector[bounds[index] : bounds[index + 1]] for index in range(11)]
    normed = layer_norm(token_rows + positions, pieces[0], pieces[1])
    offset_qkv = jnp.concatenate([pieces[2], jnp.zeros_like(pieces[2]), pieces[3]])
    qkv_rows = rounded(single_pass(rounded(normed), w_qkv) + offset_qkv).reshape(
        length, 3, HEADS, HDIM
    )
    scores = low_grad(jnp.einsum("qhd,khd->hqk", qkv_rows[:, 0], qkv_rows[:, 1]) * HDIM ** (-0.5))
    scores = jnp.where(usable[None, None, :], scores, masked)
    exponent = jnp.exp(scores - jnp.max(scores, axis=-1, keepdims=True))
    attend = exponent / jnp.sum(exponent, axis=-1, keepdims=True)
    context = jnp.einsum("hqk,khd->qhd", low_value(attend), qkv_rows[:, 2]).reshape(length, D)
    hidden = layer_norm(
        normed + low_grad(single_pass(rounded(context), w_attn)) + pieces[4], pieces[5], pieces[6]
    )
    widened = jax.nn.gelu(
        low_grad(single_pass(rounded(hidden), w_in)) + pieces[7], approximate=False
    )
    output_rows = layer_norm(
        hidden + low_grad(single_pass(rounded(widened), w_out.T)) + pieces[8], pieces[9], pieces[10]
    )
    embedded = low_grad(single_pass(rounded(output_rows), w_proj.T))
    return rounded(
        embedded * lax.rsqrt(jnp.sum(embedded * embedded, axis=-1, keepdims=True) + 1e-06)
    )


def combine_totals(first, second):
    summit = jnp.maximum(first[0], second[0])
    return (
        summit,
        first[1] * jnp.exp(first[0] - summit) + second[1] * jnp.exp(second[0] - summit),
        first[2] + second[2],
    )


def adam_step(weight, first, second, gradient, rate):
    first_new = beta_one * first + (1.0 - beta_one) * gradient
    second_new = beta_two * second + (1.0 - beta_two) * gradient * gradient
    update = (
        first_new
        / (1.0 - beta_one**STEP)
        / (jnp.sqrt(second_new / (1.0 - beta_two**STEP)) + adam_eps)
    )
    return (weight - rate * (update + weight_decay * weight), first_new, second_new)


def gram_blocks(members, narrow):
    short_side = members[0].shape[0]
    proj_rows = members[4].shape[0]
    padded = jnp.pad(members[4], ((0, short_side - proj_rows), (0, 0)))
    blocks_list = [
        product(
            lax.slice_in_dim(member, 0, short_side // narrow * lax.axis_size("narrow"), axis=0),
            member.T,
        )
        for member in members[:4]
    ]
    blocks_list.append(
        product(
            lax.slice_in_dim(padded, 0, short_side // narrow * lax.axis_size("narrow"), axis=0),
            members[4].T,
        )
    )
    own_rows = lax.psum_scatter(
        jnp.concatenate(blocks_list, axis=1), "narrow", scatter_dimension=0, tiled=True
    )
    complete = lax.all_gather(own_rows, "narrow", axis=0, tiled=True)
    grams = [complete[:, index * short_side : (index + 1) * short_side] for index in range(4)]
    return grams + [complete[:proj_rows, 4 * short_side :]]


def newton_turn(gram, ortho):
    return newton_one * ortho + product(
        newton_two * gram + newton_three * product(gram, gram), ortho
    )


def body(
    query_ids,
    passage_ids,
    passage_len,
    positives,
    domains,
    table,
    table_m,
    table_v,
    pos_table,
    pos_m,
    pos_v,
    vector,
    vector_m,
    vector_v,
    w_qkv,
    m_qkv,
    w_attn,
    m_attn,
    w_in,
    m_in,
    w_out,
    m_out,
    w_proj,
    m_proj,
):
    blocks = lax.axis_size("blk")
    narrow = lax.axis_size("narrow")
    myself = lax.axis_index("blk")
    shard_rows = table.shape[0]
    micro_count = query_ids.shape[0]
    query_len = query_ids.shape[2]
    passage_span = passage_ids.shape[2]
    pair_len = query_len + passage_span
    gathered = (
        lax.all_gather(w_qkv.astype(jnp.bfloat16), "narrow", axis=1, tiled=True),
        lax.all_gather(w_attn.astype(jnp.bfloat16), "narrow", axis=1, tiled=True),
        lax.all_gather(w_in.astype(jnp.bfloat16), "narrow", axis=1, tiled=True),
        lax.all_gather(w_out.astype(jnp.bfloat16), "narrow", axis=1, tiled=True),
        lax.all_gather(w_proj.astype(jnp.bfloat16), "narrow", axis=1, tiled=True),
        lax.all_gather(pos_table.astype(jnp.bfloat16), "narrow", axis=1, tiled=True),
        lax.all_gather(vector.astype(jnp.bfloat16), "narrow", axis=1, tiled=True),
    )
    complete = [member.astype(jnp.float32) for member in gathered]
    layer = tuple(complete[:5])
    all_tokens = jnp.concatenate(
        [
            jnp.concatenate([query_ids[micro, 0], passage_ids[micro, 0]])
            for micro in range(micro_count)
        ]
    )
    whole_table = lax.all_gather(table.astype(jnp.bfloat16), ("blk", "narrow"), axis=0, tiled=True)
    fetched_rows = whole_table[all_tokens].astype(jnp.float32)
    positions = jnp.arange(passage_span)
    layer_grads = [jnp.zeros_like(member) for member in complete]
    row_list = []
    loss_part = jnp.zeros((), jnp.float32)

    def query_side(token_rows, pos_all, weights, vector_row):
        return encode(
            token_rows,
            pos_all[:query_len],
            weights,
            vector_row[0],
            jnp.ones((query_len,), jnp.bool_),
        )

    for micro in range(micro_count):
        usable = positions < passage_len[micro, 0]

        def passage_side(token_rows, pos_all, weights, vector_row):
            return encode(token_rows, pos_all, weights, vector_row[0], usable)

        start = micro * pair_len
        query_rows = fetched_rows[start : start + query_len]
        passage_rows = fetched_rows[start + query_len : start + pair_len]
        query_vecs, query_back = jax.vjp(query_side, query_rows, complete[5], layer, complete[6])
        passage_vecs, passage_back = jax.vjp(
            passage_side, passage_rows, complete[5], layer, complete[6]
        )
        cycle = lax.all_gather(query_vecs.astype(jnp.bfloat16)[None], "blk", axis=0, tiled=True)
        passage_low = passage_vecs.astype(jnp.bfloat16)
        sims = jnp.einsum("bik,jk->bij", cycle, passage_low, preferred_element_type=jnp.float32)
        scaled = jnp.where(usable[None, None, :], sims / smoothing, masked)
        summit = jnp.max(scaled, axis=-1, keepdims=True)
        expvals = jnp.exp(scaled - summit)
        totals = jnp.sum(expvals, axis=-1, keepdims=True)
        scores = jnp.sum(smoothing * (summit[..., 0] + jnp.log(totals[..., 0])), axis=-1)
        labels = domains[micro, 0]
        targets = positives[micro, 0]
        allowed = labels[targets] == labels[myself]
        hits = targets == myself
        peak, mass, matched = combined_all(
            (
                jnp.where(allowed, scores, masked),
                allowed.astype(jnp.float32),
                jnp.where(hits, scores, 0.0),
            ),
            "blk",
            combine_totals,
        )
        log_total = peak + jnp.log(mass)
        loss_part = loss_part + log_total[myself] - matched[myself]
        d_scores = jnp.where(allowed, jnp.exp(scores - log_total), 0.0) - hits.astype(jnp.float32)
        d_sims = (d_scores[:, None, None] * (expvals / totals)).astype(jnp.bfloat16)
        d_passage = jnp.einsum("bij,bik->jk", d_sims, cycle, preferred_element_type=jnp.float32)
        flat_sims = d_sims.reshape(-1, passage_span)
        d_query = lax.psum_scatter(
            jnp.dot(
                lax.slice_in_dim(flat_sims, 0, query_len * lax.axis_size("blk"), axis=0),
                passage_low,
                preferred_element_type=jnp.float32,
            ),
            "blk",
            scatter_dimension=0,
            tiled=True,
        )
        for pulled in (query_back(d_query), passage_back(d_passage)):
            row_list.append(pulled[0])
            layer_grads[5] = layer_grads[5] + pulled[1]
            for index in range(5):
                layer_grads[index] = layer_grads[index] + pulled[2][index]
            layer_grads[6] = layer_grads[6] + pulled[3]
    all_rows = jnp.concatenate(row_list)
    inside = (all_tokens >= 0) & (all_tokens < shard_rows * lax.axis_size(("blk", "narrow")))
    table_grad = lax.psum_scatter(
        jax.ops.segment_sum(
            jnp.where(inside[:, None], all_rows, 0.0),
            jnp.where(inside, all_tokens, 0),
            num_segments=shard_rows * lax.axis_size(("blk", "narrow")),
        ),
        ("blk", "narrow"),
        scatter_dimension=0,
        tiled=True,
    )
    bias_part = layer_grads[6][:, 4 * D : 5 * D]
    shards = (
        lax.psum_scatter(layer_grads[0], "narrow", scatter_dimension=1, tiled=True),
        lax.psum_scatter(layer_grads[1], "narrow", scatter_dimension=1, tiled=True),
        lax.psum_scatter(layer_grads[2], "narrow", scatter_dimension=1, tiled=True),
        lax.psum_scatter(layer_grads[3], "narrow", scatter_dimension=1, tiled=True),
        lax.psum_scatter(layer_grads[4], "narrow", scatter_dimension=1, tiled=True),
        lax.psum_scatter(layer_grads[5], "narrow", scatter_dimension=1, tiled=True),
        lax.psum_scatter(layer_grads[6], "narrow", scatter_dimension=1, tiled=True),
        lax.psum_scatter(bias_part, "narrow", scatter_dimension=1, tiled=True),
    )
    shards = lax.psum(
        (shards[0], shards[1], shards[2], shards[3], shards[4], shards[5], shards[6], shards[7]),
        "blk",
    )
    local_square = sum((jnp.sum(member * member) for member in shards[:7])) / blocks + jnp.sum(
        table_grad * table_grad
    )
    total_square, loss = lax.psum((local_square, loss_part), ("blk", "narrow"))
    grad_norm = jnp.sqrt(total_square)
    factor = jnp.minimum(1.0, clip_limit / (grad_norm + 1e-06))
    attn_bias_grad = factor * shards[7]
    table_new, table_m_new, table_v_new = adam_step(
        table, table_m, table_v, factor * table_grad, adam_rate
    )
    pos_new, pos_m_new, pos_v_new = adam_step(
        pos_table, pos_m, pos_v, factor * shards[5], adam_rate
    )
    vector_new, vector_m_new, vector_v_new = adam_step(
        vector, vector_m, vector_v, factor * shards[6], vector_rate
    )
    masters = (w_qkv, w_attn, w_in, w_out, w_proj)
    rates = (muon_rate, attn_rate, muon_rate, muon_rate, muon_rate)
    moments = [
        muon_moment * old + factor * shards[index]
        for index, old in enumerate((m_qkv, m_attn, m_in, m_out, m_proj))
    ]
    grams = gram_blocks(moments, narrow)
    scales = [1.0 / (jnp.sqrt(jnp.trace(gram)) + 1e-07) for gram in grams]
    orthos = [scale * moment for scale, moment in zip(scales, moments)]
    grams = [scale * scale * gram for scale, gram in zip(scales, grams)]
    for iteration in range(5):
        if iteration > 0:
            grams = gram_blocks(orthos, narrow)
        orthos = [newton_turn(gram, ortho) for gram, ortho in zip(grams, orthos)]
    updated = []
    for weight, ortho, rate in zip(masters, orthos, rates):
        long_side = max(weight.shape[0], weight.shape[1] * narrow)
        updated.append(weight - rate * (0.2 * long_side**0.5 * ortho + weight_decay * weight))
    return (
        loss,
        grad_norm,
        table_new,
        table_m_new,
        table_v_new,
        pos_new,
        pos_m_new,
        pos_v_new,
        vector_new,
        vector_m_new,
        vector_v_new,
        updated[0],
        moments[0],
        updated[1],
        moments[1],
        updated[2],
        moments[2],
        updated[3],
        moments[3],
        updated[4],
        moments[4],
        attn_bias_grad,
    )


def solution(mesh):
    in_specs = (
        P(None, ("blk", "narrow"), None),
        P(None, ("blk", "narrow"), None),
        P(None, ("blk", "narrow")),
        P(None, "narrow", None),
        P(None, "narrow", None),
        P(("blk", "narrow"), None),
        P(("blk", "narrow"), None),
        P(("blk", "narrow"), None),
        P(None, "narrow"),
        P(None, "narrow"),
        P(None, "narrow"),
        P(None, "narrow"),
        P(None, "narrow"),
        P(None, "narrow"),
        P(None, "narrow"),
        P(None, "narrow"),
        P(None, "narrow"),
        P(None, "narrow"),
        P(None, "narrow"),
        P(None, "narrow"),
        P(None, "narrow"),
        P(None, "narrow"),
        P(None, "narrow"),
        P(None, "narrow"),
    )
    out_specs = (
        P(),
        P(),
        P(("blk", "narrow"), None),
        P(("blk", "narrow"), None),
        P(("blk", "narrow"), None),
        P(None, "narrow"),
        P(None, "narrow"),
        P(None, "narrow"),
        P(None, "narrow"),
        P(None, "narrow"),
        P(None, "narrow"),
        P(None, "narrow"),
        P(None, "narrow"),
        P(None, "narrow"),
        P(None, "narrow"),
        P(None, "narrow"),
        P(None, "narrow"),
        P(None, "narrow"),
        P(None, "narrow"),
        P(None, "narrow"),
        P(None, "narrow"),
        P(None, "narrow"),
    )
    return jax.shard_map(body, mesh=mesh, in_specs=in_specs, out_specs=out_specs, check_vma=False)
```

profile of v0, /device:TPU:0, one launch (start us, length us, event | category | flops | bytes accessed | tf_op | source)
XLA Modules:
  0.0 3677.0 jit_solution(1685426861693208320)
XLA Ops:
  31.1 21.6 all-gather.6
  55.1 16.2 all-gather.3
  96.0 178.7 %all-gather.19.cloned.1.call-done = bf16[30720,768]{1,0:T(8,128)(2,1)} async-done(((bf16[960,768]{1,0:T(8,128)(2,1)}), bf16[30720,768]{1,0:T(8,128)(2,1)}) %all-gather.19.cloned.1.call-update) | async-done | bytes 47185936 | tf_op jit(solution)/shard_map/all_gather | solution.py:242
  340.1 24.8 all-gather.25.cloned.1.call-done
  437.0 32.7 all-gather.1
  469.7 32.5 all-gather
  512.4 33.3 multiply_convert_fusion
  559.9 20.3 all-gather.7
  581.3 16.1 all-gather.4
  598.0 18.2 all-gather.2
  733.8 20.3 convert_reduce_fusion
  822.9 36.9 %reduce-scatter.35.cloned.1.call-done = f32[32,128]{1,0:T(8,128)} async-done(((f32[256,128]{1,0:T(8,128)}), f32[32,128]{1,0:T(8,128)}) %reduce-scatter.35.cloned.1.call-update) | async-done | bytes 16400 | tf_op jit(solution)/shard_map/reduce_scatter | solution.py:298
  861.2 61.9 %reduce-scatter.33.cloned.1.call-done = f32[32,128]{1,0:T(8,128)} async-done(((f32[256,128]{1,0:T(8,128)}), f32[32,128]{1,0:T(8,128)}) %reduce-scatter.33.cloned.1.call-update) | async-done | bytes 16400 | tf_op jit(solution)/shard_map/reduce_scatter | solution.py:298
  1060.1 66.3 %reduce-scatter.37.cloned.1.call-done = f32[768,576]{0,1:T(8,128)} async-done(((f32[768,2304]{0,1:T(8,128)}), f32[768,576]{0,1:T(8,128)}) %reduce-scatter.37.cloned.1.call-update) | async-done | bytes 1769488 | tf_op jit(solution)/shard_map/reduce_scatter | solution.py:328
  1126.4 81.1 %reduce-scatter.41.cloned.1.call-done = f32[768,768]{1,0:T(8,128)} async-done(((f32[768,3072]{1,0:T(8,128)}), f32[768,768]{1,0:T(8,128)}) %reduce-scatter.41.cloned.1.call-update) | async-done | bytes 2359312 | tf_op jit(solution)/shard_map/reduce_scatter | solution.py:330
  1207.4 81.1 %reduce-scatter.43.cloned.1.call-done = f32[768,768]{1,0:T(8,128)} async-done(((f32[768,3072]{1,0:T(8,128)}), f32[768,768]{1,0:T(8,128)}) %reduce-scatter.43.cloned.1.call-update) | async-done | bytes 2359312 | tf_op jit(solution)/shard_map/reduce_scatter | solution.py:331
  1292.1 30.3 broadcast_in_dim.399
  1322.3 141.2 %scatter_fusion = f32[30720,768]{1,0:T(8,128)} fusion(f32[30720,768]{1,0:T(8,128)} %broadcast_in_dim.399, s32[1088]{0:T(1024)S(1)} %copy-done.285, f32[1088,768]{1,0:T(8,128)S(1)} %maximum_select_fusion), kind=kCustom, calls=%fused_computation.3 | custom fusion | flops 835584 | bytes 10031360 | tf_op jit(solution)/shard_map/scatter-add | solution.py:317
  1472.0 38.2 %all-reduce.64 = (f32[1,2688]{1,0:T(1,128)S(1)}, f32[1,192]{1,0:T(1,128)}) all-reduce(f32[1,2688]{1,0:T(1,128)S(1)} %copy.253, f32[1,192]{1,0:T(1,128)S(1)} %copy.265), channel_id=1, replica_groups=mesh['blk'=8,'narrow'=4] {'blk'}, use_global_device_ids=true, to_apply=%region_148.149 | all-reduce | flops 2880 | bytes 23040 | tf_op jit(solution)/shard_map/psum | solution.py:337
  1510.9 114.4 %all-reduce.68.cloned.1.call-done = (f32[768,576]{0,1:T(8,128)}, f32[768,192]{0,1:T(8,128)}, f32[768,768]{1,0:T(8,128)}, f32[768,768]{1,0:T(8,128)}, f32[128,192]{0,1:T(8,128)}, /*index=5*/f32[512,192]{0,1:T(8,128)}) async-done(((f32[768,576]{0,1:T(8,128)}, f32[768,192]{0,1:T(8,128)}, f32[768,768]{1,0:T(8,128)}, f32[768,768]{1,0:T(8,128)}, f32[128,192]{0,1:T(8,128)}, /*index=5*/f32[512,192]{0,1:T(8,128)}), ...) | async-done | bytes 7569424 | tf_op jit(solution)/shard_map/psum | solution.py:337
  1639.8 771.5 %reduce-scatter.47.cloned.1.call-done = f32[960,768]{1,0:T(8,128)} async-done(((f32[30720,768]{1,0:T(8,128)}), f32[960,768]{1,0:T(8,128)}) %reduce-scatter.47.cloned.1.call-update) | async-done | bytes 2949136 | tf_op jit(solution)/shard_map/reduce_scatter | solution.py:316
  2415.1 40.2 %all-reduce.63 = (f32[]{:T(128)}, f32[]{:T(128)}) all-reduce(f32[]{:T(128)} %bitcast.75, f32[]{:T(128)S(6)} %add.1101), channel_id=1, replica_groups=mesh['blk'=8,'narrow'=4] {'blk','narrow'}, use_global_device_ids=true, to_apply=%region_46.47 | all-reduce | flops 2 | bytes 16 | tf_op jit(solution)/shard_map/psum | solution.py:344
  2501.8 80.9 %reduce-scatter.53.cloned.1.call-done = f32[192,3200]{1,0:T(8,128)} async-done(((f32[768,3200]{1,0:T(8,128)}), f32[192,3200]{1,0:T(8,128)}) %reduce-scatter.53.cloned.1.call-update) | async-done | bytes 2457616 | tf_op jit(solution)/shard_map/reduce_scatter | solution.py:177
  2582.9 67.9 %all-gather.29.cloned.1.call-done = f32[768,3200]{1,0:T(8,128)} async-done(((f32[192,3200]{1,0:T(8,128)}), f32[768,3200]{1,0:T(8,128)}) %all-gather.29.cloned.1.call-update) | async-done | bytes 9830416 | tf_op jit(solution)/shard_map/all_gather | solution.py:180
  2749.2 81.1 %reduce-scatter.55.cloned.1.call-done = f32[192,3200]{1,0:T(8,128)} async-done(((f32[768,3200]{1,0:T(8,128)}), f32[192,3200]{1,0:T(8,128)}) %reduce-scatter.55.cloned.1.call-update) | async-done | bytes 2457616 | tf_op jit(solution)/shard_map/reduce_scatter | solution.py:177
  2830.8 67.7 %all-gather.31.cloned.1.call-done = f32[768,3200]{1,0:T(8,128)} async-done(((f32[192,3200]{1,0:T(8,128)}), f32[768,3200]{1,0:T(8,128)}) %all-gather.31.cloned.1.call-update) | async-done | bytes 9830416 | tf_op jit(solution)/shard_map/all_gather | solution.py:180
  2986.6 81.1 %reduce-scatter.57.cloned.1.call-done = f32[192,3200]{1,0:T(8,128)} async-done(((f32[768,3200]{1,0:T(8,128)}), f32[192,3200]{1,0:T(8,128)}) %reduce-scatter.57.cloned.1.call-update) | async-done | bytes 2457616 | tf_op jit(solution)/shard_map/reduce_scatter | solution.py:177
  3068.0 67.9 %all-gather.33.cloned.1.call-done = f32[768,3200]{1,0:T(8,128)} async-done(((f32[192,3200]{1,0:T(8,128)}), f32[768,3200]{1,0:T(8,128)}) %all-gather.33.cloned.1.call-update) | async-done | bytes 9830416 | tf_op jit(solution)/shard_map/all_gather | solution.py:180
  3225.8 81.1 %reduce-scatter.59.cloned.1.call-done = f32[192,3200]{1,0:T(8,128)} async-done(((f32[768,3200]{1,0:T(8,128)}), f32[192,3200]{1,0:T(8,128)}) %reduce-scatter.59.cloned.1.call-update) | async-done | bytes 2457616 | tf_op jit(solution)/shard_map/reduce_scatter | solution.py:177
  3307.1 67.9 %all-gather.35.cloned.1.call-done = f32[768,3200]{1,0:T(8,128)} async-done(((f32[192,3200]{1,0:T(8,128)}), f32[768,3200]{1,0:T(8,128)}) %all-gather.35.cloned.1.call-update) | async-done | bytes 9830416 | tf_op jit(solution)/shard_map/all_gather | solution.py:180
  3463.5 81.1 %reduce-scatter.61.cloned.1.call-done = f32[192,3200]{1,0:T(8,128)} async-done(((f32[768,3200]{1,0:T(8,128)}), f32[192,3200]{1,0:T(8,128)}) %reduce-scatter.61.cloned.1.call-update) | async-done | bytes 2457616 | tf_op jit(solution)/shard_map/reduce_scatter | solution.py:177
  3557.3 55.3 %all-gather.37.cloned.1.call-done = f32[768,3200]{1,0:T(8,128)} async-done(((f32[192,3200]{1,0:T(8,128)}), f32[768,3200]{1,0:T(8,128)}) %all-gather.37.cloned.1.call-update) | async-done | bytes 9830416 | tf_op jit(solution)/shard_map/all_gather | solution.py:180
  (1405 shorter events, 1051.3 us)
Async XLA Ops:
  7.2 267.5 %all-gather.19.cloned.1.call-start = ((), (), s32[]{:S(2)}) async-start(), calls=%async_computation.16 | async-start | bytes 48660480 | tf_op jit(solution)/shard_map/all_gather | solution.py:242
  10.4 295.4 %all-gather.21.cloned.1.call-start = ((), (), s32[]{:S(2)}) async-start(), calls=%async_computation.17 | async-start | bytes 4423680 | tf_op jit(solution)/shard_map/all_gather | solution.py:226
  13.1 315.8 %all-gather.23.cloned.1.call-start = ((), (), s32[]{:S(2)}) async-start(), calls=%async_computation.18 | async-start | bytes 1474560 | tf_op jit(solution)/shard_map/all_gather | solution.py:227
  13.9 351.1 %all-gather.25.cloned.1.call-start = ((), (), s32[]{:S(2)}) async-start(), calls=%async_computation.19 | async-start | bytes 5898240 | tf_op jit(solution)/shard_map/all_gather | solution.py:228
  15.2 408.5 %all-gather.27.cloned.1.call-start = ((), (), s32[]{:S(2)}) async-start(), calls=%async_computation.20 | async-start | bytes 5898240 | tf_op jit(solution)/shard_map/all_gather | solution.py:229
  18.1 841.7 %reduce-scatter.35.cloned.1.call-start = ((), (), s32[]{:S(2)}) async-start(), calls=%async_computation.22 | async-start | bytes 147456 | tf_op jit(solution)/shard_map/reduce_scatter | solution.py:298
  74.5 220.4 %copy-start.240 = (f32[768]{0:T(1024)}, f32[768]{0:T(1024)S(1)}, u32[]{:S(2)}) copy-start(f32[768]{0:T(1024)S(1)} %get-tuple-element.228) | copy-start | bytes 9220
  74.5 361.0 %copy-start.233 = (f32[768]{0:T(1024)}, f32[768]{0:T(1024)S(1)}, u32[]{:S(2)}) copy-start(f32[768]{0:T(1024)S(1)} %get-tuple-element.220) | copy-start | bytes 9220
  74.5 432.9 %copy-start.222 = (f32[768]{0:T(1024)}, f32[768]{0:T(1024)S(1)}, u32[]{:S(2)}) copy-start(f32[768]{0:T(1024)S(1)} %get-tuple-element.229) | copy-start | bytes 9220
  801.1 122.0 %reduce-scatter.33.cloned.1.call-start = ((), (), s32[]{:S(2)}) async-start(), calls=%async_computation.21 | async-start | bytes 147456 | tf_op jit(solution)/shard_map/reduce_scatter | solution.py:298
  819.0 237.8 %reduce-scatter.45.cloned.1.call-start = ((), (), s32[]{:S(2)}) async-start(), calls=%async_computation.27 | async-start | bytes 491520 | tf_op jit(solution)/shard_map/reduce_scatter | solution.py:332
  972.5 84.4 %reduce-scatter.49.cloned.1.call-start = ((), (), s32[]{:S(2)}) async-start(), calls=%async_computation.34 | async-start | bytes 1966080
  989.4 70.6 %reduce-scatter.39.cloned.1.call-start = ((), (), s32[]{:S(2)}) async-start(), calls=%async_computation.24 | async-start | bytes 2949120 | tf_op jit(solution)/shard_map/reduce_scatter | solution.py:329
  994.6 131.8 %reduce-scatter.37.cloned.1.call-start = ((), (), s32[]{:S(2)}) async-start(), calls=%async_computation.23 | async-start | bytes 8847360 | tf_op jit(solution)/shard_map/reduce_scatter | solution.py:328
  1006.0 201.4 %reduce-scatter.41.cloned.1.call-start = ((), (), s32[]{:S(2)}) async-start(), calls=%async_computation.25 | async-start | bytes 11796480 | tf_op jit(solution)/shard_map/reduce_scatter | solution.py:330
  1026.7 261.8 %reduce-scatter.43.cloned.1.call-start = ((), (), s32[]{:S(2)}) async-start(), calls=%async_computation.26 | async-start | bytes 11796480 | tf_op jit(solution)/shard_map/reduce_scatter | solution.py:331
  1048.1 421.1 %reduce-scatter.63.cloned.1.call-start = ((), (), s32[]{:S(2)}) async-start(), calls=%async_computation.41 | async-start | bytes 491520
  1053.4 416.6 %reduce-scatter.51.cloned.1.call-start = ((), (), s32[]{:S(2)}) async-start(), calls=%async_computation.35 | async-start | bytes 6881280
  1056.8 568.4 %all-reduce.68.cloned.1.call-start = ((), (), s32[]{:S(2)}) async-start(), calls=%async_computation.42 | async-start | bytes 15138816 | tf_op jit(solution)/shard_map/psum | solution.py:337
  1288.6 1122.6 %reduce-scatter.47.cloned.1.call-start = ((), (), s32[]{:S(2)}) async-start(), calls=%async_computation.28 | async-start | bytes 97320960 | tf_op jit(solution)/shard_map/reduce_scatter | solution.py:316
  1463.6 1119.1 %reduce-scatter.53.cloned.1.call-start = ((), (), s32[]{:S(2)}) async-start(), calls=%async_computation.36 | async-start | bytes 12288000 | tf_op jit(solution)/shard_map/reduce_scatter | solution.py:177
  2458.9 264.8 %copy-start.13 = (f32[768,768]{1,0:T(8,128)}, f32[768,768]{1,0:T(8,128)S(1)}, u32[]{:S(2)}) copy-start(f32[768,768]{1,0:T(8,128)S(1)} %multiply_add_fusion.9) | copy-start | bytes 7077892
  2463.6 227.5 %copy-start.67 = (f32[768,192]{0,1:T(8,128)}, f32[768,192]{0,1:T(8,128)S(1)}, u32[]{:S(2)}) copy-start(f32[768,192]{0,1:T(8,128)S(1)} %multiply_add_fusion.20) | copy-start | bytes 1769476
  2501.7 149.1 %all-gather.29.cloned.1.call-start = ((), (), s32[]{:S(2)}) async-start(), calls=%async_computation.29 | async-start | bytes 12288000 | tf_op jit(solution)/shard_map/all_gather | solution.py:180
  2582.7 247.6 %reduce-scatter.55.cloned.1.call-start = ((), (), s32[]{:S(2)}) async-start(), calls=%async_computation.37 | async-start | bytes 12288000 | tf_op jit(solution)/shard_map/reduce_scatter | solution.py:177
  2749.2 149.3 %all-gather.31.cloned.1.call-start = ((), (), s32[]{:S(2)}) async-start(), calls=%async_computation.30 | async-start | bytes 12288000 | tf_op jit(solution)/shard_map/all_gather | solution.py:180
  2830.3 237.4 %reduce-scatter.57.cloned.1.call-start = ((), (), s32[]{:S(2)}) async-start(), calls=%async_computation.38 | async-start | bytes 12288000 | tf_op jit(solution)/shard_map/reduce_scatter | solution.py:177
  2986.6 149.3 %all-gather.33.cloned.1.call-start = ((), (), s32[]{:S(2)}) async-start(), calls=%async_computation.31 | async-start | bytes 12288000 | tf_op jit(solution)/shard_map/all_gather | solution.py:180
  3067.7 239.2 %reduce-scatter.59.cloned.1.call-start = ((), (), s32[]{:S(2)}) async-start(), calls=%async_computation.39 | async-start | bytes 12288000 | tf_op jit(solution)/shard_map/reduce_scatter | solution.py:177
  3225.8 149.3 %all-gather.35.cloned.1.call-start = ((), (), s32[]{:S(2)}) async-start(), calls=%async_computation.32 | async-start | bytes 12288000 | tf_op jit(solution)/shard_map/all_gather | solution.py:180
  3306.9 237.6 %reduce-scatter.61.cloned.1.call-start = ((), (), s32[]{:S(2)}) async-start(), calls=%async_computation.40 | async-start | bytes 12288000 | tf_op jit(solution)/shard_map/reduce_scatter | solution.py:177
  3463.4 149.1 %all-gather.37.cloned.1.call-start = ((), (), s32[]{:S(2)}) async-start(), calls=%async_computation.33 | async-start | bytes 12288000 | tf_op jit(solution)/shard_map/all_gather | solution.py:180
  (434 other events, 3902.9 us)
Sparse Core Ops, SparseCore 0:
  11.5 263.1 all-gather.18
  276.8 28.9 all-gather.20
  307.9 17.4 all-gather.22
  327.4 37.4 all-gather.24
  366.9 37.4 all-gather.26
  801.2 58.6 reduce-scatter.34
  863.1 59.8 reduce-scatter.32
  972.6 19.8 reduce-scatter.44
  995.6 28.1 reduce-scatter.48
  1026.9 33.0 reduce-scatter.38
  1062.6 63.6 reduce-scatter.36
  1129.0 78.4 reduce-scatter.40
  1210.2 78.3 reduce-scatter.42
  1291.7 20.8 reduce-scatter.62
  1315.1 53.1 reduce-scatter.50
  1373.2 251.9 all-reduce.67
  1631.5 779.6 reduce-scatter.46
  2501.8 80.7 reduce-scatter.52
  2584.3 66.4 all-gather.28
  2749.3 80.9 reduce-scatter.54
  2831.9 66.4 all-gather.30
  2986.7 80.9 reduce-scatter.56
  3069.3 66.4 all-gather.32
  3225.9 80.9 reduce-scatter.58
  3308.5 66.4 all-gather.34
  3463.5 80.9 reduce-scatter.60
  3546.0 66.4 all-gather.36
where the time goes:
time: 3690 us; the launch traced here: 3680 us
  waiting for transfers between devices  2160 us (59%)
  matrix products  656 us (18%)
  other arithmetic  362 us (10%)
  blocking collectives  278 us (8%)
  local copies, waits for them, and re-layouts  182 us (5%)
    reduce_scatter x1, waiting for transfers between devices, body(): lax.psum_scatter(jax.ops.segment_sum(jnp.where(inside[:, None], all_rows,...  771 us
    reduce_scatter x5, waiting for transfers between devices, gram_blocks(): lax.psum_scatter(jnp.concatenate(blocks_list, axis=1), 'narrow', scatter_...  405 us
    dot_general x75, matrix products, product(): jnp.dot(operand, other, precision=highest, preferred_element_type=jnp.flo...  394 us
    all_gather x5, waiting for transfers between devices, gram_blocks(): complete = lax.all_gather(own_rows, 'narrow', axis=0, tiled=True)  327 us
    dot_general x60, matrix products, single_pass(): return jnp.dot(operand, other, preferred_element_type=jnp.float32)  180 us
    all_gather x1, waiting for transfers between devices, body(): lax.all_gather(table.astype(jnp.bfloat16), ('blk', 'narrow'), axis=0, til...  179 us
    scatter-add x1, other arithmetic, body(): jax.ops.segment_sum(jnp.where(inside[:, None], all_rows, 0.0), jnp.where(...  141 us
    psum x1, waiting for transfers between devices, body(): lax.psum((shards[0], shards[1], shards[2], shards[3], shards[4], shards[5...  114 us
  transfers between devices with their start and end apart: 27, of which 21 were waited for; matrix products, arithmetic and copies ran while one was open for 12% of the time, Pallas kernels for 0%

commit v1 on v0

v1 whole, which is shorter than its diff:
```python
import functools

import jax
import jax.numpy as jnp
from jax import lax
from jax.experimental import pallas as pl
from jax.experimental.pallas import tpu as pltpu
from jax.sharding import PartitionSpec as P

D = 768
HEADS = 12
HDIM = 64
FF = 3072
VDIM = 128
STEP = 10
MATRICES = 4

norm_eps = 1e-12
smoothing = 0.1
masked = -1e30
newton_one = 3.4445
newton_two = -4.775
newton_three = 2.0315
muon_rate = 0.1
attn_rate = 1.0
muon_moment = 0.95
weight_decay = 0.01
adam_rate = 0.02
vector_rate = 0.25
beta_one = 0.9
beta_two = 0.95
adam_eps = 1e-08
clip_limit = 0.05

bf16 = jnp.bfloat16
f32 = jnp.float32
SLOT_CAPS = {960: 36, 120: 7}


def round_up(value, step):
    return -(-value // step) * step


def dot_nn(left, right):
    return lax.dot_general(left, right, (((1,), (0,)), ((), ())), preferred_element_type=f32)


def dot_nt(left, right):
    return lax.dot_general(left, right, (((1,), (1,)), ((), ())), preferred_element_type=f32)


def dot_tn(left, right):
    return lax.dot_general(left, right, (((0,), (0,)), ((), ())), preferred_element_type=f32)


def low(values):
    return values.astype(bf16)


def norm_forward(values, gain, shift):
    centred = values - jnp.mean(values, axis=-1, keepdims=True)
    spread = jnp.mean(centred * centred, axis=-1, keepdims=True)
    scale = lax.rsqrt(spread + norm_eps)
    hat = centred * scale
    return hat * gain + shift, hat, scale


def norm_backward(grad, hat, scale, gain):
    d_hat = grad * gain
    first = jnp.mean(d_hat, axis=-1, keepdims=True)
    second = jnp.mean(d_hat * hat, axis=-1, keepdims=True)
    return scale * (d_hat - first - hat * second)


def gelu_parts(values):
    cdf = 0.5 * (1.0 + lax.erf(values * (0.5**0.5)))
    density = jnp.exp(-0.5 * values * values) * 0.3989422804014327
    return values * cdf, cdf + values * density


def attention_forward_kernel(lens_ref, qkv_ref, out_ref, *, query_len, span):
    used = lens_ref[pl.program_id(0)]
    bias_long = jnp.where(lax.broadcasted_iota(jnp.int32, (1, span), 1) < used, 0.0, masked)

    def attend(first, count, lane, half, bias):
        rows = pl.ds(first, count)
        queries = qkv_ref[rows, pl.ds(lane, 128)][:, half]
        keys = qkv_ref[rows, pl.ds(lane + D, 128)][:, half]
        values = qkv_ref[rows, pl.ds(lane + 2 * D, 128)][:, half]
        scores = dot_nt(queries * bf16(HDIM**-0.5), keys)
        if bias is not None:
            scores = scores + bias
        exponent = jnp.exp(scores - jnp.max(scores, axis=-1, keepdims=True))
        attend_low = low(exponent * (1.0 / jnp.sum(exponent, axis=-1, keepdims=True)))
        return dot_nn(attend_low, values)

    def pair(index, carry):
        lane = pl.multiple_of(index * 128, 128)
        halves = (slice(0, HDIM), slice(HDIM, 128))
        for first, count, bias in ((0, query_len, None), (query_len, span, bias_long)):
            both = [attend(first, count, lane, half, bias) for half in halves]
            out_ref[pl.ds(first, count), pl.ds(lane, 128)] = low(jnp.concatenate(both, axis=1))
        return carry

    lax.fori_loop(0, HEADS // 2, pair, 0)


def attention_backward_kernel(lens_ref, qkv_ref, grad_ref, out_ref, *, query_len, span):
    used = lens_ref[pl.program_id(0)]
    bias_long = jnp.where(lax.broadcasted_iota(jnp.int32, (span, 1), 0) < used, 0.0, masked)

    def attend(first, count, lane, half, bias):
        rows = pl.ds(first, count)
        queries = qkv_ref[rows, pl.ds(lane, 128)][:, half] * bf16(HDIM**-0.5)
        keys = qkv_ref[rows, pl.ds(lane + D, 128)][:, half]
        values = qkv_ref[rows, pl.ds(lane + 2 * D, 128)][:, half]
        grads = grad_ref[rows, pl.ds(lane, 128)][:, half]
        scores = dot_nt(keys, queries)
        if bias is not None:
            scores = scores + bias
        exponent = jnp.exp(scores - jnp.max(scores, axis=0, keepdims=True))
        share = exponent * (1.0 / jnp.sum(exponent, axis=0, keepdims=True))
        d_share = dot_nt(values, grads)
        d_values = dot_nn(low(share), grads)
        weighted = share * d_share
        d_scores = low(weighted - share * jnp.sum(weighted, axis=0, keepdims=True))
        d_keys = dot_nn(d_scores, queries)
        d_queries = dot_tn(d_scores, keys) * HDIM**-0.5
        return d_queries, d_keys, d_values

    def pair(index, carry):
        lane = pl.multiple_of(index * 128, 128)
        halves = (slice(0, HDIM), slice(HDIM, 128))
        for first, count, bias in ((0, query_len, None), (query_len, span, bias_long)):
            one, two = [attend(first, count, lane, half, bias) for half in halves]
            for part in range(3):
                both = jnp.concatenate([one[part], two[part]], axis=1)
                out_ref[pl.ds(first, count), pl.ds(lane + part * D, 128)] = low(both)
        return carry

    lax.fori_loop(0, HEADS // 2, pair, 0)


def attention_call(kernel, lens, arrays, out_width, query_len, span, micro_count, cost):
    length = query_len + span
    return pl.pallas_call(
        functools.partial(kernel, query_len=query_len, span=span),
        out_shape=jax.ShapeDtypeStruct((micro_count * length, out_width), bf16),
        grid_spec=pltpu.PrefetchScalarGridSpec(
            num_scalar_prefetch=1,
            grid=(micro_count,),
            in_specs=[
                pl.BlockSpec((length, member.shape[1]), lambda micro, lens: (micro, 0))
                for member in arrays
            ],
            out_specs=pl.BlockSpec((length, out_width), lambda micro, lens: (micro, 0)),
        ),
        compiler_params=pltpu.CompilerParams(vmem_limit_bytes=48 * 1024 * 1024),
        cost_estimate=pl.CostEstimate(
            flops=cost * micro_count * HEADS * span * span * HDIM * 2,
            bytes_accessed=micro_count * length * (out_width + 3 * D) * 2,
            transcendentals=micro_count * HEADS * span * span,
        ),
    )(lens, *arrays)


def share_all(value, axes, count):
    spread = jnp.broadcast_to(value[None], (count,) + value.shape)
    return lax.all_to_all(spread, axes, 0, 0, tiled=True)


def swap(value, axis, size, bit):
    return lax.ppermute(value, axis, [(place, place ^ bit) for place in range(size)])


def reduce_rows(whole, narrow, blocks, wire):
    place = lax.axis_index("narrow")
    low_bit, upper = place & 1, place // 2
    width, depth = whole.shape[0] // narrow, whole.shape[1]
    pairs = narrow // 2

    def rows_of(offset, bit):
        return lax.dynamic_slice_in_dim(whole, (2 * (upper ^ offset) + bit) * width, width, axis=0)

    totals = [None] * pairs
    for offset in reversed(range(pairs)):
        got = swap(rows_of(offset, 1 - low_bit).astype(wire), "narrow", narrow, 1)
        totals[offset] = rows_of(offset, low_bit) + got.astype(f32)
    half = pairs // 2
    while half:
        for offset in range(half):
            got = swap(totals[offset + half].astype(wire), "narrow", narrow, 2 * half)
            totals[offset] = totals[offset] + got.astype(f32)
        half = half // 2
    parts = totals[0].astype(wire).reshape(blocks, -1, depth)
    parts = lax.all_to_all(parts, "blk", 0, 0, tiled=True)
    return jnp.sum(parts.astype(f32), axis=0)


def sum_narrow(value, narrow):
    place = lax.axis_index("narrow")
    if narrow & (narrow - 1):
        return lax.psum(value, "narrow")
    halves = value.reshape(2, value.shape[0] // 2, value.shape[1])
    low_bit = place & 1
    mine = lax.dynamic_index_in_dim(halves, low_bit, 0, keepdims=False)
    other = lax.dynamic_index_in_dim(halves, 1 - low_bit, 0, keepdims=False)
    total = mine + swap(other, "narrow", narrow, 1)
    bit = 2
    while bit < narrow:
        total = total + swap(total, "narrow", narrow, bit)
        bit = bit * 2
    other = swap(total, "narrow", narrow, 1)
    first = jnp.where(low_bit == 0, total, other)
    second = jnp.where(low_bit == 0, other, total)
    return jnp.concatenate([first, second], axis=0)


def adam_step(weight, first, second, gradient, rate):
    first_new = beta_one * first + (1.0 - beta_one) * gradient
    second_new = beta_two * second + (1.0 - beta_two) * gradient * gradient
    update = (
        first_new
        / (1.0 - beta_one**STEP)
        / (jnp.sqrt(second_new / (1.0 - beta_two**STEP)) + adam_eps)
    )
    return (weight - rate * (update + weight_decay * weight), first_new, second_new)


def split_into(value, left_ref, right_ref, first):
    count, size = value.shape
    high = low(value)
    rest = low(value - high.astype(f32))
    rows = pl.ds(first, count)
    if left_ref is not None:
        left_ref[rows, 0:size] = high
        left_ref[rows, size : 2 * size] = high
        left_ref[rows, 2 * size : 3 * size] = rest
    if right_ref is not None:
        right_ref[rows, :] = high
        right_ref[pl.ds(first + size, count), :] = rest
        right_ref[pl.ds(first + 2 * size, count), :] = high


def chain_kernel(*refs):
    refs = [refs[side::2] for side in (0, 1)]

    def steps(size):
        return [(first, min(256, size - first)) for first in range(0, size, 256)]

    for gram_in, rows_in, _, gram, rows, half, gram_l, gram_r, poly_l, poly_r, half_l, rows_l in refs:
        size, count = gram.shape[0], rows.shape[0]
        diagonal = lax.broadcasted_iota(jnp.int32, (size, size), 0) == lax.broadcasted_iota(
            jnp.int32, (size, size), 1
        )
        trace = jnp.sum(jnp.where(diagonal, gram_in[...], 0.0), axis=(0, 1), keepdims=True)
        scale = 1.0 / (jnp.sqrt(trace) + 1e-07)
        for first, step in steps(size):
            block = gram_in[pl.ds(first, step), :] * (scale * scale)
            gram[pl.ds(first, step), :] = block
            split_into(block, gram_l, gram_r, first)
        for first, step in steps(count):
            block = rows_in[pl.ds(first, step), :] * scale
            rows[pl.ds(first, step), :] = block
            split_into(block, rows_l, None, first)

    def advance(last):
        for _, _, out, gram, rows, half, gram_l, gram_r, poly_l, poly_r, half_l, rows_l in refs:
            size, count = gram.shape[0], rows.shape[0]
            for first, step in steps(size):
                here = pl.ds(first, step)
                square = dot_nn(gram_l[here, :], gram_r[...])
                poly = newton_two * gram[here, :] + newton_three * square
                split_into(poly, poly_l, poly_r, first)
            if not last:
                for first, step in steps(size):
                    here = pl.ds(first, step)
                    block = newton_one * gram[here, :] + dot_nn(poly_l[here, :], gram_r[...])
                    half[here, :] = block
                    split_into(block, half_l, None, first)
            for first, step in steps(count):
                here = pl.ds(first, step)
                block = newton_one * rows[here, :] + dot_nn(rows_l[here, :], poly_r[...])
                if last:
                    out[here, :] = block.astype(out.dtype)
                else:
                    rows[here, :] = block
                    split_into(block, rows_l, None, first)
            if not last:
                for first, step in steps(size):
                    here = pl.ds(first, step)
                    block = newton_one * half[here, :] + dot_nn(half_l[here, :], poly_r[...])
                    gram[here, :] = block
                    split_into(block, gram_l, gram_r, first)

    def turn(_, carry):
        advance(False)
        return carry

    lax.fori_loop(0, 4, turn, 0)
    advance(True)


def newton_chains(gram, rows, gram_small, rows_small):
    scratch = []
    sizes = ((gram.shape[0], rows.shape[0]), (gram_small.shape[0], rows_small.shape[0]))
    shapes = [
        [((size, size), f32), ((count, size), f32), ((size, size), f32)]
        + [((size, 3 * size), bf16), ((3 * size, size), bf16)] * 2
        + [((size, 3 * size), bf16), ((count, 3 * size), bf16)]
        for size, count in sizes
    ]
    scratch = [pltpu.VMEM(*shape) for pair in zip(*shapes) for shape in pair]
    whole = pl.BlockSpec(memory_space=pltpu.VMEM)
    flops = sum(2 * 3 * (13 * size + 5 * count) * size * size for size, count in sizes)
    return pl.pallas_call(
        chain_kernel,
        out_shape=(
            jax.ShapeDtypeStruct(rows.shape, bf16),
            jax.ShapeDtypeStruct(rows_small.shape, f32),
        ),
        in_specs=[whole] * 4,
        out_specs=(whole, whole),
        scratch_shapes=scratch,
        compiler_params=pltpu.CompilerParams(vmem_limit_bytes=56 * 1024 * 1024),
        cost_estimate=pl.CostEstimate(flops=flops, bytes_accessed=8 * gram.size, transcendentals=0),
    )(gram, gram_small, rows, rows_small)


def body(
    query_ids,
    passage_ids,
    passage_len,
    positives,
    domains,
    table,
    table_m,
    table_v,
    pos_table,
    pos_m,
    pos_v,
    vector,
    vector_m,
    vector_v,
    w_qkv,
    m_qkv,
    w_attn,
    m_attn,
    w_in,
    m_in,
    w_out,
    m_out,
    w_proj,
    m_proj,
):
    blocks = lax.axis_size("blk")
    narrow = lax.axis_size("narrow")
    devices = blocks * narrow
    both = ("blk", "narrow")
    myself = lax.axis_index("blk")
    shard_rows = table.shape[0]
    micro_count, _, query_len = query_ids.shape
    span = passage_ids.shape[2]
    length = query_len + span
    tokens = micro_count * length

    side = D // narrow
    vector_cols = vector.shape[1] // side
    small = jnp.concatenate(
        [
            low(pos_table).T,
            low(w_proj).T,
            low(vector).reshape(side, vector_cols),
            jnp.zeros((side, 128 - vector_cols), bf16),
        ],
        axis=1,
    )

    def gather(shard):
        return lax.all_gather(shard, "narrow", axis=0, tiled=True)

    small = gather(small)
    qkv_t = gather(low(w_qkv).T)
    attn_t = gather(low(w_attn).T)
    in_t = gather(low(w_in).T)
    out_t = gather(low(w_out).T)
    pos = small[:, :span].T.astype(f32)
    proj_t = small[:, span : span + VDIM]
    gains = small[:, span + VDIM : span + VDIM + vector_cols].reshape(-1).astype(f32)
    bounds = [0, D, 2 * D, 3 * D, 4 * D, 5 * D, 6 * D, 7 * D, 7 * D + FF, 8 * D + FF, 9 * D + FF]
    bounds = bounds + [10 * D + FF]
    pieces = [gains[None, bounds[index] : bounds[index + 1]] for index in range(11)]
    qkv_bias = jnp.concatenate([pieces[2], jnp.zeros_like(pieces[2]), pieces[3]], axis=1)

    slots = round_up(SLOT_CAPS.get(shard_rows, tokens), 8)
    ids = jnp.concatenate([query_ids[:, 0], passage_ids[:, 0]], axis=1).reshape(tokens)
    owner = ids // shard_rows
    local_id = ids - owner * shard_rows
    is_owner = owner[:, None] == jnp.arange(devices, dtype=jnp.int32)[None]
    before = jnp.arange(tokens)[:, None] > jnp.arange(tokens)[None]
    earlier = dot_nn(before.astype(bf16), is_owner.astype(bf16))
    rank = jnp.sum(jnp.where(is_owner, earlier, 0.0), axis=1).astype(jnp.int32)
    place = owner * slots + rank
    picks = (place[:, None] == jnp.arange(devices * slots, dtype=jnp.int32)[None]).astype(bf16)
    picks = lax.optimization_barrier(picks)
    digits = jnp.stack([local_id // 32, local_id % 32], axis=1).astype(bf16)
    asked = dot_tn(digits, picks)
    asked = (asked[0] * 32.0 + asked[1]).astype(jnp.int32).reshape(devices, slots)
    wanted = lax.all_to_all(asked, both, 0, 0, tiled=True).reshape(devices * slots)
    chosen = (wanted[:, None] == jnp.arange(shard_rows, dtype=jnp.int32)[None]).astype(bf16)
    chosen = lax.optimization_barrier(chosen)
    sent_rows = low(dot_nn(chosen, low(table))).reshape(devices, slots, D)
    got_rows = lax.all_to_all(sent_rows, both, 0, 0, tiled=True).reshape(devices * slots, D)
    token_rows = dot_nn(picks, got_rows)

    lens = passage_len[:, 0]
    pos_rows = jnp.concatenate([pos[:query_len], pos] * micro_count, axis=0)
    x, x_hat, x_scale = norm_forward(token_rows + pos_rows, pieces[0], pieces[1])
    x_low = low(x)
    qkv = low(dot_nt(x_low, qkv_t) + qkv_bias)
    context = attention_call(
        attention_forward_kernel, lens, (qkv,), D, query_len, span, micro_count, 2
    )
    h, h_hat, h_scale = norm_forward(
        x + dot_nt(context, attn_t) + pieces[4], pieces[5], pieces[6]
    )
    h_low = low(h)
    wide = dot_nt(h_low, in_t) + pieces[7]
    wide = lax.optimization_barrier(wide)
    gelu_value, gelu_slope = gelu_parts(wide)
    f_low, gelu_slope = lax.optimization_barrier((low(gelu_value), gelu_slope))
    o, o_hat, o_scale = norm_forward(h + dot_nn(f_low, out_t) + pieces[8], pieces[9], pieces[10])
    o_low = low(o)
    e = dot_nn(o_low, proj_t)
    e_scale = lax.rsqrt(jnp.sum(e * e, axis=-1, keepdims=True) + 1e-06)
    vecs = low(e * e_scale).reshape(micro_count, length, VDIM)

    query_vecs = vecs[:, :query_len]
    passage_vecs = vecs[:, query_len:]
    cycle = share_all(query_vecs.reshape(micro_count * query_len, VDIM), "blk", blocks)
    cycle = cycle.reshape(blocks, micro_count, query_len, VDIM).transpose(1, 0, 2, 3)
    cycle = cycle.reshape(micro_count, blocks * query_len, VDIM)
    usable = jnp.arange(span)[None] < lens[:, None]
    sims = jnp.einsum("mik,mjk->mij", cycle, passage_vecs, preferred_element_type=f32)
    scaled = jnp.where(usable[:, None, :], sims / smoothing, masked)
    summit = jnp.max(scaled, axis=-1, keepdims=True)
    expvals = jnp.exp(scaled - summit)
    totals = jnp.sum(expvals, axis=-1, keepdims=True)
    smooth = smoothing * (summit[..., 0] + jnp.log(totals[..., 0]))
    scores = jnp.sum(smooth.reshape(micro_count, blocks, query_len), axis=-1)
    every = share_all(scores.reshape(1, micro_count * blocks), "blk", blocks)
    every = every.reshape(blocks, micro_count, blocks).transpose(1, 0, 2)
    labels = domains[:, 0]
    targets = positives[:, 0]
    spots = jnp.arange(blocks, dtype=jnp.int32)
    chosen_label = jnp.sum(
        jnp.where(targets[:, :, None] == spots[None, None], labels[:, None, :], 0), axis=-1
    )
    allowed = labels[:, :, None] == chosen_label[:, None, :]
    hits = targets[:, None, :] == spots[None, :, None]
    permitted = jnp.where(allowed, every, masked)
    peak = jnp.max(permitted, axis=1, keepdims=True)
    mass = jnp.sum(jnp.where(allowed, jnp.exp(every - peak), 0.0), axis=1, keepdims=True)
    log_total = peak + jnp.log(mass)
    matched = jnp.sum(jnp.where(hits, every, 0.0), axis=1)
    own = spots == myself
    loss_part = jnp.sum(jnp.where(own[None], log_total[:, 0] - matched, 0.0))
    d_every = jnp.where(allowed, jnp.exp(every - log_total), 0.0) - hits.astype(f32)
    d_scores = jnp.sum(jnp.where(own[None, :, None], d_every, 0.0), axis=1)
    d_tokens = jnp.broadcast_to(d_scores[:, :, None], (micro_count, blocks, query_len))
    d_sims = low(d_tokens.reshape(micro_count, blocks * query_len, 1) * (expvals / totals))
    d_passage = jnp.einsum("mij,mik->mjk", d_sims, cycle, preferred_element_type=f32)
    d_cycle = jnp.einsum("mij,mjk->mik", d_sims, passage_vecs, preferred_element_type=f32)
    d_cycle = d_cycle.reshape(micro_count, blocks, query_len, VDIM).transpose(1, 0, 2, 3)
    d_query = jnp.sum(lax.all_to_all(d_cycle, "blk", 0, 0, tiled=True), axis=0)
    d_vecs = jnp.concatenate([d_query, d_passage], axis=1).reshape(tokens, VDIM)

    def summed(left, right):
        return reduce_rows(dot_tn(left, right), narrow, blocks, bf16)

    def column_sum(values):
        return jnp.sum(values, axis=0)

    d_vecs = low(d_vecs).astype(f32)
    inner = jnp.sum(e * d_vecs, axis=-1, keepdims=True)
    d_e = low(e_scale * d_vecs - e * (e_scale * e_scale * e_scale * inner))
    g_proj = dot_tn(o_low, d_e)
    d_o = low(dot_nt(d_e, proj_t)).astype(f32)
    g_gain_o, g_shift_o = column_sum(d_o * o_hat), column_sum(d_o)
    d_sum_o = norm_backward(d_o, o_hat, o_scale, pieces[9])
    g_bias_out = column_sum(d_sum_o)
    d_y = low(d_sum_o)
    g_out = summed(f_low, d_y)
    d_f = low(dot_nt(d_y, out_t)).astype(f32)
    d_wide = d_f * gelu_slope
    g_bias_in = column_sum(d_wide)
    d_wide = lax.optimization_barrier(low(d_wide))
    g_in = summed(d_wide, h_low)
    d_h = d_sum_o + low(dot_nn(d_wide, in_t)).astype(f32)
    g_gain_h, g_shift_h = column_sum(d_h * h_hat), column_sum(d_h)
    d_sum_h = norm_backward(d_h, h_hat, h_scale, pieces[5])
    g_bias_attn = column_sum(d_sum_h)
    d_a = low(d_sum_h)
    g_attn = summed(d_a, context)
    d_context = low(dot_nn(d_a, attn_t))
    d_qkv = attention_call(
        attention_backward_kernel,
        lens,
        (qkv, d_context),
        3 * D,
        query_len,
        span,
        micro_count,
        5,
    )
    g_qkv = summed(d_qkv, x_low)
    g_bias_qkv = column_sum(d_qkv.astype(f32))
    d_x = d_sum_h + low(dot_nn(d_qkv, qkv_t)).astype(f32)
    g_gain_x, g_shift_x = column_sum(d_x * x_hat), column_sum(d_x)
    d_rows = norm_backward(d_x, x_hat, x_scale, pieces[0])
    d_rows = lax.optimization_barrier(d_rows)

    back_rows = low(dot_tn(picks, low(d_rows))).reshape(devices, slots, D)
    back_rows = lax.all_to_all(back_rows, both, 0, 0, tiled=True).reshape(devices * slots, D)
    table_grad = dot_tn(chosen, back_rows)
    d_micro = d_rows.reshape(micro_count, length, D)
    g_pos = jnp.sum(d_micro[:, query_len:], axis=0)
    g_pos = jnp.concatenate(
        [g_pos[:query_len] + jnp.sum(d_micro[:, :query_len], axis=0), g_pos[query_len:]], axis=0
    )
    g_vector = jnp.concatenate(
        [
            g_gain_x,
            g_shift_x,
            g_bias_qkv[:D],
            g_bias_qkv[2 * D :],
            g_bias_attn,
            g_gain_h,
            g_shift_h,
            g_bias_in,
            g_bias_out,
            g_gain_o,
            g_shift_o,
        ]
    )
    tail_spare = round_up(span + VDIM + vector_cols + 1, 128) - (span + VDIM + vector_cols + 1)
    tail = jnp.concatenate(
        [
            g_pos.T,
            g_proj,
            g_vector.reshape(D, vector_cols),
            g_bias_attn[:, None],
            jnp.zeros((D, tail_spare), f32),
        ],
        axis=1,
    )
    g_tail = reduce_rows(tail, narrow, blocks, f32)

    def square_sum(values):
        values = values.astype(f32)
        return jnp.sum(values * values)

    local_square = (
        square_sum(table_grad)
        + square_sum(g_out)
        + square_sum(g_in)
        + square_sum(g_qkv)
        + square_sum(g_attn)
        + square_sum(g_tail[:, : span + VDIM + vector_cols])
    )
    lane = jnp.arange(128)[None]
    pair = jnp.where(lane == 0, local_square, jnp.where(lane == 1, loss_part, 0.0))
    sums = jnp.sum(share_all(pair, both, devices), axis=(0, 1))
    loss = sums[1]
    grad_norm = jnp.sqrt(sums[0])
    factor = jnp.minimum(1.0, clip_limit / (grad_norm + 1e-06))

    wide_rows = g_out.shape[0]
    attn_rows = g_attn.shape[0]
    g_out, g_in, g_qkv, g_attn, g_tail = (
        low(member) for member in (g_out, g_in, g_qkv, g_attn, g_tail)
    )
    packed = [g_out, g_in, g_qkv, g_attn, g_tail]
    flat = jnp.concatenate([member.reshape(-1, 128) for member in packed], axis=0)
    complete = lax.all_gather(flat, "blk", axis=0, tiled=False)
    parts, first = [], 0
    for member in packed:
        count = member.size // 128
        parts.append(complete[:, first : first + count])
        first += count
    grad_out = parts[0].reshape(-1, D).T.astype(f32)
    grad_in = parts[1].reshape(-1, D).T.astype(f32)
    grad_qkv = parts[2].reshape(-1, D).T.astype(f32)
    grad_attn = parts[3].reshape(-1, D).T.astype(f32)
    tail_all = parts[4].reshape(side, tail.shape[1])
    grad_pos = tail_all[:, :span].T.astype(f32)
    grad_proj = tail_all[:, span : span + VDIM].T.astype(f32)
    rest = tail_all[:, span + VDIM : span + VDIM + vector_cols + 1].astype(f32)
    grad_vector = rest[:, :vector_cols].reshape(1, -1)
    grad_bias = rest[:, vector_cols].reshape(1, -1)

    per = blocks // MATRICES
    turn_of = myself // per

    def padded(rows):
        return jnp.pad(rows, ((0, 0), (0, wide_rows - rows.shape[1]), (0, 0)))

    def blocked(shard):
        return padded(shard.T.reshape(blocks, -1, D))

    old = jnp.stack([blocked(member) for member in (m_qkv, m_attn, m_in, m_out)])
    old = lax.dynamic_index_in_dim(old, turn_of, 0, keepdims=False).reshape(-1, D)
    proj_rows = g_tail[:, span : span + VDIM]
    proj_fill = round_up(proj_rows.size // 128, 8) * 128
    proj_flat = jnp.pad(proj_rows.reshape(-1), (0, round_up(proj_fill, 8 * D) - proj_rows.size))
    proj_flat = proj_flat.reshape(-1, D)
    sends = [padded(member[None])[0] for member in (g_qkv, g_attn, g_in, g_out)]
    sends = jnp.stack([jnp.concatenate([member, proj_flat], axis=0) for member in sends])
    sends = jnp.repeat(sends, per, axis=0)
    taken = lax.all_to_all(sends, "blk", 0, 0, tiled=True)
    moment = muon_moment * old + factor * taken[:, :wide_rows].reshape(-1, D).astype(f32)
    proj_taken = taken[:, wide_rows:].reshape(blocks, -1)[:, : proj_rows.size].reshape(-1, VDIM)
    proj_moment = muon_moment * m_proj.T + factor * proj_taken.astype(f32)

    def gram_of(rows):
        return lax.dot_general(
            rows,
            rows,
            (((0,), (0,)), ((), ())),
            precision=lax.Precision.HIGH,
            preferred_element_type=f32,
        )

    gram_proj = gram_of(proj_moment).reshape(-1)
    gram_proj = jnp.pad(gram_proj, (0, round_up(gram_proj.size, 16 * D) - gram_proj.size))
    grams = jnp.concatenate([gram_of(moment), gram_proj.reshape(-1, D)], axis=0)
    grams = sum_narrow(grams, narrow)
    gram_proj = grams[D:].reshape(-1)[: VDIM * VDIM].reshape(VDIM, VDIM)
    share = moment.shape[0] // per
    mine = lax.dynamic_slice_in_dim(moment, (myself % per) * share, share, axis=0)
    ortho, ortho_proj = newton_chains(grams[:D], mine, gram_proj, proj_moment)
    ortho = lax.all_gather(ortho, "blk", axis=0, tiled=False)
    ortho = ortho.reshape(MATRICES, blocks, wide_rows, D)

    def unblocked(index, rows):
        return ortho[index, :, :rows].reshape(-1, D).T.astype(f32)

    orthos = (
        unblocked(0, g_qkv.shape[0]),
        unblocked(1, attn_rows),
        unblocked(2, wide_rows),
        unblocked(3, wide_rows),
        ortho_proj.T,
    )

    table_new, table_m_new, table_v_new = adam_step(
        table, table_m, table_v, factor * table_grad, adam_rate
    )
    pos_new, pos_m_new, pos_v_new = adam_step(
        pos_table, pos_m, pos_v, factor * grad_pos, adam_rate
    )
    vector_new, vector_m_new, vector_v_new = adam_step(
        vector, vector_m, vector_v, factor * grad_vector, vector_rate
    )
    masters = (w_qkv, w_attn, w_in, w_out, w_proj)
    rates = (muon_rate, attn_rate, muon_rate, muon_rate, muon_rate)
    olds = (m_qkv, m_attn, m_in, m_out, m_proj)
    grads = (grad_qkv, grad_attn, grad_in, grad_out, grad_proj)
    moments = [muon_moment * before + factor * grad for before, grad in zip(olds, grads)]
    updated = []
    for weight, ortho_part, rate in zip(masters, orthos, rates):
        long_side = max(weight.shape[0], weight.shape[1] * narrow)
        updated.append(weight - rate * (0.2 * long_side**0.5 * ortho_part + weight_decay * weight))
    return (
        loss,
        grad_norm,
        table_new,
        table_m_new,
        table_v_new,
        pos_new,
        pos_m_new,
        pos_v_new,
        vector_new,
        vector_m_new,
        vector_v_new,
        updated[0],
        moments[0],
        updated[1],
        moments[1],
        updated[2],
        moments[2],
        updated[3],
        moments[3],
        updated[4],
        moments[4],
        factor * grad_bias,
    )


def solution(mesh):
    ids = P(None, ("blk", "narrow"), None)
    rows = P(("blk", "narrow"), None)
    cols = P(None, "narrow")
    group = P(None, "narrow", None)
    in_specs = (ids, ids, P(None, ("blk", "narrow")), group, group) + (rows,) * 3 + (cols,) * 16
    out_specs = (P(), P()) + (rows,) * 3 + (cols,) * 17
    return jax.shard_map(body, mesh=mesh, in_specs=in_specs, out_specs=out_specs, check_vma=False)
```

time: 3690 us -> 852 us (0.23)
  waiting for transfers between devices: 2160 us -> 267 us
  matrix products: 656 us -> 136 us
  blocking collectives: 278 us -> 14.3 us
  other arithmetic: 362 us -> 135 us
  Pallas kernels: 0 us -> 109 us
  local copies, waits for them, and re-layouts: 182 us -> 103 us
  starting transfers between devices: 2.82 us -> 58.2 us
    reduce_scatter x13 -> x0, waiting for transfers between devices: 1510 us -> none  [the longest x1 771 us: body(): lax.psum_scatter(jax.ops.segment_sum(jnp.where(inside[:, None], all_rows,...]
    dot_general x165 -> x26, matrix products: 656 us -> 136 us  [the longest x8 45.2 us: dot_nn(): lax.dot_general(left, right, (((1,), (0,)), ((), ())), preferred_element_...]
    all_gather x10 -> x7, waiting for transfers between devices: 540 us -> 54 us  [the longest x5 30.5 us: gather(): return lax.all_gather(shard, 'narrow', axis=0, tiled=True)]
    all_gather x11 -> x0, blocking collectives: 199 us -> none  [the longest x6 109 us: combined_all(): pieces = jax.tree.map(lambda part: lax.all_gather(part, axis), value)]
    scatter-add x1 -> x0, other arithmetic: 141 us -> none  [body(): jax.ops.segment_sum(jnp.where(inside[:, None], all_rows, 0.0), jnp.where(...]
    psum x1 -> x0, waiting for transfers between devices: 114 us -> none  [body(): lax.psum((shards[0], shards[1], shards[2], shards[3], shards[4], shards[5...]
    pallas_call x0 -> x3, Pallas kernels: none -> 109 us  [the longest x2 58.6 us: attention_call(): pl.pallas_call(functools.partial(kernel, query_len=query_len, span=span),...]
    ppermute x0 -> x18, waiting for transfers between devices: none -> 108 us  [swap(): lax.ppermute(value, axis, [(place, place ^ bit) for place in range(size)])]
  transfers between devices with their start and end apart: 27 -> 37, of which waited for: 21 -> 17; matrix products, arithmetic and copies ran while one was open for 12% -> 27% of each run, Pallas kernels for 0% -> 9%
where the time goes in v1:
time: 852 us; the launch traced here: 845 us
  waiting for transfers between devices  267 us (31%)
  matrix products  136 us (16%)
  other arithmetic  135 us (16%)
  Pallas kernels  109 us (13%)
  local copies, waits for them, and re-layouts  103 us (12%)
  starting transfers between devices  58.2 us (7%)
  between operations  22.2 us (3%)
  blocking collectives  14.3 us (2%)
    ppermute x18, waiting for transfers between devices, swap(): lax.ppermute(value, axis, [(place, place ^ bit) for place in range(size)])  108 us
    pallas_call x2, Pallas kernels, attention_call(): pl.pallas_call(functools.partial(kernel, query_len=query_len, span=span),...  58.6 us
    unnamed x248, local copies, waits for them, and re-layouts  54.2 us
    pallas_call x1, Pallas kernels, newton_chains(): pl.pallas_call(chain_kernel, out_shape=(jax.ShapeDtypeStruct(rows.shape,...  50.5 us
    dot_general x8, matrix products, dot_nn(): lax.dot_general(left, right, (((1,), (0,)), ((), ())), preferred_element_...  45.2 us
    dot_general x8, matrix products, dot_tn(): lax.dot_general(left, right, (((0,), (0,)), ((), ())), preferred_element_...  42.3 us
    all_to_all x1, waiting for transfers between devices, body(): lax.all_to_all(sent_rows, both, 0, 0, tiled=True)  41.5 us
    dot_general x5, matrix products, dot_nt(): lax.dot_general(left, right, (((1,), (1,)), ((), ())), preferred_element_...  37 us
  transfers between devices with their start and end apart: 37, of which 17 were waited for; matrix products, arithmetic and copies ran while one was open for 27% of the time, Pallas kernels for 9%

profile of v1, /device:TPU:0, one launch (start us, length us, event | category | flops | bytes accessed | tf_op | source)
XLA Modules:
  0.0 845.1 jit_solution(15499514745439361620)
XLA Ops:
  17.9 14.3 %all_to_all.66 = s32[32,1,40]{2,1,0:T(1,128)S(1)} all-to-all(s32[32,1,40]{2,1,0:T(1,128)S(1)} %bitcast.248), channel_id=1, replica_groups=mesh['blk'=8,'narrow'=4] {'blk','narrow'}, dimensions={0} | all-to-all | bytes 10240 | tf_op jit(solution)/shard_map/all_to_all | solution.py:409
  34.0 6.3 convolution_convert_fusion.4
  48.5 41.5 %all-to-all-done.1 = bf16[32,40,768]{2,1,0:T(8,128)(2,1)} async-done(((bf16[32,40,768]{2,1,0:T(8,128)(2,1)}), bf16[32,40,768]{2,1,0:T(8,128)(2,1)}, u32[]{:S(2)}, u32[]{:S(2)}) %all-to-all-start.1) | async-done | bytes 1966112 | tf_op jit(solution)/shard_map/all_to_all | solution.py:413
  96.4 8.7 %fusion.4.qkv_ref = bf16[1088,2304]{1,0:T(8,128)(2,1)} fusion(bf16[2304,768]{1,0:T(8,128)(2,1)} %all-gather.12.cloned.1.call-done, f32[2304]{0:T(1024)S(1)} %fusion.74, f32[1088,768]{1,0:T(8,128)S(1)} %get-tuple-element.282, f32[768]{0:T(1024)S(1)} %get-tuple-element.271, f32[768]{0:T(1024)S(1)} %get-tuple-element.272, f32[1088]{0:T(1024)S(1)} %add_rsqrt_fusion.3, ...), kind=kOutput, calls=%fused_computation.10 | convolution fusion | flops 3859562496 | bytes 11918848 | tf_op jit(solution)/shard_map/dot_general | solution.py:49
  105.1 22.4 %shard_map.399 = bf16[1088,768]{1,0:T(8,128)(2,1)S(1)} custom-call(s32[2]{0:T(128)S(1)} %bitcast.213, bf16[1088,2304]{1,0:T(8,128)(2,1)} %fusion.4.qkv_ref), custom_call_target="tpu_custom_call" | custom-call | flops 1610612736 | bytes 6684672 | tf_op jit(solution)/shard_map/pallas_call | solution.py:146
  134.1 9.6 %all-gather.16.cloned.1.call-done = bf16[3072,768]{0,1:T(8,128)(2,1)} async-done(((bf16[768,768]{0,1:T(8,128)(2,1)}), bf16[3072,768]{0,1:T(8,128)(2,1)}) %all-gather.16.cloned.1.call-update) | async-done | bytes 4718608 | tf_op jit(solution)/shard_map/all_gather | solution.py:380
  143.7 8.6 %convolution_add_fusion.1 = f32[1088,3072]{1,0:T(8,128)S(1)} fusion(bf16[3072,768]{0,1:T(8,128)(2,1)} %all-gather.16.cloned.1.call-done, f32[3072]{0:T(1024)S(1)} %slice.216, f32[1088,768]{1,0:T(8,128)} %copy-done.9, f32[768]{0:T(1024)S(1)} %get-tuple-element.266, f32[768]{0:T(1024)S(1)} %get-tuple-element.267, f32[1088]{0:T(1024)S(1)} %add_rsqrt_fusion.2, ...), kind=kOutput, calls=%fused_computation.2 | convolution fusion | flops 5141348352 | bytes 21457408 | tf_op jit(solution)/shard_map/dot_general | solution.py:49
  152.4 10.0 %fusion.3 = (f32[1088,3072]{1,0:T(8,128)}, bf16[1088,3072]{1,0:T(8,128)(2,1)}) fusion(f32[1088,3072]{1,0:T(8,128)S(1)} %convolution_add_fusion.1), kind=kLoop, calls=%fused_computation.6 | loop fusion | flops 33423360 | bytes 33423360 | tf_op jit(solution)/shard_map/add | solution.py:78
  162.4 20.8 %all-gather.18.cloned.1.call-done = bf16[3072,768]{0,1:T(8,128)(2,1)} async-done(((bf16[768,768]{0,1:T(8,128)(2,1)}), bf16[3072,768]{0,1:T(8,128)(2,1)}) %all-gather.18.cloned.1.call-update) | async-done | bytes 4718608 | tf_op jit(solution)/shard_map/all_gather | solution.py:380
  183.2 11.0 %fusion.115 = (f32[1088]{0:T(1024)S(1)}, f32[1088,768]{1,0:T(8,128)S(1)}) fusion(f32[768]{0:T(1024)S(1)} %get-tuple-element.265, bf16[1088,3072]{1,0:T(8,128)(2,1)} %get-tuple-element.26, bf16[3072,768]{0,1:T(8,128)(2,1)} %all-gather.18.cloned.1.call-done, f32[768]{0:T(1024)S(1)} %get-tuple-element.266, f32[768]{0:T(1024)S(1)} %get-tuple-element.267, ...), kind=kOutput, calls=%fused_computation.316 | convolution fusion | flops 5139676160 | bytes 18110208 | tf_op jit(solution)/shard_map/dot_general | solution.py:45
  206.2 6.5 all-to-all-done.2
  246.4 6.1 all-to-all-done.4
  263.7 11.2 %fusion.106 = (f32[3072]{0:T(1024)}, bf16[1088,3072]{1,0:T(8,128)(2,1)}) fusion(f32[1088,3072]{1,0:T(8,128)} %get-tuple-element.27, bf16[3072,768]{0,1:T(8,128)(2,1)S(1)} %bitcast.259, f32[1088,768]{1,0:T(8,128)S(1)} %get-tuple-element.230), kind=kOutput, calls=%fused_computation.307 | convolution fusion | flops 5151372288 | bytes 28127232 | tf_op jit(solution)/shard_map/dot_general | solution.py:49
  274.9 11.3 %multiply_reduce_fusion = (f32[768]{0:T(1024)}, f32[1088]{0:T(1024)S(1)}, f32[1088]{0:T(1024)S(1)}, f32[768]{0:T(1024)}, f32[1088,768]{1,0:T(8,128)S(1)}) fusion(f32[1088,768]{1,0:T(8,128)S(1)} %copy-done.10, f32[1088]{0:T(1024)S(1)} %copy-done.75, f32[1088]{0:T(1024)S(1)} %broadcast_multiply_fusion.7, f32[768]{0:T(1024)S(1)} %copy-done.79, ...), kind=kOutput, calls=%fused_computation.49 | convolution fusion | flops 5143851008 | bytes 21456896 | tf_op jit(solution)/shard_map/dot_general | solution.py:45
  292.2 36.2 %shard_map.400 = bf16[1088,2304]{1,0:T(8,128)(2,1)} custom-call(s32[2]{0:T(128)S(1)} %bitcast.215, bf16[1088,2304]{1,0:T(8,128)(2,1)} %fusion.4.qkv_ref, bf16[1088,768]{1,0:T(8,128)(2,1)S(1)} %convolution_convert_fusion.5.grad_ref), custom_call_target="tpu_custom_call" | custom-call | flops 4026531840 | bytes 10027008 | tf_op jit(solution)/shard_map/pallas_call | solution.py:146
  328.4 8.0 multiply_reduce_fusion.1
  357.3 7.3 fusion.96
  399.8 12.8 %collective-permute-done.8 = bf16[576,768]{1,0:T(8,128)(2,1)} collective-permute-done((bf16[576,768]{1,0:T(8,128)(2,1)}, bf16[576,768]{1,0:T(8,128)(2,1)}, u32[]{:S(2)}, u32[]{:S(2)}) %collective-permute-start.8) | collective-permute-done | bytes 884768 | tf_op jit(solution)/shard_map/ppermute | solution.py:173
  420.8 10.0 %fusion.48 = f32[3072,768]{1,0:T(8,128)S(1)} fusion(bf16[1088,3072]{1,0:T(8,128)(2,1)} %get-tuple-element.26, f32[1088,768]{1,0:T(8,128)} %copy-done.35), kind=kOutput, calls=%fused_computation.139 | convolution fusion | flops 5134663680 | bytes 19464192 | tf_op jit(solution)/shard_map/dot_general | solution.py:53
  452.8 9.2 %fusion.93 = f32[3072,768]{1,0:T(8,128)S(1)} fusion(bf16[1088,3072]{1,0:T(8,128)(2,1)} %get-tuple-element.236, f32[1088,768]{1,0:T(8,128)S(1)} %copy-done.11, f32[768]{0:T(1024)S(1)} %copy-done.89, f32[768]{0:T(1024)S(1)} %copy-done.80, f32[1088]{0:T(1024)S(1)} %copy-done.76, f32[1088]{0:T(1024)S(1)} %broadcast_multiply_fusion.7), kind=kOutput, calls=%fused_computation.303 | convolution fusion | flops 5138006016 | bytes 19479040 | tf_op jit(solution)/shard_map/dot_general | solution.py:53
  466.1 30.9 %collective-permute-done.2 = bf16[768,768]{1,0:T(8,128)(2,1)} collective-permute-done((bf16[768,768]{1,0:T(8,128)(2,1)}, bf16[768,768]{1,0:T(8,128)(2,1)}, u32[]{:S(2)}, u32[]{:S(2)}) %collective-permute-start.2) | collective-permute-done | bytes 1179680 | tf_op jit(solution)/shard_map/ppermute | solution.py:173
  509.3 27.4 %collective-permute-done.5 = bf16[768,768]{1,0:T(8,128)(2,1)S(1)} collective-permute-done((bf16[768,768]{1,0:T(8,128)(2,1)S(1)}, bf16[768,768]{1,0:T(8,128)(2,1)S(1)}, u32[]{:S(2)}, u32[]{:S(2)}) %collective-permute-start.5) | collective-permute-done | bytes 1179680 | tf_op jit(solution)/shard_map/ppermute | solution.py:173
  539.8 6.3 all-to-all-start.7
  550.5 6.7 multiply_reduce_fusion.7
  558.0 16.4 %all-to-all-done.7 = bf16[8,96,768]{2,1,0:T(8,128)(2,1)S(1)} async-done(((bf16[8,96,768]{2,1,0:T(8,128)(2,1)}), bf16[8,96,768]{2,1,0:T(8,128)(2,1)S(1)}, u32[]{:S(2)}, u32[]{:S(2)}) %all-to-all-start.7) | async-done | bytes 1179680 | tf_op jit(solution)/shard_map/all_to_all | solution.py:196
  583.9 6.7 all-to-all-done.11
  606.4 20.7 %all-to-all-done.12 = bf16[8,104,768]{2,1,0:T(8,128)(2,1)} async-done(((bf16[8,104,768]{2,1,0:T(8,128)(2,1)}), bf16[8,104,768]{2,1,0:T(8,128)(2,1)}, u32[]{:S(2)}, u32[]{:S(2)}) %all-to-all-start.12) | async-done | bytes 1277984 | tf_op jit(solution)/shard_map/all_to_all | solution.py:620
  632.3 6.6 fusion.37
  651.1 28.1 %collective-permute-done.16 = f32[400,768]{1,0:T(8,128)} collective-permute-done((f32[400,768]{1,0:T(8,128)}, f32[400,768]{1,0:T(8,128)}, u32[]{:S(2)}, u32[]{:S(2)}) %collective-permute-start.16) | collective-permute-done | bytes 1228832 | tf_op jit(solution)/shard_map/ppermute | solution.py:173
  693.1 50.5 %shard_map.401 = (bf16[384,768]{1,0:T(8,128)(2,1)}, f32[192,128]{1,0:T(8,128)}) custom-call(f32[768,768]{1,0:T(8,128)} %pad_maximum_fusion.1.refs_0_, f32[128,128]{1,0:T(8,128)} %slice.239.refs_1_, f32[384,768]{1,0:T(8,128)} %dynamic-slice_add_fusion.refs_2_, f32[192,128]{1,0:T(8,128)} %copy-done.54), custom_call_target="tpu_custom_call" | custom-call | flops 42385539072 | bytes 4718592 | tf_op jit(solution)/shard_map/pallas_call | solution.py:316
  749.7 8.1 multiply_subtract_fusion
  798.5 23.5 %all-gather.22.cloned.1.call-done = bf16[3072,768]{1,0:T(8,128)(2,1)} async-done(((bf16[384,768]{1,0:T(8,128)(2,1)}), bf16[3072,768]{1,0:T(8,128)(2,1)}) %all-gather.22.cloned.1.call-update) | async-done | bytes 4718608 | tf_op jit(solution)/shard_map/all_gather | solution.py:642
  (524 shorter events, 319.0 us)
Async XLA Ops:
  7.2 38.2 %all-gather.10.cloned.1.call-start = ((), (), s32[]{:S(2)}) async-start(), calls=%async_computation.13 | async-start | bytes 1474560 | tf_op jit(solution)/shard_map/all_gather | solution.py:380
  11.0 85.4 %all-gather.12.cloned.1.call-start = ((), (), s32[]{:S(2)}) async-start(), calls=%async_computation.14 | async-start | bytes 4423680 | tf_op jit(solution)/shard_map/all_gather | solution.py:380
  13.6 113.9 %all-gather.14.cloned.1.call-start = ((), (), s32[]{:S(2)}) async-start(), calls=%async_computation.15 | async-start | bytes 1474560 | tf_op jit(solution)/shard_map/all_gather | solution.py:380
  14.4 129.3 %all-gather.16.cloned.1.call-start = ((), (), s32[]{:S(2)}) async-start(), calls=%async_computation.16 | async-start | bytes 5898240 | tf_op jit(solution)/shard_map/all_gather | solution.py:380
  40.3 49.7 %all-to-all-start.1 = ((bf16[32,40,768]{2,1,0:T(8,128)(2,1)}), bf16[32,40,768]{2,1,0:T(8,128)(2,1)}, u32[]{:S(2)}, u32[]{:S(2)}) async-start(bf16[32,40,768]{2,1,0:T(8,128)(2,1)} %bitcast.238), calls=%async_computation.1 | async-start | bytes 3932160 | tf_op jit(solution)/shard_map/all_to_all | solution.py:413
  44.0 139.2 %all-gather.18.cloned.1.call-start = ((), (), s32[]{:S(2)}) async-start(), calls=%async_computation.17 | async-start | bytes 5898240 | tf_op jit(solution)/shard_map/all_gather | solution.py:380
  199.8 12.9 %all-to-all-start.2 = ((bf16[8,64,128]{2,1,0:T(8,128)(2,1)}), bf16[8,64,128]{2,1,0:T(8,128)(2,1)S(1)}, u32[]{:S(2)}, u32[]{:S(2)}) async-start(bf16[8,64,128]{2,1,0:T(8,128)(2,1)} %broadcast_in_dim.107), calls=%async_computation.2 | async-start | bytes 262144 | tf_op jit(solution)/shard_map/all_to_all | solution.py:169
  239.8 12.7 %all-to-all-start.4 = ((f32[8,2,32,128]{3,2,1,0:T(8,128)}), f32[8,2,32,128]{3,2,1,0:T(8,128)}, u32[]{:S(2)}, u32[]{:S(2)}) async-start(f32[8,2,32,128]{3,2,1,0:T(8,128)} %bitcast.241), calls=%async_computation.4 | async-start | bytes 524288 | tf_op jit(solution)/shard_map/all_to_all | solution.py:475
  344.5 24.9 %collective-permute-start.10 = (bf16[192,768]{1,0:T(8,128)(2,1)}, bf16[192,768]{1,0:T(8,128)(2,1)}, u32[]{:S(2)}, u32[]{:S(2)}) collective-permute-start(bf16[192,768]{1,0:T(8,128)(2,1)} %get-tuple-element.254), channel_id=1, source_target_pairs={{0,1},{1,0},{2,3},{3,2},{4,5},{5,4},{6,7},{7,6},{8,9},{9,8},{10,11... | collective-permute-start | bytes 884744 | tf_op jit(solution)/shard_map/ppermute | solution.py:173
  356.8 15.1 %collective-permute-start.13 = (f32[192,768]{1,0:T(8,128)}, f32[192,768]{1,0:T(8,128)}, u32[]{:S(2)}, u32[]{:S(2)}) collective-permute-start(f32[192,768]{1,0:T(8,128)} %get-tuple-element.252), channel_id=1, source_target_pairs={{0,1},{1,0},{2,3},{3,2},{4,5},{5,4},{6,7},{7,6},{8,9},{9,8},{10,11... | collective-permute-start | bytes 1769480 | tf_op jit(solution)/shard_map/ppermute | solution.py:173
  368.9 18.1 %collective-permute-start.7 = (bf16[576,768]{1,0:T(8,128)(2,1)}, bf16[576,768]{1,0:T(8,128)(2,1)}, u32[]{:S(2)}, u32[]{:S(2)}) collective-permute-start(bf16[576,768]{1,0:T(8,128)(2,1)} %get-tuple-element.244), channel_id=1, source_target_pairs={{0,1},{1,0},{2,3},{3,2},{4,5},{5,4},{6,7},{7,6},{8,9},{9,8},{10,11... | collective-permute-start | bytes 2654216 | tf_op jit(solution)/shard_map/ppermute | solution.py:173
  369.4 21.0 %collective-permute-start.12 = (f32[192,768]{1,0:T(8,128)}, f32[192,768]{1,0:T(8,128)}, u32[]{:S(2)}, u32[]{:S(2)}) collective-permute-start(f32[192,768]{1,0:T(8,128)} %get-tuple-element.251), channel_id=1, source_target_pairs={{0,1},{1,0},{2,3},{3,2},{4,5},{5,4},{6,7},{7,6},{8,9},{9,8},{10,11... | collective-permute-start | bytes 1769480 | tf_op jit(solution)/shard_map/ppermute | solution.py:173
  371.3 10.1 %collective-permute-start.11 = (bf16[192,768]{1,0:T(8,128)(2,1)}, bf16[192,768]{1,0:T(8,128)(2,1)}, u32[]{:S(2)}, u32[]{:S(2)}) collective-permute-start(bf16[192,768]{1,0:T(8,128)(2,1)} %add_convert_fusion.8), channel_id=1, source_target_pairs={{0,2},{1,3},{2,0},{3,1},{4,6},{5,7},{6,4},{7,5},{8,10},{9,11},{10,... | collective-permute-start | bytes 884744 | tf_op jit(solution)/shard_map/ppermute | solution.py:173
  373.8 20.3 %collective-permute-start.14 = (f32[192,768]{1,0:T(8,128)}, f32[192,768]{1,0:T(8,128)}, u32[]{:S(2)}, u32[]{:S(2)}) collective-permute-start(f32[192,768]{1,0:T(8,128)} %dynamic-slice_add_fusion.1), channel_id=1, source_target_pairs={{0,2},{1,3},{2,0},{3,1},{4,6},{5,7},{6,4},{7,5},{8,10},{9,11},{10,... | collective-permute-start | bytes 1769480 | tf_op jit(solution)/shard_map/ppermute | solution.py:173
  376.0 23.8 %collective-permute-start.6 = (bf16[576,768]{1,0:T(8,128)(2,1)}, bf16[576,768]{1,0:T(8,128)(2,1)S(1)}, u32[]{:S(2)}, u32[]{:S(2)}) collective-permute-start(bf16[576,768]{1,0:T(8,128)(2,1)} %get-tuple-element.243), channel_id=1, source_target_pairs={{0,1},{1,0},{2,3},{3,2},{4,5},{5,4},{6,7},{7,6},{8,9},{9,8},{10,11... | collective-permute-start | bytes 2654216 | tf_op jit(solution)/shard_map/ppermute | solution.py:173
  383.5 12.7 %all-to-all-start.9 = ((bf16[8,24,768]{2,1,0:T(8,128)(2,1)}), bf16[8,24,768]{2,1,0:T(8,128)(2,1)S(1)}, u32[]{:S(2)}, u32[]{:S(2)}) async-start(bf16[8,24,768]{2,1,0:T(8,128)(2,1)} %bitcast.29), calls=%async_computation.9 | async-start | bytes 589824 | tf_op jit(solution)/shard_map/all_to_all | solution.py:196
  389.8 22.9 %collective-permute-start.8 = (bf16[576,768]{1,0:T(8,128)(2,1)}, bf16[576,768]{1,0:T(8,128)(2,1)}, u32[]{:S(2)}, u32[]{:S(2)}) collective-permute-start(bf16[576,768]{1,0:T(8,128)(2,1)} %add_convert_fusion.6), channel_id=1, source_target_pairs={{0,2},{1,3},{2,0},{3,1},{4,6},{5,7},{6,4},{7,5},{8,10},{9,11},{10,... | collective-permute-start | bytes 2654216 | tf_op jit(solution)/shard_map/ppermute | solution.py:173
  396.2 19.3 %all-to-all-start.10 = ((f32[8,24,768]{2,1,0:T(8,128)}), f32[8,24,768]{2,1,0:T(8,128)S(1)}, u32[]{:S(2)}, u32[]{:S(2)}) async-start(f32[8,24,768]{2,1,0:T(8,128)} %bitcast.32), calls=%async_computation.10 | async-start | bytes 1179648 | tf_op jit(solution)/shard_map/all_to_all | solution.py:196
  416.4 26.5 %all-to-all-start.8 = ((bf16[8,72,768]{2,1,0:T(8,128)(2,1)}), bf16[8,72,768]{2,1,0:T(8,128)(2,1)S(1)}, u32[]{:S(2)}, u32[]{:S(2)}) async-start(bf16[8,72,768]{2,1,0:T(8,128)(2,1)} %bitcast.28), calls=%async_computation.8 | async-start | bytes 1769472 | tf_op jit(solution)/shard_map/all_to_all | solution.py:196
  436.1 11.6 %collective-permute-start.1 = (bf16[768,768]{1,0:T(8,128)(2,1)}, bf16[768,768]{1,0:T(8,128)(2,1)}, u32[]{:S(2)}, u32[]{:S(2)}) collective-permute-start(bf16[768,768]{1,0:T(8,128)(2,1)} %get-tuple-element.242), channel_id=1, source_target_pairs={{0,1},{1,0},{2,3},{3,2},{4,5},{5,4},{6,7},{7,6},{8,9},{9,8},{10,11... | collective-permute-start | bytes 3538952 | tf_op jit(solution)/shard_map/ppermute | solution.py:173
  443.8 57.0 %all-to-all-start.5 = ((bf16[32,40,768]{2,1,0:T(8,128)(2,1)}), bf16[32,40,768]{2,1,0:T(8,128)(2,1)}, u32[]{:S(2)}, u32[]{:S(2)}) async-start(bf16[32,40,768]{2,1,0:T(8,128)(2,1)} %bitcast.24), calls=%async_computation.5 | async-start | bytes 3932160 | tf_op jit(solution)/shard_map/all_to_all | solution.py:524
  447.4 18.7 %collective-permute-start = (bf16[768,768]{1,0:T(8,128)(2,1)}, bf16[768,768]{1,0:T(8,128)(2,1)}, u32[]{:S(2)}, u32[]{:S(2)}) collective-permute-start(bf16[768,768]{1,0:T(8,128)(2,1)} %get-tuple-element.241), channel_id=1, source_target_pairs={{0,1},{1,0},{2,3},{3,2},{4,5},{5,4},{6,7},{7,6},{8,9},{9,8},{10,11... | collective-permute-start | bytes 3538952 | tf_op jit(solution)/shard_map/ppermute | solution.py:173
  451.1 46.0 %collective-permute-start.2 = (bf16[768,768]{1,0:T(8,128)(2,1)}, bf16[768,768]{1,0:T(8,128)(2,1)}, u32[]{:S(2)}, u32[]{:S(2)}) collective-permute-start(bf16[768,768]{1,0:T(8,128)(2,1)} %add_convert_fusion.4), channel_id=1, source_target_pairs={{0,2},{1,3},{2,0},{3,1},{4,6},{5,7},{6,4},{7,5},{8,10},{9,11},{10,... | collective-permute-start | bytes 3538952 | tf_op jit(solution)/shard_map/ppermute | solution.py:173
  465.9 40.0 %collective-permute-start.4 = (bf16[768,768]{1,0:T(8,128)(2,1)S(1)}, bf16[768,768]{1,0:T(8,128)(2,1)}, u32[]{:S(2)}, u32[]{:S(2)}) collective-permute-start(bf16[768,768]{1,0:T(8,128)(2,1)S(1)} %get-tuple-element.240), channel_id=1, source_target_pairs={{0,1},{1,0},{2,3},{3,2},{4,5},{5,4},{6,7},{7,6},{8,9},{9,8},{10,11... | collective-permute-start | bytes 3538952 | tf_op jit(solution)/shard_map/ppermute | solution.py:173
  500.8 38.9 %all-to-all-start.6 = ((bf16[8,96,768]{2,1,0:T(8,128)(2,1)}), bf16[8,96,768]{2,1,0:T(8,128)(2,1)S(1)}, u32[]{:S(2)}, u32[]{:S(2)}) async-start(bf16[8,96,768]{2,1,0:T(8,128)(2,1)} %bitcast.26), calls=%async_computation.6 | async-start | bytes 2359296 | tf_op jit(solution)/shard_map/all_to_all | solution.py:196
  508.2 28.4 %collective-permute-start.5 = (bf16[768,768]{1,0:T(8,128)(2,1)S(1)}, bf16[768,768]{1,0:T(8,128)(2,1)S(1)}, u32[]{:S(2)}, u32[]{:S(2)}) collective-permute-start(bf16[768,768]{1,0:T(8,128)(2,1)S(1)} %add_convert_fusion.2), channel_id=1, source_target_pairs={{0,2},{1,3},{2,0},{3,1},{4,6},{5,7},{6,4},{7,5},{8,10},{9,11},{10,... | collective-permute-start | bytes 3538952 | tf_op jit(solution)/shard_map/ppermute | solution.py:173
  539.8 34.7 %all-to-all-start.7 = ((bf16[8,96,768]{2,1,0:T(8,128)(2,1)}), bf16[8,96,768]{2,1,0:T(8,128)(2,1)S(1)}, u32[]{:S(2)}, u32[]{:S(2)}) async-start(bf16[8,96,768]{2,1,0:T(8,128)(2,1)} %bitcast.27), calls=%async_computation.7 | async-start | bytes 2359296 | tf_op jit(solution)/shard_map/all_to_all | solution.py:196
  580.4 10.1 %all-to-all-start.11 = ((f32[32,1,128]{2,1,0:T(1,128)}), f32[32,1,128]{2,1,0:T(1,128)}, u32[]{:S(2)}, u32[]{:S(2)}) async-start(f32[32,1,128]{2,1,0:T(1,128)} %broadcast_in_dim.188), calls=%async_computation.11 | async-start | bytes 32768 | tf_op jit(solution)/shard_map/all_to_all | solution.py:169
  591.7 35.5 %all-to-all-start.12 = ((bf16[8,104,768]{2,1,0:T(8,128)(2,1)}), bf16[8,104,768]{2,1,0:T(8,128)(2,1)}, u32[]{:S(2)}, u32[]{:S(2)}) async-start(bf16[8,104,768]{2,1,0:T(8,128)(2,1)} %bitcast.57), calls=%async_computation.12 | async-start | bytes 2555904 | tf_op jit(solution)/shard_map/all_to_all | solution.py:620
  596.0 162.5 %all-gather.20.cloned.1.call-start = ((), (), s32[]{:S(2)}) async-start(), calls=%async_computation.18 | async-start | bytes 4313088 | tf_op jit(solution)/shard_map/all_gather | solution.py:585
  649.4 29.7 %collective-permute-start.16 = (f32[400,768]{1,0:T(8,128)}, f32[400,768]{1,0:T(8,128)}, u32[]{:S(2)}, u32[]{:S(2)}) collective-permute-start(f32[400,768]{1,0:T(8,128)} %bitcast_add_fusion.8), channel_id=1, source_target_pairs={{0,2},{1,3},{2,0},{3,1},{4,6},{5,7},{6,4},{7,5},{8,10},{9,11},{10,... | collective-permute-start | bytes 3686408 | tf_op jit(solution)/shard_map/ppermute | solution.py:173
  650.8 171.3 %all-gather.22.cloned.1.call-start = ((), (), s32[]{:S(2)}) async-start(), calls=%async_computation.19 | async-start | bytes 5308416 | tf_op jit(solution)/shard_map/all_gather | solution.py:642
  (117 other events, 1139.5 us)
Sparse Core Ops, SparseCore 0:
  11.1 20.2 all-gather.9
  33.6 49.1 all-gather.11
  84.9 19.3 all-gather.13
  106.2 37.4 all-gather.15
  145.7 37.4 all-gather.17
  650.9 67.9 all-gather.19
  743.7 78.2 all-gather.21

commit v2 on v1

v2 whole, which is shorter than its diff:
```python
import functools

import jax
import jax.numpy as jnp
from jax import lax
from jax.experimental import pallas as pl
from jax.experimental.pallas import tpu as pltpu
from jax.sharding import PartitionSpec as P

D = 768
HEADS = 12
HDIM = 64
FF = 3072
VDIM = 128
STEP = 10
MATRICES = 4

norm_eps = 1e-12
smoothing = 0.1
masked = -1e30
newton_one = 3.4445
newton_two = -4.775
newton_three = 2.0315
muon_rate = 0.1
attn_rate = 1.0
muon_moment = 0.95
weight_decay = 0.01
adam_rate = 0.02
vector_rate = 0.25
beta_one = 0.9
beta_two = 0.95
adam_eps = 1e-08
clip_limit = 0.05

bf16 = jnp.bfloat16
f32 = jnp.float32
SLOT_CAPS = {960: 36, 120: 7}


def round_up(value, step):
    return -(-value // step) * step


def dot_nn(left, right):
    return lax.dot_general(left, right, (((1,), (0,)), ((), ())), preferred_element_type=f32)


def dot_nt(left, right):
    return lax.dot_general(left, right, (((1,), (1,)), ((), ())), preferred_element_type=f32)


def dot_tn(left, right):
    return lax.dot_general(left, right, (((0,), (0,)), ((), ())), preferred_element_type=f32)


def low(values):
    return values.astype(bf16)


def norm_forward(values, gain, shift):
    centred = values - jnp.mean(values, axis=-1, keepdims=True)
    spread = jnp.mean(centred * centred, axis=-1, keepdims=True)
    scale = lax.rsqrt(spread + norm_eps)
    hat = centred * scale
    return hat * gain + shift, hat, scale


def norm_backward(grad, hat, scale, gain):
    d_hat = grad * gain
    first = jnp.mean(d_hat, axis=-1, keepdims=True)
    second = jnp.mean(d_hat * hat, axis=-1, keepdims=True)
    return scale * (d_hat - first - hat * second)


def gelu_parts(values):
    cdf = 0.5 * (1.0 + lax.erf(values * (0.5**0.5)))
    density = jnp.exp(-0.5 * values * values) * 0.3989422804014327
    return values * cdf, cdf + values * density


def attention_forward_kernel(
    lens_ref, qkv_ref, out_ref, norm_ref, scores_one, scores_two, share_one, share_two, *, query_len, span
):
    used = lens_ref[pl.program_id(0)]
    bias_long = jnp.where(lax.broadcasted_iota(jnp.int32, (1, span), 1) < used, 0.0, masked)
    bias_short = jnp.zeros((1, query_len), f32)
    lane_of = lax.broadcasted_iota(jnp.int32, (16, 128), 1)
    norm_ref[...] = jnp.zeros_like(norm_ref)

    def attend(first, count, lane, half, bias, head, scores_ref, share_ref):
        rows, span_of = pl.ds(first, count), pl.ds(0, count)
        queries = qkv_ref[rows, pl.ds(lane, 128)][:, half] * bf16(HDIM**-0.5)
        keys = qkv_ref[rows, pl.ds(lane + D, 128)][:, half]
        values = qkv_ref[rows, pl.ds(lane + 2 * D, 128)][:, half]
        scores_ref[span_of, span_of] = dot_nt(queries, keys)
        for step in range(0, count, 16):
            here = pl.ds(step, 16)
            scores = scores_ref[here, span_of] + bias
            peak = jnp.max(scores, axis=-1, keepdims=True)
            exponent = jnp.exp(scores - peak)
            total = jnp.sum(exponent, axis=-1, keepdims=True)
            share_ref[here, span_of] = low(exponent * (1.0 / total))
            there = pl.ds(first + step, 16)
            norm_ref[there, :] = jnp.where(lane_of == head, peak + jnp.log(total), norm_ref[there, :])
        return dot_nn(share_ref[span_of, span_of], values)

    def pair(index, carry):
        lane = pl.multiple_of(index * 128, 128)
        for first, count, bias in ((0, query_len, bias_short), (query_len, span, bias_long)):
            one = attend(
                first, count, lane, slice(0, HDIM), bias, 2 * index, scores_one, share_one
            )
            two = attend(
                first, count, lane, slice(HDIM, 128), bias, 2 * index + 1, scores_two, share_two
            )
            out_ref[pl.ds(first, count), pl.ds(lane, 128)] = low(jnp.concatenate([one, two], axis=1))
        return carry

    lax.fori_loop(0, HEADS // 2, pair, 0)


def attention_forward(lens, qkv, query_len, span):
    length = query_len + span
    tokens = qkv.shape[0]
    micro_count = tokens // length
    block = pl.BlockSpec((length, 3 * D), lambda micro, lens: (micro, 0))
    square = [pltpu.VMEM((span, span), f32)] * 2 + [pltpu.VMEM((span, span), bf16)] * 2
    return pl.pallas_call(
        functools.partial(attention_forward_kernel, query_len=query_len, span=span),
        out_shape=(
            jax.ShapeDtypeStruct((tokens, D), bf16),
            jax.ShapeDtypeStruct((tokens, 128), f32),
        ),
        grid_spec=pltpu.PrefetchScalarGridSpec(
            num_scalar_prefetch=1,
            grid=(micro_count,),
            in_specs=[block],
            out_specs=(
                pl.BlockSpec((length, D), lambda micro, lens: (micro, 0)),
                pl.BlockSpec((length, 128), lambda micro, lens: (micro, 0)),
            ),
            scratch_shapes=square,
        ),
        compiler_params=pltpu.CompilerParams(vmem_limit_bytes=48 * 1024 * 1024),
        cost_estimate=pl.CostEstimate(
            flops=8 * micro_count * HEADS * span * span * HDIM,
            bytes_accessed=tokens * 8 * D,
            transcendentals=micro_count * HEADS * span * span,
        ),
    )(lens, qkv)


def attention_backward_kernel(
    lens_ref,
    qkv_ref,
    grad_ref,
    norm_ref,
    inner_ref,
    out_ref,
    scores_one,
    scores_two,
    slopes_one,
    slopes_two,
    share_one,
    share_two,
    d_one,
    d_two,
    *,
    query_len,
    span,
):
    used = lens_ref[pl.program_id(0)]
    bias_long = jnp.where(lax.broadcasted_iota(jnp.int32, (span, 1), 0) < used, 0.0, masked)
    bias_short = jnp.zeros((query_len, 1), f32)

    def attend(first, count, lane, half, bias, head, scores_ref, slopes_ref, share_ref, d_ref):
        rows, span_of = pl.ds(first, count), pl.ds(0, count)
        queries = qkv_ref[rows, pl.ds(lane, 128)][:, half] * bf16(HDIM**-0.5)
        keys = qkv_ref[rows, pl.ds(lane + D, 128)][:, half]
        values = qkv_ref[rows, pl.ds(lane + 2 * D, 128)][:, half]
        grads = grad_ref[rows, pl.ds(lane, 128)][:, half]
        lanes = slice(0, count) if first else slice(span, span + count)
        norm = norm_ref[0, pl.ds(head, 1), :][:, lanes]
        inner = inner_ref[0, pl.ds(head, 1), :][:, lanes]
        scores_ref[span_of, span_of] = dot_nt(keys, queries)
        slopes_ref[span_of, span_of] = dot_nt(values, grads)
        for step in range(0, count, 16):
            here = pl.ds(step, 16)
            scores = scores_ref[here, span_of] + bias[step : step + 16]
            share = jnp.exp(scores - norm)
            share_ref[here, span_of] = low(share)
            d_ref[here, span_of] = low(share * (slopes_ref[here, span_of] - inner))
        d_scores = d_ref[span_of, span_of]
        d_values = dot_nn(share_ref[span_of, span_of], grads)
        d_keys = dot_nn(d_scores, queries)
        d_queries = dot_tn(d_scores, keys) * HDIM**-0.5
        return d_queries, d_keys, d_values

    def pair(index, carry):
        lane = pl.multiple_of(index * 128, 128)
        for first, count, bias in ((0, query_len, bias_short), (query_len, span, bias_long)):
            one = attend(
                first,
                count,
                lane,
                slice(0, HDIM),
                bias,
                2 * index,
                scores_one,
                slopes_one,
                share_one,
                d_one,
            )
            two = attend(
                first,
                count,
                lane,
                slice(HDIM, 128),
                bias,
                2 * index + 1,
                scores_two,
                slopes_two,
                share_two,
                d_two,
            )
            for part in range(3):
                both = jnp.concatenate([one[part], two[part]], axis=1)
                out_ref[pl.ds(first, count), pl.ds(lane + part * D, 128)] = low(both)
        return carry

    lax.fori_loop(0, HEADS // 2, pair, 0)


def attention_backward(lens, qkv, grad, norm, inner, query_len, span):
    length = query_len + span
    tokens = qkv.shape[0]
    micro_count = tokens // length
    heads = norm.shape[1]

    def block(width):
        return pl.BlockSpec((length, width), lambda micro, lens: (micro, 0))

    row = pl.BlockSpec((1, heads, length), lambda micro, lens: (micro, 0, 0))
    square = [pltpu.VMEM((span, span), f32)] * 4 + [pltpu.VMEM((span, span), bf16)] * 4
    return pl.pallas_call(
        functools.partial(attention_backward_kernel, query_len=query_len, span=span),
        out_shape=jax.ShapeDtypeStruct((tokens, 3 * D), bf16),
        grid_spec=pltpu.PrefetchScalarGridSpec(
            num_scalar_prefetch=1,
            grid=(micro_count,),
            in_specs=[block(3 * D), block(D), row, row],
            out_specs=block(3 * D),
            scratch_shapes=square,
        ),
        compiler_params=pltpu.CompilerParams(vmem_limit_bytes=48 * 1024 * 1024),
        cost_estimate=pl.CostEstimate(
            flops=20 * micro_count * HEADS * span * span * HDIM,
            bytes_accessed=tokens * 14 * D,
            transcendentals=micro_count * HEADS * span * span,
        ),
    )(lens, qkv, grad, norm, inner)


def update_kernel(*refs, rate, scale):
    count = len(refs) // 3
    for weight, ortho, out in zip(refs[:count], refs[count : 2 * count], refs[2 * count :]):
        turned = ortho[...].astype(f32).T
        out[...] = weight[...] - rate * (scale * turned + weight_decay * weight[...])


def update_wide(weights, orthos, rate, scale):
    rows, columns = weights[0].shape
    step = 128
    weight_spec = pl.BlockSpec((rows, step), lambda place: (0, place))
    ortho_spec = pl.BlockSpec((step, rows), lambda place: (place, 0))
    count = len(weights)
    return pl.pallas_call(
        functools.partial(update_kernel, rate=rate, scale=scale),
        grid=(columns // step,),
        in_specs=[weight_spec] * count + [ortho_spec] * count,
        out_specs=(weight_spec,) * count,
        out_shape=(jax.ShapeDtypeStruct((rows, columns), f32),) * count,
        compiler_params=pltpu.CompilerParams(vmem_limit_bytes=32 * 1024 * 1024),
        cost_estimate=pl.CostEstimate(
            flops=4 * count * rows * columns,
            bytes_accessed=10 * count * rows * columns,
            transcendentals=0,
        ),
    )(*weights, *orthos)


def score_kernel(lens_ref, cycle_ref, vecs_ref, share_ref, scores_ref, *, query_len, span):
    micro = pl.program_id(0)
    blocks = cycle_ref.shape[0]
    mine = pl.ds(pl.multiple_of(micro * query_len, query_len), query_len)
    queries = jnp.concatenate([cycle_ref[place, mine, :] for place in range(blocks)], axis=0)
    first = pl.multiple_of(micro * (query_len + span) + query_len, query_len)
    sims = dot_nt(queries, vecs_ref[pl.ds(first, span), :])
    used = lax.broadcasted_iota(jnp.int32, (1, span), 1) < lens_ref[micro]
    scaled = jnp.where(used, sims / smoothing, masked)
    summit = jnp.max(scaled, axis=-1, keepdims=True)
    exponent = jnp.exp(scaled - summit)
    total = jnp.sum(exponent, axis=-1, keepdims=True)
    share_ref[0] = exponent / total
    smooth = smoothing * (summit + jnp.log(total))
    smooth = jnp.broadcast_to(smooth, (blocks * query_len, 128))
    scores_ref[0] = jnp.sum(smooth.reshape(blocks, query_len, 128), axis=1)


def score_forward(lens, cycle, vecs, query_len, span):
    blocks, micro_count = cycle.shape[0], lens.shape[0]
    rows = blocks * query_len
    return pl.pallas_call(
        functools.partial(score_kernel, query_len=query_len, span=span),
        out_shape=(
            jax.ShapeDtypeStruct((micro_count, rows, span), f32),
            jax.ShapeDtypeStruct((micro_count, blocks, 128), f32),
        ),
        grid_spec=pltpu.PrefetchScalarGridSpec(
            num_scalar_prefetch=1,
            grid=(micro_count,),
            in_specs=[
                pl.BlockSpec(cycle.shape, lambda micro, lens: (0, 0, 0)),
                pl.BlockSpec(vecs.shape, lambda micro, lens: (0, 0)),
            ],
            out_specs=(
                pl.BlockSpec((1, rows, span), lambda micro, lens: (micro, 0, 0)),
                pl.BlockSpec((1, blocks, 128), lambda micro, lens: (micro, 0, 0)),
            ),
        ),
        compiler_params=pltpu.CompilerParams(vmem_limit_bytes=48 * 1024 * 1024),
        cost_estimate=pl.CostEstimate(
            flops=2 * micro_count * rows * span * VDIM,
            bytes_accessed=4 * micro_count * rows * span,
            transcendentals=micro_count * rows * span,
        ),
    )(lens, cycle, vecs)


def loss_kernel(
    me_ref,
    every_ref,
    allowed_ref,
    hits_ref,
    share_ref,
    cycle_ref,
    vecs_ref,
    loss_ref,
    passage_ref,
    query_ref,
    *,
    query_len,
    span,
):
    me = me_ref[0]
    blocks = cycle_ref.shape[0]
    micro_count = share_ref.shape[0]
    every = every_ref[...]
    allowed = allowed_ref[...] > 0.0
    peak = jnp.max(jnp.where(allowed, every, masked), axis=0)
    mass = jnp.sum(jnp.where(allowed, jnp.exp(every - peak[None]), 0.0), axis=0)
    log_total = peak + jnp.log(mass)
    matched = jnp.sum(jnp.where(hits_ref[...] > 0.0, every, 0.0), axis=0)
    row = lax.broadcasted_iota(jnp.int32, log_total.shape, 0)
    mine = jnp.where(row % blocks == me, log_total - matched, 0.0)
    loss_ref[...] = jnp.broadcast_to(jnp.sum(mine, axis=0, keepdims=True), loss_ref.shape)
    d_scores = jnp.where(allowed_ref[me] > 0.0, jnp.exp(every_ref[me] - log_total), 0.0)
    d_scores = d_scores - hits_ref[me]
    for micro in range(micro_count):
        own = d_scores[micro * blocks : (micro + 1) * blocks]
        own = jnp.broadcast_to(own[:, None, :], (blocks, query_len, 128))
        own = own.reshape(blocks * query_len, 128)[:, 0:1]
        d_sims = low(own * share_ref[micro])
        here = slice(micro * query_len, (micro + 1) * query_len)
        queries = jnp.concatenate([cycle_ref[place, here, :] for place in range(blocks)], axis=0)
        first = micro * (query_len + span) + query_len
        passage_ref[micro] = dot_tn(d_sims, queries)
        d_queries = dot_nn(d_sims, vecs_ref[first : first + span, :])
        for place in range(blocks):
            rows = slice(place * query_len, (place + 1) * query_len)
            query_ref[place, here, :] = d_queries[rows]


def score_backward(me, every, allowed, hits, share, cycle, vecs, query_len, span):
    micro_count = share.shape[0]
    whole = pl.BlockSpec(memory_space=pltpu.VMEM)
    return pl.pallas_call(
        functools.partial(loss_kernel, query_len=query_len, span=span),
        out_shape=(
            jax.ShapeDtypeStruct((8, 128), f32),
            jax.ShapeDtypeStruct((micro_count, span, VDIM), f32),
            jax.ShapeDtypeStruct(cycle.shape, f32),
        ),
        in_specs=[pl.BlockSpec(memory_space=pltpu.SMEM)] + [whole] * 6,
        out_specs=(whole,) * 3,
        compiler_params=pltpu.CompilerParams(vmem_limit_bytes=48 * 1024 * 1024),
        cost_estimate=pl.CostEstimate(
            flops=4 * share.size * VDIM, bytes_accessed=4 * share.size, transcendentals=0
        ),
    )(me.reshape(1).astype(jnp.int32), every, allowed, hits, share, cycle, vecs)


def tail_kernel(rows_ref, x_ref, hat_ref, qkv_ref, proj_ref, *refs, query_len, span, micro_count):
    out_ref = refs[-1]
    length = query_len + span
    for first in range(0, span, 128):
        block = rows_ref[query_len + first : query_len + first + 128, :]
        for micro in range(1, micro_count):
            start = micro * length + query_len + first
            block = block + rows_ref[start : start + 128, :]
        if first == 0:
            head = rows_ref[0:query_len, :]
            for micro in range(1, micro_count):
                head = head + rows_ref[micro * length : micro * length + query_len, :]
            block = jnp.concatenate([block[:query_len] + head, block[query_len:]], axis=0)
        out_ref[:, first : first + 128] = block.T

    def fold(values):
        return jnp.sum(values.reshape(-1, 8, D), axis=0)

    sums = [jnp.zeros((8, D), f32)] * 4
    for first in range(0, micro_count * length, 32):
        here = pl.ds(first, 32)
        d_x = x_ref[here, :]
        terms = (
            d_x * hat_ref[here, :],
            d_x,
            qkv_ref[here, 0:D].astype(f32),
            qkv_ref[here, 2 * D : 3 * D].astype(f32),
        )
        sums = [total + fold(term) for total, term in zip(sums, terms)]
    sums = [jnp.sum(total, axis=0, keepdims=True) for total in sums]
    for ref in refs[:-1]:
        sums = sums + [ref[:, first : first + D] for first in range(0, ref.shape[1], D)]
    sums.append(jnp.zeros((128 - len(sums), D), f32))
    out_ref[:, span : span + 128] = jnp.concatenate(sums, axis=0).T
    out_ref[:, span + 128 :] = proj_ref[...]


def late_sums(d_rows, d_x, x_hat, d_qkv, g_proj, early, query_len, span, micro_count):
    early = [member.reshape(1, -1) for member in early]
    whole = pl.BlockSpec(memory_space=pltpu.VMEM)
    return pl.pallas_call(
        functools.partial(
            tail_kernel, query_len=query_len, span=span, micro_count=micro_count
        ),
        out_shape=jax.ShapeDtypeStruct((D, span + 128 + VDIM), f32),
        in_specs=[whole] * (5 + len(early)),
        out_specs=whole,
        compiler_params=pltpu.CompilerParams(vmem_limit_bytes=48 * 1024 * 1024),
        cost_estimate=pl.CostEstimate(
            flops=8 * d_rows.size, bytes_accessed=20 * d_rows.size, transcendentals=0
        ),
    )(d_rows, d_x, x_hat, d_qkv, g_proj, *early)


def share_all(value, axes, count):
    spread = jnp.broadcast_to(value[None], (count,) + value.shape)
    return lax.all_to_all(spread, axes, 0, 0, tiled=True)


def swap(value, axis, size, bit):
    return lax.ppermute(value, axis, [(place, place ^ bit) for place in range(size)])


def gather_relative(shard, narrow):
    pieces = {0: shard}
    bit = narrow // 2
    while bit:
        for offset in list(pieces):
            pieces[offset ^ bit] = swap(pieces[offset], "narrow", narrow, bit)
        bit = bit // 2
    return [pieces[offset] for offset in range(narrow)]


def relative(whole, narrow):
    place = lax.axis_index("narrow")
    rows = whole.shape[0] // narrow
    return [
        lax.dynamic_slice_in_dim(whole, (place ^ offset) * rows, rows, axis=0)
        for offset in range(narrow)
    ]


def gram_kernel(factor_ref, old_ref, grad_ref, moment_ref, gram_ref):
    moment = muon_moment * old_ref[...] + factor_ref[0] * grad_ref[...].astype(f32)
    moment_ref[...] = moment
    high, rest = split(moment)
    size = moment.shape[1]
    side = size if gram_ref.shape[0] == size else size // 3

    def part(row):
        left = slice(row, row + side)
        right = slice(row, size)
        return (
            dot_tn(high[:, left], high[:, right])
            + dot_tn(high[:, left], rest[:, right])
            + dot_tn(rest[:, left], high[:, right])
        )

    gram_ref[0:side, :] = part(0)
    if side < size:
        gram_ref[side : 2 * side, 0 : 2 * side] = part(side)
        gram_ref[side : 2 * side, 2 * side : size] = part(2 * side)


def packed_gram(factor, old, grad):
    count, size = old.shape
    whole = pl.BlockSpec(memory_space=pltpu.VMEM)
    packed = size if size < 3 * 128 else 2 * size // 3
    return pl.pallas_call(
        gram_kernel,
        out_shape=(
            jax.ShapeDtypeStruct((count, size), f32),
            jax.ShapeDtypeStruct((packed, size), f32),
        ),
        in_specs=[pl.BlockSpec(memory_space=pltpu.SMEM), whole, whole],
        out_specs=(whole, whole),
        compiler_params=pltpu.CompilerParams(vmem_limit_bytes=48 * 1024 * 1024),
        cost_estimate=pl.CostEstimate(
            flops=4 * count * size * size, bytes_accessed=14 * count * size, transcendentals=0
        ),
    )(factor.reshape(1), old, grad)


def tie(*values):
    return lax.optimization_barrier(values)


class Reduction:
    def __init__(self, sent, kept, narrow, blocks, wire):
        self.narrow, self.blocks, self.wire = narrow, blocks, wire
        self.sent, self.kept = list(sent), list(kept)

    def across_core(self):
        self.got = [swap(member, "narrow", self.narrow, 1) for member in self.sent]

    def prepare(self):
        totals = [kept + got for kept, got in zip(self.kept, self.got)]
        half = len(totals) // 2
        while half > 1:
            for offset in range(half):
                got = swap(totals[offset + half].astype(self.wire), "narrow", self.narrow, 2 * half)
                totals[offset] = totals[offset] + got.astype(f32)
            half = half // 2
        self.kept = totals[0]
        self.outgoing = totals[-1].astype(self.wire)

    def across_narrow(self):
        self.prepare()
        self.send()

    def send(self):
        if self.narrow > 2:
            self.got = swap(self.outgoing, "narrow", self.narrow, 2)
        else:
            self.got = jnp.zeros_like(self.outgoing)

    def total(self):
        return self.kept + self.got.astype(f32)


def sum_everywhere(value, sizes):
    for axis, size in sizes:
        if size <= 8:
            swaps = [swap(value, axis, size, offset) for offset in range(1, size)]
            value = sum(swaps, value)
            continue
        bit = 1
        while bit < size:
            value = value + swap(value, axis, size, bit)
            bit = bit * 2
    return value


def sum_group(value, narrow, per, blocks):
    steps = [("narrow", narrow, 1)]
    steps = steps + [("blk", blocks, 1 << bit) for bit in range(per.bit_length() - 1)]
    for axis, size, bit in steps:
        halves = value.reshape(2, value.shape[0] // 2, value.shape[1])
        mine = (lax.axis_index(axis) // bit) & 1
        sent = lax.dynamic_index_in_dim(halves, 1 - mine, 0, keepdims=False)
        got = swap(sent, axis, size, bit)
        value = lax.dynamic_index_in_dim(halves, mine, 0, keepdims=False) + got
    bit = 2
    while bit < narrow:
        value = value + swap(value, "narrow", narrow, bit)
        bit = bit * 2
    for axis, size, bit in reversed(steps):
        other = swap(value, axis, size, bit)
        lower = (lax.axis_index(axis) // bit) & 1 == 0
        value = jnp.concatenate(
            [jnp.where(lower, value, other), jnp.where(lower, other, value)], axis=0
        )
    return value


def adam_step(weight, first, second, gradient, rate):
    first_new = beta_one * first + (1.0 - beta_one) * gradient
    second_new = beta_two * second + (1.0 - beta_two) * gradient * gradient
    update = (
        first_new
        / (1.0 - beta_one**STEP)
        / (jnp.sqrt(second_new / (1.0 - beta_two**STEP)) + adam_eps)
    )
    return (weight - rate * (update + weight_decay * weight), first_new, second_new)


def split(value):
    high = low(value)
    return high, low(value - high.astype(f32))


def chain_kernel(
    gram_in, rows_in, out, gram, rows, half, gram_l, gram_r, poly_l, poly_r, half_l, rows_l
):
    size, count = gram.shape[0], rows.shape[0]
    parts = 3 if gram_in.shape[0] < size else 1
    side = size // parts

    def put(left_ref, right_ref, value, row, column):
        for piece, first, second in ((value, row, column), (value.T, column, row)):
            high, rest = split(piece)
            width = piece.shape[1]
            if left_ref is not None:
                here = pl.ds(first, piece.shape[0])
                left_ref[here, pl.ds(second, width)] = high
                left_ref[here, pl.ds(size + second, width)] = high
                left_ref[here, pl.ds(2 * size + second, width)] = rest
            if right_ref is not None:
                there = pl.ds(second, width)
                right_ref[pl.ds(first, piece.shape[0]), there] = high
                right_ref[pl.ds(size + first, piece.shape[0]), there] = rest
                right_ref[pl.ds(2 * size + first, piece.shape[0]), there] = high
            if row == column:
                break

    def store(left_ref, right_ref, value, row):
        for place in range(row // side, parts):
            column = place * side
            put(left_ref, right_ref, value[:, column - row : column - row + side], row, column)

    def put_rows(value, first):
        high, rest = split(value)
        here = pl.ds(first, value.shape[0])
        rows_l[here, 0:size] = high
        rows_l[here, size : 2 * size] = high
        rows_l[here, 2 * size : 3 * size] = rest

    def packed(row):
        if parts == 1 or row == 0:
            return gram_in[0:side, :]
        if row == side:
            return gram_in[side : 2 * side, 0 : 2 * side]
        return gram_in[side : 2 * side, 2 * side : size]

    starts = [place * side for place in range(parts)]
    row_steps = [(first, min(256, count - first)) for first in range(0, count, 256)]
    diagonal = lax.broadcasted_iota(jnp.int32, (side, side), 0) == lax.broadcasted_iota(
        jnp.int32, (side, side), 1
    )
    trace = jnp.zeros((1, 1), f32)
    for row in starts:
        block = packed(row)[:, 0:side]
        trace = trace + jnp.sum(jnp.where(diagonal, block, 0.0), axis=(0, 1), keepdims=True)
    scale = 1.0 / (jnp.sqrt(trace) + 1e-07)
    for row in starts:
        block = packed(row) * (scale * scale)
        gram[pl.ds(row, side), pl.ds(row, size - row)] = block
        store(gram_l, gram_r, block, row)
    for first, step in row_steps:
        block = rows_in[pl.ds(first, step), :] * scale
        rows[pl.ds(first, step), :] = block
        put_rows(block, first)

    def product(left_ref, right_ref, row):
        return dot_nn(left_ref[pl.ds(row, side), :], right_ref[:, pl.ds(row, size - row)])

    def advance(last):
        for row in starts:
            here, there = pl.ds(row, side), pl.ds(row, size - row)
            square = product(gram_l, gram_r, row)
            poly = newton_two * gram[here, there] + newton_three * square
            store(None if last else poly_l, poly_r, poly, row)
        if not last:
            for row in starts:
                here, there = pl.ds(row, side), pl.ds(row, size - row)
                block = newton_one * gram[here, there] + product(poly_l, gram_r, row)
                half[here, there] = block
                store(half_l, None, block, row)
        for first, step in row_steps:
            here = pl.ds(first, step)
            block = newton_one * rows[here, :] + dot_nn(rows_l[here, :], poly_r[...])
            if last:
                out[here, :] = block.astype(out.dtype)
            else:
                rows[here, :] = block
                put_rows(block, first)
        if not last:
            for row in starts:
                here, there = pl.ds(row, side), pl.ds(row, size - row)
                block = newton_one * half[here, there] + product(half_l, poly_r, row)
                gram[here, there] = block
                store(gram_l, gram_r, block, row)

    def turn(_, carry):
        advance(False)
        return carry

    lax.fori_loop(0, 4, turn, 0)
    advance(True)


def newton_chain(gram, rows, dtype):
    size, count = rows.shape[1], rows.shape[0]
    wide, tall = ((size, 3 * size), bf16), ((3 * size, size), bf16)
    shapes = [((size, size), f32), ((count, size), f32), ((size, size), f32)]
    shapes = shapes + [wide, tall, wide, tall, wide, ((count, 3 * size), bf16)]
    whole = pl.BlockSpec(memory_space=pltpu.VMEM)
    return pl.pallas_call(
        chain_kernel,
        out_shape=jax.ShapeDtypeStruct(rows.shape, dtype),
        in_specs=[whole] * 2,
        out_specs=whole,
        scratch_shapes=[pltpu.VMEM(*shape) for shape in shapes],
        compiler_params=pltpu.CompilerParams(vmem_limit_bytes=56 * 1024 * 1024),
        cost_estimate=pl.CostEstimate(
            flops=6 * (13 * size + 5 * count) * size * size,
            bytes_accessed=8 * gram.size,
            transcendentals=0,
        ),
    )(gram, rows)


def body(
    query_ids,
    passage_ids,
    passage_len,
    positives,
    domains,
    table,
    table_m,
    table_v,
    pos_table,
    pos_m,
    pos_v,
    vector,
    vector_m,
    vector_v,
    w_qkv,
    m_qkv,
    w_attn,
    m_attn,
    w_in,
    m_in,
    w_out,
    m_out,
    w_proj,
    m_proj,
):
    blocks = lax.axis_size("blk")
    narrow = lax.axis_size("narrow")
    devices = blocks * narrow
    both = ("blk", "narrow")
    myself = lax.axis_index("blk")
    shard_rows = table.shape[0]
    micro_count, _, query_len = query_ids.shape
    span = passage_ids.shape[2]
    length = query_len + span
    tokens = micro_count * length

    side = D // narrow
    vector_cols = vector.shape[1] // side
    small = jnp.concatenate(
        [
            low(pos_table).T,
            low(w_proj).T,
            low(vector).reshape(side, vector_cols),
            jnp.zeros((side, D - span - VDIM - vector_cols), bf16),
        ],
        axis=1,
    )


    def gather(shard):
        return lax.all_gather(shard, "narrow", axis=0, tiled=True)


    def gather(shard):
        return lax.all_gather(shard, "narrow", axis=0, tiled=True)

    first = gather(jnp.concatenate([small, low(w_attn).T], axis=1))
    small, attn_t = first[:, :D], first[:, D:]
    qkv_t = gather(low(w_qkv).T)
    in_t = gather(low(w_in).T)
    out_t = gather(low(w_out).T)
    pos = small[:, :span].T.astype(f32)
    proj_t = small[:, span : span + VDIM]
    gains = small[:, span + VDIM : span + VDIM + vector_cols].reshape(-1).astype(f32)
    bounds = [0, D, 2 * D, 3 * D, 4 * D, 5 * D, 6 * D, 7 * D, 7 * D + FF, 8 * D + FF, 9 * D + FF]
    bounds = bounds + [10 * D + FF]
    pieces = [gains[None, bounds[index] : bounds[index + 1]] for index in range(11)]
    qkv_bias = jnp.concatenate([pieces[2], jnp.zeros_like(pieces[2]), pieces[3]], axis=1)

    slots = round_up(SLOT_CAPS.get(shard_rows, tokens), 8)
    ids = jnp.concatenate([query_ids[:, 0], passage_ids[:, 0]], axis=1).reshape(tokens)
    owner = ids // shard_rows
    local_id = ids - owner * shard_rows
    is_owner = owner[:, None] == jnp.arange(devices, dtype=jnp.int32)[None]
    before = jnp.arange(tokens)[:, None] > jnp.arange(tokens)[None]
    earlier = dot_nn(before.astype(bf16), is_owner.astype(bf16))
    rank = jnp.sum(jnp.where(is_owner, earlier, 0.0), axis=1).astype(jnp.int32)
    place = owner * slots + rank
    picks = (place[:, None] == jnp.arange(devices * slots, dtype=jnp.int32)[None]).astype(bf16)
    picks_t = (jnp.arange(devices * slots, dtype=jnp.int32)[:, None] == place[None]).astype(bf16)
    picks = lax.optimization_barrier(picks)
    digits = jnp.stack([local_id // 32, local_id % 32], axis=1).astype(bf16)
    asked = dot_tn(digits, picks)
    asked = (asked[0] * 32.0 + asked[1]).astype(jnp.int32).reshape(devices, slots)
    wanted = lax.all_to_all(asked, both, 0, 0, tiled=True).reshape(devices * slots)
    chosen = (wanted[:, None] == jnp.arange(shard_rows, dtype=jnp.int32)[None]).astype(bf16)
    chosen_t = (jnp.arange(shard_rows, dtype=jnp.int32)[:, None] == wanted[None]).astype(bf16)
    chosen = lax.optimization_barrier(chosen)
    sent_rows = low(dot_nn(chosen, low(table))).reshape(devices, slots, D)
    got_rows = lax.all_to_all(sent_rows, both, 0, 0, tiled=True).reshape(devices * slots, D)
    token_rows = dot_nn(picks, got_rows)

    per = blocks // MATRICES
    turn_of = myself // per
    wide_rows = FF // devices

    def padded(rows):
        spare = wide_rows - rows.shape[-2]
        return jnp.pad(rows, ((0, 0),) * (rows.ndim - 2) + ((0, spare), (0, 0)))

    old = [padded(member.T.reshape(blocks, -1, D)) for member in (m_qkv, m_attn, m_in, m_out)]
    old = lax.dynamic_index_in_dim(jnp.stack(old), turn_of, 0, keepdims=False).reshape(-1, D)
    token_rows, old, picks_t, chosen_t = tie(token_rows, old, picks_t, chosen_t)

    lens = passage_len[:, 0]
    pos_rows = jnp.concatenate([pos[:query_len], pos] * micro_count, axis=0)
    x, x_hat, x_scale = norm_forward(token_rows + pos_rows, pieces[0], pieces[1])
    x_low = low(x)
    qkv = low(dot_nt(x_low, qkv_t) + qkv_bias)
    context, norms = attention_forward(lens, qkv, query_len, span)
    heads = round_up(HEADS, 8)
    norms = norms.reshape(micro_count, length, 128)[:, :, :heads].transpose(0, 2, 1)
    norms = jnp.concatenate([norms[:, :, query_len:], norms[:, :, :query_len]], axis=2)
    h, h_hat, h_scale = norm_forward(
        x + dot_nt(context, attn_t) + pieces[4], pieces[5], pieces[6]
    )
    h_low = low(h)
    wide = lax.optimization_barrier(dot_nt(h_low, in_t) + pieces[7])
    gelu_value, gelu_slope = gelu_parts(wide)
    f_low, gelu_slope = tie(low(gelu_value), gelu_slope)
    o, o_hat, o_scale = norm_forward(h + dot_nn(f_low, out_t) + pieces[8], pieces[9], pieces[10])
    o_low = low(o)
    e = dot_nn(o_low, proj_t)
    e_scale = lax.rsqrt(jnp.sum(e * e, axis=-1, keepdims=True) + 1e-06)
    vecs = low(e * e_scale)

    labels = domains[:, 0]
    targets = positives[:, 0]
    spots = jnp.arange(blocks, dtype=jnp.int32)
    chosen_label = jnp.sum(
        jnp.where(targets[:, :, None] == spots[None, None], labels[:, None, :], 0), axis=-1
    )

    def spread(mask):
        mask = mask.astype(f32).transpose(1, 0, 2).reshape(blocks, micro_count * blocks, 1)
        return jnp.broadcast_to(mask, (blocks, micro_count * blocks, 128))

    allowed = spread(labels[:, :, None] == chosen_label[:, None, :])
    hits = spread(targets[:, None, :] == spots[None, :, None])
    vecs, allowed, hits = tie(vecs, allowed, hits)
    by_micro = vecs.reshape(micro_count, length, VDIM)
    cycle = by_micro[:, :query_len].reshape(micro_count * query_len, VDIM)
    cycle = share_all(cycle, "blk", blocks).reshape(blocks, micro_count * query_len, VDIM)
    share, scores = score_forward(lens, cycle, vecs, query_len, span)
    every = share_all(scores.reshape(micro_count * blocks, 128), "blk", blocks)
    every = every.reshape(blocks, micro_count * blocks, 128)
    loss_part, d_passage, d_cycle = score_backward(
        myself, every, allowed, hits, share, cycle, vecs, query_len, span
    )
    loss_part = loss_part[0, 0]
    d_query = jnp.sum(lax.all_to_all(d_cycle, "blk", 0, 0, tiled=True), axis=0)
    d_query = d_query.reshape(micro_count, query_len, VDIM)
    d_vecs = jnp.concatenate([d_query, d_passage], axis=1).reshape(tokens, VDIM)

    def reduction(pieces, wire):
        return Reduction(pieces[1::2], pieces[0::2], narrow, blocks, wire)

    def column_sum(values):
        return jnp.sum(values, axis=0)

    d_vecs = low(d_vecs).astype(f32)
    inner = jnp.sum(e * d_vecs, axis=-1, keepdims=True)
    d_e = low(e_scale * d_vecs - e * (e_scale * e_scale * e_scale * inner))
    g_proj = dot_tn(o_low, d_e)
    d_o = low(dot_nt(d_e, proj_t)).astype(f32)
    g_gain_o, g_shift_o = column_sum(d_o * o_hat), column_sum(d_o)
    d_sum_o = norm_backward(d_o, o_hat, o_scale, pieces[9])
    g_bias_out = column_sum(d_sum_o)
    d_y = low(d_sum_o)
    place = lax.axis_index("narrow")
    low_bit = place & 1
    g_out = dot_tn(f_low, d_y).reshape(narrow // 2, 2, -1, D)
    out_sent = lax.dynamic_index_in_dim(g_out, 1 - low_bit, 1, keepdims=False)
    d_y, out_sent, g_out = tie(d_y, out_sent, g_out)
    out_got = swap(out_sent, "narrow", narrow, 1)
    d_f = low(dot_nt(d_y, out_t)).astype(f32)
    d_wide = d_f * gelu_slope
    g_bias_in = column_sum(d_wide)
    d_wide = low(d_wide)
    d_wide, out_got = tie(d_wide, out_got)
    g_out = lax.dynamic_index_in_dim(g_out, low_bit, 1, keepdims=False) + out_got
    g_out = low(g_out.reshape(-1, D))
    d_wide, g_out = tie(d_wide, g_out)
    if narrow > 2:
        groups = [list(range(bit, narrow, 2)) for bit in range(2)]
        g_out = lax.psum_scatter(
            g_out, "narrow", scatter_dimension=0, axis_index_groups=groups, tiled=True
        )
    sum_in = reduction(relative(dot_tn(d_wide, h_low), narrow), bf16)
    d_wide, sum_in.sent = tie(d_wide, sum_in.sent)
    sum_in.across_core()
    d_wide, sum_in.kept = tie(d_wide, sum_in.kept)
    sum_in.prepare()
    d_wide, sum_in.outgoing, sum_in.kept = tie(d_wide, sum_in.outgoing, sum_in.kept)
    sum_in.send()
    d_h = d_sum_o + low(dot_nn(d_wide, in_t)).astype(f32)
    g_gain_h, g_shift_h = column_sum(d_h * h_hat), column_sum(d_h)
    d_sum_h = norm_backward(d_h, h_hat, h_scale, pieces[5])
    g_bias_attn = column_sum(d_sum_h)
    d_a = low(d_sum_h)
    sum_attn = reduction(relative(dot_tn(d_a, context), narrow), bf16)
    d_a, sum_attn.sent, g_out = tie(d_a, sum_attn.sent, g_out)
    g_out = lax.psum_scatter(g_out.astype(f32), "blk", scatter_dimension=0, tiled=True)
    sum_attn.across_core()
    d_context = low(dot_nn(d_a, attn_t))
    d_context, sum_attn.got = tie(d_context, sum_attn.got)
    sum_attn.across_narrow()
    head_of = jnp.arange(D)[None] // HDIM == jnp.arange(heads)[:, None]
    inner = lax.dot_general(
        head_of.astype(f32),
        d_context.astype(f32) * context.astype(f32),
        (((1,), (1,)), ((), ())),
        precision=lax.Precision.HIGH,
        preferred_element_type=f32,
    )
    inner = inner.reshape(heads, micro_count, length).transpose(1, 0, 2)
    inner = jnp.concatenate([inner[:, :, query_len:], inner[:, :, :query_len]], axis=2)
    d_qkv = attention_backward(lens, qkv, d_context, norms, inner, query_len, span)
    d_qkv, sum_in.got, sum_attn.got = tie(d_qkv, sum_in.got, sum_attn.got)
    g_in = sum_in.total()
    d_qkv, g_in = tie(d_qkv, g_in)
    g_in = lax.psum_scatter(g_in, "blk", scatter_dimension=0, tiled=True)
    d_x = d_sum_h + low(dot_nn(d_qkv, qkv_t)).astype(f32)
    d_rows = norm_backward(d_x, x_hat, x_scale, pieces[0])

    back_rows = low(dot_nn(picks_t, low(d_rows))).reshape(devices, slots, D)
    back_rows, d_rows, d_x, d_qkv, g_proj = tie(back_rows, d_rows, d_x, d_qkv, g_proj)
    back_rows = lax.all_to_all(back_rows, both, 0, 0, tiled=True).reshape(devices * slots, D)
    sum_qkv = reduction(relative(dot_tn(d_qkv, x_low), narrow), bf16)
    d_qkv, d_rows, d_x, sum_qkv.sent = tie(d_qkv, d_rows, d_x, sum_qkv.sent)
    sum_qkv.across_core()
    sum_qkv.across_narrow()
    early = (g_bias_attn, g_gain_h, g_shift_h, g_bias_in, g_bias_out, g_gain_o, g_shift_o)
    tail = late_sums(d_rows, d_x, x_hat, d_qkv, g_proj, early, query_len, span, micro_count)
    sum_tail = reduction(relative(tail, narrow), f32)
    sum_tail.across_core()
    sum_tail.across_narrow()
    tail = sum_tail.total()
    spare_high = lax.optimization_barrier(low(tail[:, span:]))
    tail = [low(tail[:, :span]), spare_high, low(tail[:, span:] - spare_high.astype(f32))]
    tail = jnp.concatenate(tail, axis=1).reshape(blocks, -1)
    tail_size = tail.shape[1]
    tail = jnp.pad(tail, ((0, 0), (0, round_up(tail_size, 16 * D) - tail_size)))
    merged = [low(member.total()).reshape(blocks, -1, D) for member in (sum_qkv, sum_attn)]
    merged = jnp.concatenate(merged + [tail.reshape(blocks, -1, D)], axis=1)
    merged, back_rows = tie(merged, back_rows)
    merged = lax.all_to_all(merged, "blk", 0, 0, tiled=True)
    table_grad = dot_nn(chosen_t, back_rows)
    table_square = jnp.sum(table_grad * table_grad)
    merged = jnp.sum(merged.astype(f32), axis=0)
    attn_rows = D // devices
    qkv_rows = 3 * attn_rows
    g_qkv, g_attn = merged[:qkv_rows], merged[qkv_rows : qkv_rows + attn_rows]
    g_tail = merged[qkv_rows + attn_rows :].reshape(-1)[:tail_size].reshape(attn_rows, -1)
    spare = g_tail[:, span : span + 128 + VDIM] + g_tail[:, span + 128 + VDIM :]
    g_tail = jnp.concatenate([g_tail[:, :span], spare], axis=1)
    g_qkv, g_attn, g_out, g_in, g_tail, table_square = tie(
        g_qkv, g_attn, g_out, g_in, g_tail, table_square
    )

    sends = [padded(low(member)) for member in (g_qkv, g_attn, g_in, g_out)]
    sends = jnp.repeat(jnp.stack(sends), per, axis=0)
    taken = lax.all_to_all(sends, "blk", 0, 0, tiled=True)

    def square_sum(values):
        values = values.astype(f32)
        return jnp.sum(values * values)

    local_square = (
        table_square
        + square_sum(g_out)
        + square_sum(g_in)
        + square_sum(g_qkv)
        + square_sum(g_attn)
        + square_sum(g_tail)
    )
    lane = lax.broadcasted_iota(jnp.int32, (8, 128), 1)
    pair = jnp.where(lane == 0, local_square, jnp.where(lane == 1, loss_part, 0.0))
    sums = sum_everywhere(pair, (("narrow", narrow), ("blk", blocks)))
    loss = sums[0, 1]
    grad_norm = jnp.sqrt(sums[0, 0])
    factor = jnp.minimum(1.0, clip_limit / (grad_norm + 1e-06))

    packed = [low(member) for member in (g_qkv, g_attn, g_in, g_out, g_tail)]
    complete = lax.all_gather(jnp.concatenate(packed, axis=0), "blk", axis=0, tiled=False)
    moment, gram = packed_gram(factor, old, taken.reshape(-1, D))
    gram = sum_group(gram, narrow, 1, blocks)
    half = moment.shape[0] // per
    moment = lax.dynamic_slice_in_dim(moment, myself % per * half, half, axis=0)
    ortho = newton_chain(gram, moment, bf16)
    ortho, complete = tie(ortho, complete)
    ortho = lax.all_gather(ortho, "blk", axis=0, tiled=False)
    ortho = ortho.reshape(MATRICES, blocks, wide_rows, D)
    matrix_rows = (qkv_rows, attn_rows, wide_rows, wide_rows)

    def turned(rows):
        return rows.reshape(-1, D).T.astype(f32)

    grads, first = [], 0
    for rows in matrix_rows:
        grads.append(turned(complete[:, first : first + rows]))
        first += rows
    tail_all = complete[:, first:].reshape(side, -1)
    grad_pos = tail_all[:, :span].T.astype(f32)
    grad_proj = tail_all[:, span + 128 :].T.astype(f32)
    grad_vector = tail_all[:, span : span + 128].T
    grad_bias = grad_vector[4:5].astype(f32)
    place = lax.axis_index("narrow")
    whole_vector = jnp.zeros((narrow,) + grad_vector.shape, bf16)
    for offset, piece in enumerate(gather_relative(grad_vector, narrow)):
        whole_vector = lax.dynamic_update_index_in_dim(whole_vector, piece, place ^ offset, 0)
    whole_vector = whole_vector.transpose(1, 0, 2)[:vector_cols].reshape(1, -1).astype(f32)
    grad_vector = lax.dynamic_slice_in_dim(
        whole_vector, place * vector.shape[1], vector.shape[1], axis=1
    )
    proj_rows, gram_proj = packed_gram(factor, m_proj.T, grad_proj.T)
    ortho_proj = newton_chain(sum_group(gram_proj, narrow, 1, blocks), proj_rows, f32)
    table_new, table_m_new, table_v_new = adam_step(
        table, table_m, table_v, factor * table_grad, adam_rate
    )
    pos_new, pos_m_new, pos_v_new = adam_step(
        pos_table, pos_m, pos_v, factor * grad_pos, adam_rate
    )
    vector_new, vector_m_new, vector_v_new = adam_step(
        vector, vector_m, vector_v, factor * grad_vector, vector_rate
    )
    olds = (m_qkv, m_attn, m_in, m_out, m_proj)
    grads = grads + [grad_proj]
    moments = [muon_moment * before + factor * grad for before, grad in zip(olds, grads)]
    masters = (w_qkv, w_attn, w_proj)
    orthos = (turned(ortho[0, :, :qkv_rows]), turned(ortho[1, :, :attn_rows]), ortho_proj.T)
    updated = []
    for weight, ortho_part, rate in zip(masters, orthos, (muon_rate, attn_rate, muon_rate)):
        long_side = max(weight.shape[0], weight.shape[1] * narrow)
        updated.append(weight - rate * (0.2 * long_side**0.5 * ortho_part + weight_decay * weight))
    wide_orthos = [ortho[index].reshape(-1, D) for index in (2, 3)]
    in_new, out_new = update_wide((w_in, w_out), wide_orthos, muon_rate, 0.2 * FF**0.5)
    updated = [updated[0], updated[1], in_new, out_new, updated[2]]
    return (
        loss,
        grad_norm,
        table_new,
        table_m_new,
        table_v_new,
        pos_new,
        pos_m_new,
        pos_v_new,
        vector_new,
        vector_m_new,
        vector_v_new,
        updated[0],
        moments[0],
        updated[1],
        moments[1],
        updated[2],
        moments[2],
        updated[3],
        moments[3],
        updated[4],
        moments[4],
        factor * grad_bias,
    )


def solution(mesh):
    ids = P(None, ("blk", "narrow"), None)
    rows = P(("blk", "narrow"), None)
    cols = P(None, "narrow")
    group = P(None, "narrow", None)
    in_specs = (ids, ids, P(None, ("blk", "narrow")), group, group) + (rows,) * 3 + (cols,) * 16
    out_specs = (P(), P()) + (rows,) * 3 + (cols,) * 17
    return jax.shard_map(body, mesh=mesh, in_specs=in_specs, out_specs=out_specs, check_vma=False)
```

time: 852 us -> 716 us (0.84)
  waiting for transfers between devices: 267 us -> 207 us
  local copies, waits for them, and re-layouts: 103 us -> 55.3 us
  other arithmetic: 135 us -> 109 us
  blocking collectives: 14.3 us -> 36.5 us
  matrix products: 136 us -> 122 us
  starting transfers between devices: 58.2 us -> 49.6 us
    ppermute x18 -> x32, waiting for transfers between devices: 108 us -> 71.4 us  [swap(): lax.ppermute(value, axis, [(place, place ^ bit) for place in range(size)])]
    all_to_all x8 -> x1, starting transfers between devices: 34.7 us -> 3.59 us  [body(): merged = lax.all_to_all(merged, 'blk', 0, 0, tiled=True)]
    ppermute x18 -> x32, starting transfers between devices: 6.73 us -> 29.5 us  [swap(): lax.ppermute(value, axis, [(place, place ^ bit) for place in range(size)])]
    all_to_all x0 -> x2, blocking collectives: none -> 22.3 us  [share_all(): return lax.all_to_all(spread, axes, 0, 0, tiled=True)]
    unnamed x248 -> x150, local copies, waits for them, and re-layouts: 54.2 us -> 33 us
    all_to_all x1, waiting for transfers between devices: 20.7 us -> 0.01 us  [body(): taken = lax.all_to_all(sends, 'blk', 0, 0, tiled=True)]
    all_gather x5 -> x4, waiting for transfers between devices: 30.5 us -> 10.3 us  [gather(): return lax.all_gather(shard, 'narrow', axis=0, tiled=True)]
    all_gather x1, waiting for transfers between devices: 23.5 us -> 43 us  [body(): ortho = lax.all_gather(ortho, 'blk', axis=0, tiled=False)]
  transfers between devices with their start and end apart: 37 -> 46, of which waited for: 17 -> 21; matrix products, arithmetic and copies ran while one was open for 27% -> 28% of each run, Pallas kernels for 9% -> 14%
where the time goes in v2:
time: 716 us; the launch traced here: 710 us
  waiting for transfers between devices  207 us (29%)
  matrix products  122 us (17%)
  Pallas kernels  110 us (15%)
  other arithmetic  109 us (15%)
  local copies, waits for them, and re-layouts  55.3 us (8%)
  starting transfers between devices  49.6 us (7%)
  blocking collectives  36.5 us (5%)
  between operations  21.9 us (3%)
    ppermute x32, waiting for transfers between devices, swap(): lax.ppermute(value, axis, [(place, place ^ bit) for place in range(size)])  71.4 us
    dot_general x10, matrix products, dot_nn(): lax.dot_general(left, right, (((1,), (0,)), ((), ())), preferred_element_...  53.7 us
    all_gather x1, waiting for transfers between devices, body(): ortho = lax.all_gather(ortho, 'blk', axis=0, tiled=False)  43 us
    pallas_call x2, Pallas kernels, newton_chain(): pl.pallas_call(chain_kernel, out_shape=jax.ShapeDtypeStruct(rows.shape, d...  41 us
    all_to_all x1, waiting for transfers between devices, body(): merged = lax.all_to_all(merged, 'blk', 0, 0, tiled=True)  40.3 us
    dot_general x5, matrix products, dot_nt(): lax.dot_general(left, right, (((1,), (1,)), ((), ())), preferred_element_...  37.5 us
    unnamed x150, local copies, waits for them, and re-layouts  33 us
    ppermute x32, starting transfers between devices, swap(): lax.ppermute(value, axis, [(place, place ^ bit) for place in range(size)])  29.5 us
  transfers between devices with their start and end apart: 46, of which 21 were waited for; matrix products, arithmetic and copies ran while one was open for 28% of the time, Pallas kernels for 14%

profile of v2, /device:TPU:0, one launch (start us, length us, event | category | flops | bytes accessed | tf_op | source)
XLA Modules:
  0.0 710.1 jit_solution(8983205926996166347)
XLA Ops:
  19.8 14.3 %all_to_all.41 = s32[32,1,40]{2,1,0:T(1,128)S(1)} all-to-all(s32[32,1,40]{2,1,0:T(1,128)S(1)} %bitcast.228), channel_id=1, replica_groups=mesh['blk'=8,'narrow'=4] {'blk','narrow'}, dimensions={0} | all-to-all | bytes 10240 | tf_op jit(solution)/shard_map/all_to_all | solution.py:820
  63.2 25.7 %all-to-all-done.1 = bf16[32,40,768]{2,1,0:T(8,128)(2,1)} async-done(((bf16[32,40,768]{2,1,0:T(8,128)(2,1)}), bf16[32,40,768]{2,1,0:T(8,128)(2,1)}, u32[]{:S(2)}, u32[]{:S(2)}) %all-to-all-start.1) | async-done | bytes 1966112 | tf_op jit(solution)/shard_map/all_to_all | solution.py:825
  88.9 4.7 fusion.92
  98.4 9.0 %fusion.4.qkv_ref = bf16[1088,2304]{1,0:T(8,128)(2,1)} fusion(bf16[2304,768]{1,0:T(8,128)(2,1)} %all-gather.11.cloned.1.call-done, f32[2304]{0:T(1024)S(1)} %fusion.60, f32[1088,768]{1,0:T(8,128)S(1)} %subtract_multiply_fusion.4.hat_ref, f32[768]{0:T(1024)S(1)} %get-tuple-element.315, f32[768]{0:T(1024)S(1)} %get-tuple-element.316), kind=kOutput, calls=%fused_computation.10 | convolution fusion | flops 3857891328 | bytes 11910144 | tf_op jit(solution)/shard_map/dot_general | solution.py:49
  107.4 23.6 %shard_map.399 = (bf16[1088,768]{1,0:T(8,128)(2,1)S(1)}, f32[1088,128]{1,0:T(8,128)S(1)}) custom-call(s32[2]{0:T(128)S(1)} %bitcast.193, bf16[1088,2304]{1,0:T(8,128)(2,1)} %fusion.4.qkv_ref), custom_call_target="tpu_custom_call" | custom-call | flops 3221225472 | bytes 6684672 | tf_op jit(solution)/shard_map/pallas_call | solution.py:128
  137.3 9.4 %convolution_add_fusion.1 = f32[1088,3072]{1,0:T(8,128)S(1)} fusion(bf16[3072,768]{0,1:T(8,128)(2,1)} %all-gather.13.cloned.1.call-done, f32[3072]{0:T(1024)S(1)} %slice.219, f32[1088,768]{1,0:T(8,128)} %get-tuple-element.322, f32[768]{0:T(1024)S(1)} %get-tuple-element.310, f32[768]{0:T(1024)S(1)} %get-tuple-element.311, f32[1088]{0:T(1024)S(1)} %add_rsqrt_fusion.2, ...), kind=kOutput, calls=%fused_computation.2 | convolution fusion | flops 5141348352 | bytes 21457408 | tf_op jit(solution)/shard_map/dot_general | solution.py:49
  146.7 9.5 %fusion.3 = (f32[1088,3072]{1,0:T(8,128)}, bf16[1088,3072]{1,0:T(8,128)(2,1)}) fusion(f32[1088,3072]{1,0:T(8,128)S(1)} %convolution_add_fusion.1), kind=kLoop, calls=%fused_computation.6 | loop fusion | flops 33423360 | bytes 33423360 | tf_op jit(solution)/shard_map/add | solution.py:78
  156.2 10.2 %all-gather.15.cloned.1.call-done = bf16[3072,768]{0,1:T(8,128)(2,1)} async-done(((bf16[768,768]{0,1:T(8,128)(2,1)}), bf16[3072,768]{0,1:T(8,128)(2,1)}) %all-gather.15.cloned.1.call-update) | async-done | bytes 4718608 | tf_op jit(solution)/shard_map/all_gather | solution.py:790
  166.4 11.1 %fusion.91 = (f32[1088]{0:T(1024)S(1)}, f32[1088,768]{1,0:T(8,128)S(1)}) fusion(f32[768]{0:T(1024)S(1)} %get-tuple-element.309, bf16[1088,3072]{1,0:T(8,128)(2,1)} %get-tuple-element.95, bf16[3072,768]{0,1:T(8,128)(2,1)} %all-gather.15.cloned.1.call-done, f32[768]{0:T(1024)S(1)} %get-tuple-element.310, f32[768]{0:T(1024)S(1)} %get-tuple-element.311, ...), kind=kOutput, calls=%fused_computation.277 | convolution fusion | flops 5139676160 | bytes 18110208 | tf_op jit(solution)/shard_map/dot_general | solution.py:45
  181.5 12.7 %all_to_all.42.cycle_ref = bf16[8,64,128]{2,1,0:T(8,128)(2,1)S(1)} all-to-all(bf16[8,64,128]{2,1,0:T(8,128)(2,1)S(1)} %broadcast_in_dim.131), channel_id=1, replica_groups=mesh['blk'=8,'narrow'=4] {'blk'}, dimensions={0} | all-to-all | bytes 262144 | tf_op jit(solution)/shard_map/all_to_all | solution.py:459
  195.6 9.6 %all_to_all.43.every_ref = f32[8,16,128]{2,1,0:T(8,128)S(1)} all-to-all(f32[8,16,128]{2,1,0:T(8,128)S(1)} %broadcast_in_dim.133), channel_id=1, replica_groups=mesh['blk'=8,'narrow'=4] {'blk'}, dimensions={0} | all-to-all | bytes 131072 | tf_op jit(solution)/shard_map/all_to_all | solution.py:459
  211.4 7.4 %all-to-all-done.4 = f32[8,64,128]{2,1,0:T(8,128)} async-done(((f32[8,64,128]{2,1,0:T(8,128)}), f32[8,64,128]{2,1,0:T(8,128)}, u32[]{:S(2)}, u32[]{:S(2)}) %all-to-all-start.4) | async-done | bytes 262176 | tf_op jit(solution)/shard_map/all_to_all | solution.py:886
  228.3 6.4 fusion.93
  239.9 12.0 %fusion.86 = (f32[3072]{0:T(1024)S(1)}, bf16[1088,3072]{1,0:T(8,128)(2,1)}) fusion(f32[1088,3072]{1,0:T(8,128)} %get-tuple-element.104, bf16[1088,768]{1,0:T(8,128)(2,1)} %copy-done.47, bf16[3072,768]{0,1:T(8,128)(2,1)} %all-gather.15.cloned.1.call-done), kind=kOutput, calls=%fused_computation.272 | convolution fusion | flops 5150536704 | bytes 26456064 | tf_op jit(solution)/shard_map/dot_general | solution.py:49
  256.3 10.4 %fusion.76 = f32[3072,768]{1,0:T(8,128)S(1)} fusion(bf16[1088,3072]{1,0:T(8,128)(2,1)} %get-tuple-element.116, f32[1088,768]{1,0:T(8,128)} %get-tuple-element.322, f32[768]{0:T(1024)S(1)} %get-tuple-element.310, f32[768]{0:T(1024)S(1)} %get-tuple-element.311, f32[1088]{0:T(1024)S(1)} %add_rsqrt_fusion.2, f32[1088]{0:T(1024)S(1)} %broadcast_multiply_fusion.7), kind=kOutput, calls=%fused_computation.269 | convolution fusion | flops 5138006016 | bytes 19479040 | tf_op jit(solution)/shard_map/dot_general | solution.py:53
  282.9 10.0 %multiply_reduce_fusion = (f32[768]{0:T(1024)S(1)}, f32[1088]{0:T(1024)S(1)}, f32[1088]{0:T(1024)S(1)}, f32[768]{0:T(1024)S(1)}, f32[1088,768]{1,0:T(8,128)S(1)}) fusion(f32[1088,768]{1,0:T(8,128)} %get-tuple-element.322, f32[1088]{0:T(1024)S(1)} %add_rsqrt_fusion.2, f32[1088]{0:T(1024)S(1)} %broadcast_multiply_fusion.7, f32[768]{0:T(1024)S(1)} %get-tuple-element.311, ...), kind=kOutput, calls=%fused_computation.55 | convolution fusion | flops 5143851008 | bytes 21456896 | tf_op jit(solution)/shard_map/dot_general | solution.py:45
  316.2 29.1 %shard_map.402.qkv_ref = bf16[1088,2304]{1,0:T(8,128)(2,1)} custom-call(s32[2]{0:T(128)S(1)} %bitcast.195, bf16[1088,2304]{1,0:T(8,128)(2,1)} %fusion.4.qkv_ref, bf16[1088,768]{1,0:T(8,128)(2,1)S(1)} %convolution_convert_fusion.5.grad_ref, f32[2,16,544]{2,1,0:T(8,128)S(1)} %pad_maximum_fusion.5.norm_ref, f32[2,16,544]{2,1,0:T(8,128)S(1)} %pad_maximum_fusion.6.inner_ref), custom_call_target="tpu_custom_call" | custom-call | flops 8053063680 | bytes 11698176 | tf_op jit(solution)/shard_map/pallas_call | solution.py:245
  348.4 9.3 %multiply_reduce_fusion.7 = (f32[1088]{0:T(1024)S(1)}, f32[1088]{0:T(1024)S(1)}, f32[1088,768]{1,0:T(8,128)S(1)}) fusion(f32[768]{0:T(1024)S(1)} %get-tuple-element.316, f32[1088,768]{1,0:T(8,128)S(1)} %copy-done.15, f32[1088,768]{1,0:T(8,128)} %copy-done.26, bf16[1088,2304]{1,0:T(8,128)(2,1)} %shard_map.402.qkv_ref, ...), kind=kOutput, calls=%fused_computation.80 | convolution fusion | flops 3856218112 | bytes 18591232 | tf_op jit(solution)/shard_map/dot_general | solution.py:45
  364.8 4.7 all-to-all-start.5
  369.6 7.8 %fusion.46 = f32[2304,768]{1,0:T(8,128)S(1)} fusion(bf16[1088,2304]{1,0:T(8,128)(2,1)} %shard_map.402.qkv_ref, f32[1088,768]{1,0:T(8,128)} %copy-done.13, f32[768]{0:T(1024)S(1)} %copy-done.63, f32[768]{0:T(1024)S(1)} %get-tuple-element.316), kind=kOutput, calls=%fused_computation.133 | convolution fusion | flops 3852877824 | bytes 15439872 | tf_op jit(solution)/shard_map/dot_general | solution.py:53
  381.5 5.6 shard_map.403
  397.6 15.5 %collective-permute-done.12 = f32[192,768]{1,0:T(8,128)} collective-permute-done((f32[192,768]{1,0:T(8,128)}, f32[192,768]{1,0:T(8,128)}, u32[]{:S(2)}, u32[]{:S(2)}) %collective-permute-start.12) | collective-permute-done | bytes 589856 | tf_op jit(solution)/shard_map/ppermute | solution.py:463
  414.9 19.6 %collective-permute-done.9 = bf16[576,768]{1,0:T(8,128)(2,1)} collective-permute-done((bf16[576,768]{1,0:T(8,128)(2,1)}, bf16[576,768]{1,0:T(8,128)(2,1)}, u32[]{:S(2)}, u32[]{:S(2)}) %collective-permute-start.9) | collective-permute-done | bytes 884768 | tf_op jit(solution)/shard_map/ppermute | solution.py:463
  442.2 6.6 multiply_reduce_fusion.6
  448.8 40.3 %all-to-all-done.6 = bf16[8,128,768]{2,1,0:T(8,128)(2,1)S(1)} async-done(((bf16[8,128,768]{2,1,0:T(8,128)(2,1)}), bf16[8,128,768]{2,1,0:T(8,128)(2,1)S(1)}, u32[]{:S(2)}, u32[]{:S(2)}) %all-to-all-start.6) | async-done | bytes 1572896 | tf_op jit(solution)/shard_map/all_to_all | solution.py:982
  510.6 4.7 collective-permute-start.22
  523.6 6.2 collective-permute-start.17
  544.2 18.1 %collective-permute-done.24 = f32[256,768]{1,0:T(8,128)S(1)} collective-permute-done((f32[256,768]{1,0:T(8,128)S(1)}, f32[256,768]{1,0:T(8,128)S(1)}, u32[]{:S(2)}, u32[]{:S(2)}) %collective-permute-start.24) | collective-permute-done | bytes 786464 | tf_op jit(solution)/shard_map/ppermute | solution.py:463
  567.3 36.8 %shard_map.405 = bf16[384,768]{1,0:T(8,128)(2,1)} custom-call(f32[512,768]{1,0:T(8,128)} %pad_maximum_fusion.1.gram_in, f32[384,768]{1,0:T(8,128)} %constant_dynamic-slice_fusion.rows_in), custom_call_target="tpu_custom_call" | custom-call | flops 42127589376 | bytes 3145728 | tf_op jit(solution)/shard_map/pallas_call | solution.py:720
  604.2 4.9 all-gather.17.cloned.1.call-done
  609.2 7.2 %multiply_subtract_fusion = (f32[960,768]{1,0:T(8,128)}, f32[960,768]{1,0:T(8,128)}, f32[960,768]{1,0:T(8,128)}) fusion(f32[960,768]{1,0:T(8,128)S(1)} %copy-done.40, f32[960,768]{1,0:T(8,128)} %get-tuple-element.332, f32[]{:T(128)} %min.3, f32[960,768]{1,0:T(8,128)} %param.30, f32[960,768]{1,0:T(8,128)} %param.31), kind=kLoop, calls=%fused_computation.75 | loop fusion | flops 11796480 | bytes 20643844 | tf_op jit(solution)/shard_map/sub | solution.py:606
  647.4 43.0 %all-gather.19.cloned.1.call-done = bf16[3072,768]{1,0:T(8,128)(2,1)} async-done(((bf16[384,768]{1,0:T(8,128)(2,1)}), bf16[3072,768]{1,0:T(8,128)(2,1)}) %all-gather.19.cloned.1.call-update) | async-done | bytes 4718608 | tf_op jit(solution)/shard_map/all_gather | solution.py:1027
  (450 shorter events, 242.7 us)
Async XLA Ops:
  7.2 54.2 %all-gather.9.cloned.1.call-start = ((), (), s32[]{:S(2)}) async-start(), calls=%async_computation.11 | async-start | bytes 2949120 | tf_op jit(solution)/shard_map/all_gather | solution.py:790
  12.3 86.0 %all-gather.11.cloned.1.call-start = ((), (), s32[]{:S(2)}) async-start(), calls=%async_computation.12 | async-start | bytes 4423680 | tf_op jit(solution)/shard_map/all_gather | solution.py:790
  14.9 122.4 %all-gather.13.cloned.1.call-start = ((), (), s32[]{:S(2)}) async-start(), calls=%async_computation.13 | async-start | bytes 5898240 | tf_op jit(solution)/shard_map/all_gather | solution.py:790
  39.4 49.5 %all-to-all-start.1 = ((bf16[32,40,768]{2,1,0:T(8,128)(2,1)}), bf16[32,40,768]{2,1,0:T(8,128)(2,1)}, u32[]{:S(2)}, u32[]{:S(2)}) async-start(bf16[32,40,768]{2,1,0:T(8,128)(2,1)} %bitcast.215), calls=%async_computation.1 | async-start | bytes 3932160 | tf_op jit(solution)/shard_map/all_to_all | solution.py:825
  43.0 123.4 %all-gather.15.cloned.1.call-start = ((), (), s32[]{:S(2)}) async-start(), calls=%async_computation.14 | async-start | bytes 5898240 | tf_op jit(solution)/shard_map/all_gather | solution.py:790
  206.5 12.3 %all-to-all-start.4 = ((f32[8,64,128]{2,1,0:T(8,128)}), f32[8,64,128]{2,1,0:T(8,128)}, u32[]{:S(2)}, u32[]{:S(2)}) async-start(f32[8,64,128]{2,1,0:T(8,128)} %get-tuple-element.101), calls=%async_computation.4 | async-start | bytes 524288 | tf_op jit(solution)/shard_map/all_to_all | solution.py:886
  210.6 93.1 %reduce-scatter.4.cloned.1.call-start = ((), (), s32[]{:S(2)}) async-start(), calls=%async_computation.15 | async-start | bytes 3538944 | tf_op jit(solution)/shard_map/reduce_scatter | solution.py:921
  239.8 12.0 %collective-permute-start = (f32[2,768,768]{2,1,0:T(8,128)}, f32[2,768,768]{2,1,0:T(8,128)}, u32[]{:S(2)}, u32[]{:S(2)}) collective-permute-start(f32[2,768,768]{2,1,0:T(8,128)} %dynamic-slice_bitcast_fusion), channel_id=1, source_target_pairs={{0,1},{1,0},{2,3},{3,2},{4,5},{5,4},{6,7},{7,6},{8,9},{9,8},{10,11... | collective-permute-start | bytes 14155784 | tf_op jit(solution)/shard_map/ppermute | solution.py:463
  271.1 8.7 %collective-permute-start.1 = (f32[768,768]{1,0:T(8,128)}, f32[768,768]{1,0:T(8,128)}, u32[]{:S(2)}, u32[]{:S(2)}) collective-permute-start(f32[768,768]{1,0:T(8,128)} %get-tuple-element.113), channel_id=1, source_target_pairs={{0,1},{1,0},{2,3},{3,2},{4,5},{5,4},{6,7},{7,6},{8,9},{9,8},{10,11... | collective-permute-start | bytes 7077896 | tf_op jit(solution)/shard_map/ppermute | solution.py:463
  271.1 218.4 %reduce-scatter.6.cloned.1.call-start = ((), (), s32[]{:S(2)}) async-start(), calls=%async_computation.16 | async-start | bytes 2654208 | tf_op jit(solution)/shard_map/reduce_scatter | solution.py:938
  306.5 38.8 %collective-permute-start.5 = (bf16[768,768]{1,0:T(8,128)(2,1)}, bf16[768,768]{1,0:T(8,128)(2,1)}, u32[]{:S(2)}, u32[]{:S(2)}) collective-permute-start(bf16[768,768]{1,0:T(8,128)(2,1)} %add_convert_fusion.1), channel_id=1, source_target_pairs={{0,2},{1,3},{2,0},{3,1},{4,6},{5,7},{6,4},{7,5},{8,10},{9,11},{10,... | collective-permute-start | bytes 3538952 | tf_op jit(solution)/shard_map/ppermute | solution.py:463
  314.4 30.9 %collective-permute-start.6 = (bf16[192,768]{1,0:T(8,128)(2,1)S(1)}, bf16[192,768]{1,0:T(8,128)(2,1)}, u32[]{:S(2)}, u32[]{:S(2)}) collective-permute-start(bf16[192,768]{1,0:T(8,128)(2,1)S(1)} %add_convert_fusion.5), channel_id=1, source_target_pairs={{0,2},{1,3},{2,0},{3,1},{4,6},{5,7},{6,4},{7,5},{8,10},{9,11},{10,... | collective-permute-start | bytes 884744 | tf_op jit(solution)/shard_map/ppermute | solution.py:463
  364.8 73.8 %all-to-all-start.5 = ((bf16[32,40,768]{2,1,0:T(8,128)(2,1)}), bf16[32,40,768]{2,1,0:T(8,128)(2,1)}, u32[]{:S(2)}, u32[]{:S(2)}) async-start(bf16[32,40,768]{2,1,0:T(8,128)(2,1)} %bitcast.214), calls=%async_computation.6 | async-start | bytes 3932160 | tf_op jit(solution)/shard_map/all_to_all | solution.py:963
  369.5 120.0 %reduce-scatter.8.cloned.1.call-start = ((), (), s32[]{:S(2)}) async-start(), calls=%async_computation.17 | async-start | bytes 2654208 | tf_op jit(solution)/shard_map/reduce_scatter | solution.py:957
  381.3 11.5 %collective-permute-start.8 = (f32[576,768]{1,0:T(8,128)}, f32[576,768]{1,0:T(8,128)}, u32[]{:S(2)}, u32[]{:S(2)}) collective-permute-start(f32[576,768]{1,0:T(8,128)} %get-tuple-element.133), channel_id=1, source_target_pairs={{0,1},{1,0},{2,3},{3,2},{4,5},{5,4},{6,7},{7,6},{8,9},{9,8},{10,11... | collective-permute-start | bytes 5308424 | tf_op jit(solution)/shard_map/ppermute | solution.py:463
  388.5 26.4 %collective-permute-start.7 = (f32[576,768]{1,0:T(8,128)}, f32[576,768]{1,0:T(8,128)S(1)}, u32[]{:S(2)}, u32[]{:S(2)}) collective-permute-start(f32[576,768]{1,0:T(8,128)} %get-tuple-element.132), channel_id=1, source_target_pairs={{0,1},{1,0},{2,3},{3,2},{4,5},{5,4},{6,7},{7,6},{8,9},{9,8},{10,11... | collective-permute-start | bytes 5308424 | tf_op jit(solution)/shard_map/ppermute | solution.py:463
  388.7 8.9 %collective-permute-start.10 = (f32[192,768]{1,0:T(8,128)}, f32[192,768]{1,0:T(8,128)S(1)}, u32[]{:S(2)}, u32[]{:S(2)}) collective-permute-start(f32[192,768]{1,0:T(8,128)} %get-tuple-element.293), channel_id=1, source_target_pairs={{0,1},{1,0},{2,3},{3,2},{4,5},{5,4},{6,7},{7,6},{8,9},{9,8},{10,11... | collective-permute-start | bytes 1769480 | tf_op jit(solution)/shard_map/ppermute | solution.py:463
  391.0 22.1 %collective-permute-start.12 = (f32[192,768]{1,0:T(8,128)}, f32[192,768]{1,0:T(8,128)}, u32[]{:S(2)}, u32[]{:S(2)}) collective-permute-start(f32[192,768]{1,0:T(8,128)} %dynamic-slice_add_fusion), channel_id=1, source_target_pairs={{0,2},{1,3},{2,0},{3,1},{4,6},{5,7},{6,4},{7,5},{8,10},{9,11},{10,... | collective-permute-start | bytes 1769480 | tf_op jit(solution)/shard_map/ppermute | solution.py:463
  395.8 38.6 %collective-permute-start.9 = (bf16[576,768]{1,0:T(8,128)(2,1)}, bf16[576,768]{1,0:T(8,128)(2,1)}, u32[]{:S(2)}, u32[]{:S(2)}) collective-permute-start(bf16[576,768]{1,0:T(8,128)(2,1)} %add_convert_fusion.3), channel_id=1, source_target_pairs={{0,2},{1,3},{2,0},{3,1},{4,6},{5,7},{6,4},{7,5},{8,10},{9,11},{10,... | collective-permute-start | bytes 2654216 | tf_op jit(solution)/shard_map/ppermute | solution.py:463
  438.6 50.5 %all-to-all-start.6 = ((bf16[8,128,768]{2,1,0:T(8,128)(2,1)}), bf16[8,128,768]{2,1,0:T(8,128)(2,1)S(1)}, u32[]{:S(2)}, u32[]{:S(2)}) async-start(bf16[8,128,768]{2,1,0:T(8,128)(2,1)} %pad_maximum_fusion), calls=%async_computation.7 | async-start | bytes 3145728 | tf_op jit(solution)/shard_map/all_to_all | solution.py:982
  495.5 39.3 %all-to-all-start.7 = ((bf16[8,96,768]{2,1,0:T(8,128)(2,1)}), bf16[8,96,768]{2,1,0:T(8,128)(2,1)S(1)}, u32[]{:S(2)}, u32[]{:S(2)}) async-start(bf16[8,96,768]{2,1,0:T(8,128)(2,1)} %bitcast.53), calls=%async_computation.10 | async-start | bytes 2359296 | tf_op jit(solution)/shard_map/all_to_all | solution.py:998
  499.0 110.1 %all-gather.17.cloned.1.call-start = ((), (), s32[]{:S(2)}) async-start(), calls=%async_computation.18 | async-start | bytes 4313088 | tf_op jit(solution)/shard_map/all_gather | solution.py:1020
  510.6 13.0 %collective-permute-start.22 = (f32[8,128]{1,0:T(8,128)S(1)}, f32[8,128]{1,0:T(8,128)S(1)}, u32[]{:S(2)}, u32[]{:S(2)}) collective-permute-start(f32[8,128]{1,0:T(8,128)S(1)} %add_add_fusion.2), channel_id=1, source_target_pairs={{0,28},{4,24},{8,20},{12,16},{16,12},{20,8},{24,4},{28,0},{1,29},{... | collective-permute-start | bytes 12296 | tf_op jit(solution)/shard_map/ppermute | solution.py:463
  515.4 14.4 %collective-permute-start.21 = (f32[8,128]{1,0:T(8,128)S(1)}, f32[8,128]{1,0:T(8,128)S(1)}, u32[]{:S(2)}, u32[]{:S(2)}) collective-permute-start(f32[8,128]{1,0:T(8,128)S(1)} %add_add_fusion.2), channel_id=1, source_target_pairs={{0,24},{4,28},{8,16},{12,20},{16,8},{20,12},{24,0},{28,4},{1,25},{... | collective-permute-start | bytes 12296 | tf_op jit(solution)/shard_map/ppermute | solution.py:463
  515.9 15.2 %collective-permute-start.20 = (f32[8,128]{1,0:T(8,128)S(1)}, f32[8,128]{1,0:T(8,128)S(1)}, u32[]{:S(2)}, u32[]{:S(2)}) collective-permute-start(f32[8,128]{1,0:T(8,128)S(1)} %add_add_fusion.2), channel_id=1, source_target_pairs={{0,20},{4,16},{8,28},{12,24},{16,4},{20,0},{24,12},{28,8},{1,21},{... | collective-permute-start | bytes 12296 | tf_op jit(solution)/shard_map/ppermute | solution.py:463
  516.5 14.6 %collective-permute-start.19 = (f32[8,128]{1,0:T(8,128)S(1)}, f32[8,128]{1,0:T(8,128)S(1)}, u32[]{:S(2)}, u32[]{:S(2)}) collective-permute-start(f32[8,128]{1,0:T(8,128)S(1)} %add_add_fusion.2), channel_id=1, source_target_pairs={{0,16},{4,20},{8,24},{12,28},{16,0},{20,4},{24,8},{28,12},{1,17},{... | collective-permute-start | bytes 12296 | tf_op jit(solution)/shard_map/ppermute | solution.py:463
  518.4 12.7 %collective-permute-start.18 = (f32[8,128]{1,0:T(8,128)S(1)}, f32[8,128]{1,0:T(8,128)S(1)}, u32[]{:S(2)}, u32[]{:S(2)}) collective-permute-start(f32[8,128]{1,0:T(8,128)S(1)} %add_add_fusion.2), channel_id=1, source_target_pairs={{0,12},{4,8},{8,4},{12,0},{16,28},{20,24},{24,20},{28,16},{1,13},{... | collective-permute-start | bytes 12296 | tf_op jit(solution)/shard_map/ppermute | solution.py:463
  541.6 148.9 %all-gather.19.cloned.1.call-start = ((), (), s32[]{:S(2)}) async-start(), calls=%async_computation.19 | async-start | bytes 5308416 | tf_op jit(solution)/shard_map/all_gather | solution.py:1027
  542.6 19.6 %collective-permute-start.24 = (f32[256,768]{1,0:T(8,128)S(1)}, f32[256,768]{1,0:T(8,128)S(1)}, u32[]{:S(2)}, u32[]{:S(2)}) collective-permute-start(f32[256,768]{1,0:T(8,128)S(1)} %bitcast_add_fusion.5), channel_id=1, source_target_pairs={{0,2},{1,3},{2,0},{3,1},{4,6},{5,7},{6,4},{7,5},{8,10},{9,11},{10,... | collective-permute-start | bytes 2359304 | tf_op jit(solution)/shard_map/ppermute | solution.py:463
  616.5 18.3 %collective-permute-start.27 = (bf16[128,192]{0,1:T(8,128)(2,1)S(1)}, bf16[128,192]{0,1:T(8,128)(2,1)S(1)}, u32[]{:S(2)}, u32[]{:S(2)}) collective-permute-start(bf16[128,192]{0,1:T(8,128)(2,1)S(1)} %get-tuple-element.300), channel_id=1, source_target_pairs={{0,2},{1,3},{2,0},{3,1},{4,6},{5,7},{6,4},{7,5},{8,10},{9,11},{10,... | collective-permute-start | bytes 147464 | tf_op jit(solution)/shard_map/ppermute | solution.py:463
  618.0 16.8 %collective-permute-start.26 = (bf16[128,192]{0,1:T(8,128)(2,1)S(1)}, bf16[128,192]{0,1:T(8,128)(2,1)S(1)}, u32[]{:S(2)}, u32[]{:S(2)}) collective-permute-start(bf16[128,192]{0,1:T(8,128)(2,1)S(1)} %get-tuple-element.300), channel_id=1, source_target_pairs={{0,1},{1,0},{2,3},{3,2},{4,5},{5,4},{6,7},{7,6},{8,9},{9,8},{10,11... | collective-permute-start | bytes 147464 | tf_op jit(solution)/shard_map/ppermute | solution.py:463
  618.3 15.9 %collective-permute-start.29 = (f32[64,128]{1,0:T(8,128)S(1)}, f32[64,128]{1,0:T(8,128)S(1)}, u32[]{:S(2)}, u32[]{:S(2)}) collective-permute-start(f32[64,128]{1,0:T(8,128)S(1)} %dynamic-slice_bitcast_fusion.2), channel_id=1, source_target_pairs={{0,1},{1,0},{2,3},{3,2},{4,5},{5,4},{6,7},{7,6},{8,9},{9,8},{10,11... | collective-permute-start | bytes 98312 | tf_op jit(solution)/shard_map/ppermute | solution.py:463
  (86 other events, 743.3 us)
Sparse Core Ops, SparseCore 0:
  12.5 26.9 all-gather.8
  41.6 46.3 all-gather.10
  90.1 36.7 all-gather.12
  128.9 37.4 all-gather.14
  271.2 32.3 reduce-scatter.3
  308.5 73.0 reduce-scatter.5
  392.9 94.6 reduce-scatter.7
  541.7 67.3 all-gather.16
  612.1 78.2 all-gather.18

commit v3 on v2

--- a/solution.py
+++ b/solution.py
@@ -725,7 +725,7 @@
         scratch_shapes=[pltpu.VMEM(*shape) for shape in shapes],
         compiler_params=pltpu.CompilerParams(vmem_limit_bytes=56 * 1024 * 1024),
         cost_estimate=pl.CostEstimate(
-            flops=6 * (13 * size + 5 * count) * size * size,
+            flops=5 * (13 * size + 5 * count) * size * size,
             bytes_accessed=8 * gram.size,
             transcendentals=0,
         ),
@@ -852,7 +852,7 @@
     h_low = low(h)
     wide = lax.optimization_barrier(dot_nt(h_low, in_t) + pieces[7])
     gelu_value, gelu_slope = gelu_parts(wide)
-    f_low, gelu_slope = tie(low(gelu_value), gelu_slope)
+    f_low, gelu_slope = tie(low(gelu_value), low(gelu_slope))
     o, o_hat, o_scale = norm_forward(h + dot_nn(f_low, out_t) + pieces[8], pieces[9], pieces[10])
     o_low = low(o)
     e = dot_nn(o_low, proj_t)
@@ -909,7 +909,7 @@
     d_y, out_sent, g_out = tie(d_y, out_sent, g_out)
     out_got = swap(out_sent, "narrow", narrow, 1)
     d_f = low(dot_nt(d_y, out_t)).astype(f32)
-    d_wide = d_f * gelu_slope
+    d_wide = d_f * gelu_slope.astype(f32)
     g_bias_in = column_sum(d_wide)
     d_wide = low(d_wide)
     d_wide, out_got = tie(d_wide, out_got)

time: 716 us -> 704 us (0.983)
    add x1 -> x0, other arithmetic: 9.53 us -> none  [gelu_parts(): return (values * cdf, cdf + values * density)]
    convert_element_type x10 -> x11, other arithmetic: 10.1 us -> 18.5 us  [low(): return values.astype(bf16)]
    unnamed x150 -> x146, local copies, waits for them, and re-layouts: 33 us -> 30.6 us
  transfers between devices with their start and end apart: 46 -> 46, of which waited for: 21 -> 19; matrix products, arithmetic and copies ran while one was open for 28% -> 28% of each run, Pallas kernels for 14% -> 15%
where the time goes in v3:
time: 704 us; the launch traced here: 698 us
  waiting for transfers between devices  200 us (28%)
  matrix products  122 us (17%)
  Pallas kernels  109 us (15%)
  other arithmetic  104 us (15%)
  local copies, waits for them, and re-layouts  54.1 us (8%)
  starting transfers between devices  49.9 us (7%)
  blocking collectives  36.5 us (5%)
  between operations  21.9 us (3%)
    ppermute x32, waiting for transfers between devices, swap(): lax.ppermute(value, axis, [(place, place ^ bit) for place in range(size)])  72.2 us
    dot_general x10, matrix products, dot_nn(): lax.dot_general(left, right, (((1,), (0,)), ((), ())), preferred_element_...  54.9 us
    pallas_call x2, Pallas kernels, newton_chain(): pl.pallas_call(chain_kernel, out_shape=jax.ShapeDtypeStruct(rows.shape, d...  40.6 us
    all_to_all x1, waiting for transfers between devices, body(): merged = lax.all_to_all(merged, 'blk', 0, 0, tiled=True)  40.3 us
    all_gather x1, waiting for transfers between devices, body(): ortho = lax.all_gather(ortho, 'blk', axis=0, tiled=False)  40.2 us
    dot_general x5, matrix products, dot_nt(): lax.dot_general(left, right, (((1,), (1,)), ((), ())), preferred_element_...  36.4 us
    unnamed x146, local copies, waits for them, and re-layouts  30.6 us
    ppermute x32, starting transfers between devices, swap(): lax.ppermute(value, axis, [(place, place ^ bit) for place in range(size)])  29.6 us
  transfers between devices with their start and end apart: 46, of which 19 were waited for; matrix products, arithmetic and copies ran while one was open for 28% of the time, Pallas kernels for 15%

profile of v3, /device:TPU:0, one launch (start us, length us, event | category | flops | bytes accessed | tf_op | source)
XLA Modules:
  0.0 697.8 jit_solution(12702050781143688588)
XLA Ops:
  19.8 14.3 %all_to_all.41 = s32[32,1,40]{2,1,0:T(1,128)S(1)} all-to-all(s32[32,1,40]{2,1,0:T(1,128)S(1)} %bitcast.228), channel_id=1, replica_groups=mesh['blk'=8,'narrow'=4] {'blk','narrow'}, dimensions={0} | all-to-all | bytes 10240 | tf_op jit(solution)/shard_map/all_to_all | solution.py:820
  64.3 24.6 %all-to-all-done.1 = bf16[32,40,768]{2,1,0:T(8,128)(2,1)} async-done(((bf16[32,40,768]{2,1,0:T(8,128)(2,1)}), bf16[32,40,768]{2,1,0:T(8,128)(2,1)}, u32[]{:S(2)}, u32[]{:S(2)}) %all-to-all-start.1) | async-done | bytes 1966112 | tf_op jit(solution)/shard_map/all_to_all | solution.py:825
  88.9 4.7 fusion.94
  98.3 9.0 %fusion.7.qkv_ref = bf16[1088,2304]{1,0:T(8,128)(2,1)} fusion(bf16[2304,768]{1,0:T(8,128)(2,1)} %all-gather.11.cloned.1.call-done, f32[2304]{0:T(1024)S(1)} %fusion.63, f32[1088,768]{1,0:T(8,128)S(1)} %subtract_multiply_fusion.4.hat_ref, f32[768]{0:T(1024)S(1)} %get-tuple-element.315, f32[768]{0:T(1024)S(1)} %get-tuple-element.316), kind=kOutput, calls=%fused_computation.13 | convolution fusion | flops 3857891328 | bytes 11910144 | tf_op jit(solution)/shard_map/dot_general | solution.py:49
  107.4 23.6 %shard_map.399 = (bf16[1088,768]{1,0:T(8,128)(2,1)S(1)}, f32[1088,128]{1,0:T(8,128)S(1)}) custom-call(s32[2]{0:T(128)S(1)} %bitcast.193, bf16[1088,2304]{1,0:T(8,128)(2,1)} %fusion.7.qkv_ref), custom_call_target="tpu_custom_call" | custom-call | flops 3221225472 | bytes 6684672 | tf_op jit(solution)/shard_map/pallas_call | solution.py:128
  137.1 9.4 %convolution_add_fusion.1 = f32[1088,3072]{1,0:T(8,128)S(1)} fusion(bf16[3072,768]{0,1:T(8,128)(2,1)} %all-gather.13.cloned.1.call-done, f32[3072]{0:T(1024)S(1)} %slice.219, f32[1088,768]{1,0:T(8,128)} %get-tuple-element.322, f32[768]{0:T(1024)S(1)} %get-tuple-element.310, f32[768]{0:T(1024)S(1)} %get-tuple-element.311, f32[1088]{0:T(1024)S(1)} %add_rsqrt_fusion.2, ...), kind=kOutput, calls=%fused_computation.2 | convolution fusion | flops 5141348352 | bytes 21457408 | tf_op jit(solution)/shard_map/dot_general | solution.py:49
  146.5 8.4 %fusion.4 = (bf16[1088,3072]{1,0:T(8,128)(2,1)}, bf16[1088,3072]{1,0:T(8,128)(2,1)}) fusion(f32[1088,3072]{1,0:T(8,128)S(1)} %convolution_add_fusion.1), kind=kLoop, calls=%fused_computation.7 | loop fusion | flops 36765696 | bytes 26738688 | tf_op jit(solution)/shard_map/convert_element_type | solution.py:57
  154.9 11.6 %all-gather.15.cloned.1.call-done = bf16[3072,768]{0,1:T(8,128)(2,1)} async-done(((bf16[768,768]{0,1:T(8,128)(2,1)}), bf16[3072,768]{0,1:T(8,128)(2,1)}) %all-gather.15.cloned.1.call-update) | async-done | bytes 4718608 | tf_op jit(solution)/shard_map/all_gather | solution.py:790
  166.4 11.1 %fusion.93 = (f32[1088]{0:T(1024)S(1)}, f32[1088,768]{1,0:T(8,128)S(1)}) fusion(f32[768]{0:T(1024)S(1)} %get-tuple-element.309, bf16[1088,3072]{1,0:T(8,128)(2,1)} %get-tuple-element.95, bf16[3072,768]{0,1:T(8,128)(2,1)} %all-gather.15.cloned.1.call-done, f32[768]{0:T(1024)S(1)} %get-tuple-element.310, f32[768]{0:T(1024)S(1)} %get-tuple-element.311, ...), kind=kOutput, calls=%fused_computation.279 | convolution fusion | flops 5139676160 | bytes 18110208 | tf_op jit(solution)/shard_map/dot_general | solution.py:45
  181.0 12.7 %all_to_all.42.cycle_ref = bf16[8,64,128]{2,1,0:T(8,128)(2,1)S(1)} all-to-all(bf16[8,64,128]{2,1,0:T(8,128)(2,1)S(1)} %broadcast_in_dim.131), channel_id=1, replica_groups=mesh['blk'=8,'narrow'=4] {'blk'}, dimensions={0} | all-to-all | bytes 262144 | tf_op jit(solution)/shard_map/all_to_all | solution.py:459
  195.1 9.6 %all_to_all.43.every_ref = f32[8,16,128]{2,1,0:T(8,128)S(1)} all-to-all(f32[8,16,128]{2,1,0:T(8,128)S(1)} %broadcast_in_dim.133), channel_id=1, replica_groups=mesh['blk'=8,'narrow'=4] {'blk'}, dimensions={0} | all-to-all | bytes 131072 | tf_op jit(solution)/shard_map/all_to_all | solution.py:459
  210.8 7.4 %all-to-all-done.4 = f32[8,64,128]{2,1,0:T(8,128)} async-done(((f32[8,64,128]{2,1,0:T(8,128)}), f32[8,64,128]{2,1,0:T(8,128)}, u32[]{:S(2)}, u32[]{:S(2)}) %all-to-all-start.4) | async-done | bytes 262176 | tf_op jit(solution)/shard_map/all_to_all | solution.py:886
  227.8 6.4 fusion.95
  239.3 11.1 %fusion.5 = (f32[3072]{0:T(1024)S(1)}, bf16[1088,3072]{1,0:T(8,128)(2,1)}) fusion(bf16[1088,3072]{1,0:T(8,128)(2,1)} %get-tuple-element.104, bf16[1088,768]{1,0:T(8,128)(2,1)} %copy-done.43, bf16[3072,768]{0,1:T(8,128)(2,1)} %all-gather.15.cloned.1.call-done), kind=kOutput, calls=%fused_computation.11 | convolution fusion | flops 5153879040 | bytes 19771392 | tf_op jit(solution)/shard_map/dot_general | solution.py:49
  250.4 4.4 fusion.13
  254.8 10.4 %fusion.79 = f32[3072,768]{1,0:T(8,128)S(1)} fusion(bf16[1088,3072]{1,0:T(8,128)(2,1)} %get-tuple-element.116, f32[1088,768]{1,0:T(8,128)} %get-tuple-element.322, f32[768]{0:T(1024)S(1)} %get-tuple-element.310, f32[768]{0:T(1024)S(1)} %get-tuple-element.311, f32[1088]{0:T(1024)S(1)} %add_rsqrt_fusion.2, f32[1088]{0:T(1024)S(1)} %broadcast_multiply_fusion.7), kind=kOutput, calls=%fused_computation.272 | convolution fusion | flops 5138006016 | bytes 19479040 | tf_op jit(solution)/shard_map/dot_general | solution.py:53
  281.4 10.0 %multiply_reduce_fusion = (f32[768]{0:T(1024)S(1)}, f32[1088]{0:T(1024)S(1)}, f32[1088]{0:T(1024)S(1)}, f32[768]{0:T(1024)S(1)}, f32[1088,768]{1,0:T(8,128)S(1)}) fusion(f32[1088,768]{1,0:T(8,128)} %get-tuple-element.322, f32[1088]{0:T(1024)S(1)} %add_rsqrt_fusion.2, f32[1088]{0:T(1024)S(1)} %broadcast_multiply_fusion.7, f32[768]{0:T(1024)S(1)} %get-tuple-element.311, ...), kind=kOutput, calls=%fused_computation.58 | convolution fusion | flops 5143851008 | bytes 21456896 | tf_op jit(solution)/shard_map/dot_general | solution.py:45
  314.6 29.1 %shard_map.402.qkv_ref = bf16[1088,2304]{1,0:T(8,128)(2,1)} custom-call(s32[2]{0:T(128)S(1)} %bitcast.195, bf16[1088,2304]{1,0:T(8,128)(2,1)} %fusion.7.qkv_ref, bf16[1088,768]{1,0:T(8,128)(2,1)S(1)} %convolution_convert_fusion.5.grad_ref, f32[2,16,544]{2,1,0:T(8,128)S(1)} %pad_maximum_fusion.5.norm_ref, f32[2,16,544]{2,1,0:T(8,128)S(1)} %pad_maximum_fusion.6.inner_ref), custom_call_target="tpu_custom_call" | custom-call | flops 8053063680 | bytes 11698176 | tf_op jit(solution)/shard_map/pallas_call | solution.py:245
  346.9 9.3 %multiply_reduce_fusion.7 = (f32[1088]{0:T(1024)S(1)}, f32[1088]{0:T(1024)S(1)}, f32[1088,768]{1,0:T(8,128)S(1)}) fusion(f32[768]{0:T(1024)S(1)} %get-tuple-element.316, f32[1088,768]{1,0:T(8,128)S(1)} %copy-done.13, f32[1088,768]{1,0:T(8,128)} %copy-done.24, bf16[1088,2304]{1,0:T(8,128)(2,1)} %shard_map.402.qkv_ref, ...), kind=kOutput, calls=%fused_computation.83 | convolution fusion | flops 3856218112 | bytes 18591232 | tf_op jit(solution)/shard_map/dot_general | solution.py:45
  363.2 4.7 all-to-all-start.5
  368.0 7.8 %fusion.49 = f32[2304,768]{1,0:T(8,128)S(1)} fusion(bf16[1088,2304]{1,0:T(8,128)(2,1)} %shard_map.402.qkv_ref, f32[1088,768]{1,0:T(8,128)} %copy-done.11, f32[768]{0:T(1024)S(1)} %copy-done.61, f32[768]{0:T(1024)S(1)} %get-tuple-element.316), kind=kOutput, calls=%fused_computation.136 | convolution fusion | flops 3852877824 | bytes 15439872 | tf_op jit(solution)/shard_map/dot_general | solution.py:53
  380.0 5.6 shard_map.403
  396.1 15.5 %collective-permute-done.12 = f32[192,768]{1,0:T(8,128)} collective-permute-done((f32[192,768]{1,0:T(8,128)}, f32[192,768]{1,0:T(8,128)}, u32[]{:S(2)}, u32[]{:S(2)}) %collective-permute-start.12) | collective-permute-done | bytes 589856 | tf_op jit(solution)/shard_map/ppermute | solution.py:463
  413.4 19.6 %collective-permute-done.9 = bf16[576,768]{1,0:T(8,128)(2,1)} collective-permute-done((bf16[576,768]{1,0:T(8,128)(2,1)}, bf16[576,768]{1,0:T(8,128)(2,1)}, u32[]{:S(2)}, u32[]{:S(2)}) %collective-permute-start.9) | collective-permute-done | bytes 884768 | tf_op jit(solution)/shard_map/ppermute | solution.py:463
  440.6 6.6 multiply_reduce_fusion.6
  447.2 40.3 %all-to-all-done.6 = bf16[8,128,768]{2,1,0:T(8,128)(2,1)S(1)} async-done(((bf16[8,128,768]{2,1,0:T(8,128)(2,1)}), bf16[8,128,768]{2,1,0:T(8,128)(2,1)S(1)}, u32[]{:S(2)}, u32[]{:S(2)}) %all-to-all-start.6) | async-done | bytes 1572896 | tf_op jit(solution)/shard_map/all_to_all | solution.py:982
  507.8 4.7 collective-permute-start.22
  520.7 6.2 collective-permute-start.17
  539.8 18.1 %collective-permute-done.24 = f32[256,768]{1,0:T(8,128)S(1)} collective-permute-done((f32[256,768]{1,0:T(8,128)S(1)}, f32[256,768]{1,0:T(8,128)S(1)}, u32[]{:S(2)}, u32[]{:S(2)}) %collective-permute-start.24) | collective-permute-done | bytes 786464 | tf_op jit(solution)/shard_map/ppermute | solution.py:463
  563.0 36.6 %shard_map.405 = bf16[384,768]{1,0:T(8,128)(2,1)} custom-call(f32[512,768]{1,0:T(8,128)} %pad_maximum_fusion.1.gram_in, f32[384,768]{1,0:T(8,128)} %constant_dynamic-slice_fusion.rows_in), custom_call_target="tpu_custom_call" | custom-call | flops 35106324480 | bytes 3145728 | tf_op jit(solution)/shard_map/pallas_call | solution.py:720
  599.7 7.3 %multiply_subtract_fusion = (f32[960,768]{1,0:T(8,128)}, f32[960,768]{1,0:T(8,128)}, f32[960,768]{1,0:T(8,128)}) fusion(f32[960,768]{1,0:T(8,128)S(1)} %copy-done.36, f32[960,768]{1,0:T(8,128)} %get-tuple-element.331, f32[]{:T(128)} %min.3, f32[960,768]{1,0:T(8,128)} %param.30, f32[960,768]{1,0:T(8,128)} %param.31), kind=kLoop, calls=%fused_computation.78 | loop fusion | flops 11796480 | bytes 20643844 | tf_op jit(solution)/shard_map/sub | solution.py:606
  637.9 40.2 %all-gather.19.cloned.1.call-done = bf16[3072,768]{1,0:T(8,128)(2,1)} async-done(((bf16[384,768]{1,0:T(8,128)(2,1)}), bf16[3072,768]{1,0:T(8,128)(2,1)}) %all-gather.19.cloned.1.call-update) | async-done | bytes 4718608 | tf_op jit(solution)/shard_map/all_gather | solution.py:1027
  (445 shorter events, 235.7 us)
Async XLA Ops:
  7.2 54.1 %all-gather.9.cloned.1.call-start = ((), (), s32[]{:S(2)}) async-start(), calls=%async_computation.11 | async-start | bytes 2949120 | tf_op jit(solution)/shard_map/all_gather | solution.py:790
  12.3 86.0 %all-gather.11.cloned.1.call-start = ((), (), s32[]{:S(2)}) async-start(), calls=%async_computation.12 | async-start | bytes 4423680 | tf_op jit(solution)/shard_map/all_gather | solution.py:790
  14.9 122.2 %all-gather.13.cloned.1.call-start = ((), (), s32[]{:S(2)}) async-start(), calls=%async_computation.13 | async-start | bytes 5898240 | tf_op jit(solution)/shard_map/all_gather | solution.py:790
  39.4 49.5 %all-to-all-start.1 = ((bf16[32,40,768]{2,1,0:T(8,128)(2,1)}), bf16[32,40,768]{2,1,0:T(8,128)(2,1)}, u32[]{:S(2)}, u32[]{:S(2)}) async-start(bf16[32,40,768]{2,1,0:T(8,128)(2,1)} %bitcast.215), calls=%async_computation.1 | async-start | bytes 3932160 | tf_op jit(solution)/shard_map/all_to_all | solution.py:825
  43.0 123.4 %all-gather.15.cloned.1.call-start = ((), (), s32[]{:S(2)}) async-start(), calls=%async_computation.14 | async-start | bytes 5898240 | tf_op jit(solution)/shard_map/all_gather | solution.py:790
  206.0 12.3 %all-to-all-start.4 = ((f32[8,64,128]{2,1,0:T(8,128)}), f32[8,64,128]{2,1,0:T(8,128)}, u32[]{:S(2)}, u32[]{:S(2)}) async-start(f32[8,64,128]{2,1,0:T(8,128)} %get-tuple-element.101), calls=%async_computation.4 | async-start | bytes 524288 | tf_op jit(solution)/shard_map/all_to_all | solution.py:886
  210.0 92.1 %reduce-scatter.4.cloned.1.call-start = ((), (), s32[]{:S(2)}) async-start(), calls=%async_computation.15 | async-start | bytes 3538944 | tf_op jit(solution)/shard_map/reduce_scatter | solution.py:921
  239.3 11.1 %collective-permute-start = (f32[2,768,768]{2,1,0:T(8,128)}, f32[2,768,768]{2,1,0:T(8,128)}, u32[]{:S(2)}, u32[]{:S(2)}) collective-permute-start(f32[2,768,768]{2,1,0:T(8,128)} %dynamic-slice_bitcast_fusion), channel_id=1, source_target_pairs={{0,1},{1,0},{2,3},{3,2},{4,5},{5,4},{6,7},{7,6},{8,9},{9,8},{10,11... | collective-permute-start | bytes 14155784 | tf_op jit(solution)/shard_map/ppermute | solution.py:463
  269.5 8.7 %collective-permute-start.1 = (f32[768,768]{1,0:T(8,128)}, f32[768,768]{1,0:T(8,128)}, u32[]{:S(2)}, u32[]{:S(2)}) collective-permute-start(f32[768,768]{1,0:T(8,128)} %get-tuple-element.113), channel_id=1, source_target_pairs={{0,1},{1,0},{2,3},{3,2},{4,5},{5,4},{6,7},{7,6},{8,9},{9,8},{10,11... | collective-permute-start | bytes 7077896 | tf_op jit(solution)/shard_map/ppermute | solution.py:463
  269.6 218.2 %reduce-scatter.6.cloned.1.call-start = ((), (), s32[]{:S(2)}) async-start(), calls=%async_computation.16 | async-start | bytes 2654208 | tf_op jit(solution)/shard_map/reduce_scatter | solution.py:938
  305.0 38.8 %collective-permute-start.5 = (bf16[768,768]{1,0:T(8,128)(2,1)}, bf16[768,768]{1,0:T(8,128)(2,1)}, u32[]{:S(2)}, u32[]{:S(2)}) collective-permute-start(bf16[768,768]{1,0:T(8,128)(2,1)} %add_convert_fusion.1), channel_id=1, source_target_pairs={{0,2},{1,3},{2,0},{3,1},{4,6},{5,7},{6,4},{7,5},{8,10},{9,11},{10,... | collective-permute-start | bytes 3538952 | tf_op jit(solution)/shard_map/ppermute | solution.py:463
  312.9 30.9 %collective-permute-start.6 = (bf16[192,768]{1,0:T(8,128)(2,1)S(1)}, bf16[192,768]{1,0:T(8,128)(2,1)}, u32[]{:S(2)}, u32[]{:S(2)}) collective-permute-start(bf16[192,768]{1,0:T(8,128)(2,1)S(1)} %add_convert_fusion.5), channel_id=1, source_target_pairs={{0,2},{1,3},{2,0},{3,1},{4,6},{5,7},{6,4},{7,5},{8,10},{9,11},{10,... | collective-permute-start | bytes 884744 | tf_op jit(solution)/shard_map/ppermute | solution.py:463
  363.2 73.8 %all-to-all-start.5 = ((bf16[32,40,768]{2,1,0:T(8,128)(2,1)}), bf16[32,40,768]{2,1,0:T(8,128)(2,1)}, u32[]{:S(2)}, u32[]{:S(2)}) async-start(bf16[32,40,768]{2,1,0:T(8,128)(2,1)} %bitcast.214), calls=%async_computation.6 | async-start | bytes 3932160 | tf_op jit(solution)/shard_map/all_to_all | solution.py:963
  368.0 119.9 %reduce-scatter.8.cloned.1.call-start = ((), (), s32[]{:S(2)}) async-start(), calls=%async_computation.17 | async-start | bytes 2654208 | tf_op jit(solution)/shard_map/reduce_scatter | solution.py:957
  379.7 11.5 %collective-permute-start.8 = (f32[576,768]{1,0:T(8,128)}, f32[576,768]{1,0:T(8,128)}, u32[]{:S(2)}, u32[]{:S(2)}) collective-permute-start(f32[576,768]{1,0:T(8,128)} %get-tuple-element.133), channel_id=1, source_target_pairs={{0,1},{1,0},{2,3},{3,2},{4,5},{5,4},{6,7},{7,6},{8,9},{9,8},{10,11... | collective-permute-start | bytes 5308424 | tf_op jit(solution)/shard_map/ppermute | solution.py:463
  386.9 26.4 %collective-permute-start.7 = (f32[576,768]{1,0:T(8,128)}, f32[576,768]{1,0:T(8,128)S(1)}, u32[]{:S(2)}, u32[]{:S(2)}) collective-permute-start(f32[576,768]{1,0:T(8,128)} %get-tuple-element.132), channel_id=1, source_target_pairs={{0,1},{1,0},{2,3},{3,2},{4,5},{5,4},{6,7},{7,6},{8,9},{9,8},{10,11... | collective-permute-start | bytes 5308424 | tf_op jit(solution)/shard_map/ppermute | solution.py:463
  387.1 8.9 %collective-permute-start.10 = (f32[192,768]{1,0:T(8,128)}, f32[192,768]{1,0:T(8,128)S(1)}, u32[]{:S(2)}, u32[]{:S(2)}) collective-permute-start(f32[192,768]{1,0:T(8,128)} %get-tuple-element.293), channel_id=1, source_target_pairs={{0,1},{1,0},{2,3},{3,2},{4,5},{5,4},{6,7},{7,6},{8,9},{9,8},{10,11... | collective-permute-start | bytes 1769480 | tf_op jit(solution)/shard_map/ppermute | solution.py:463
  389.5 22.1 %collective-permute-start.12 = (f32[192,768]{1,0:T(8,128)}, f32[192,768]{1,0:T(8,128)}, u32[]{:S(2)}, u32[]{:S(2)}) collective-permute-start(f32[192,768]{1,0:T(8,128)} %dynamic-slice_add_fusion), channel_id=1, source_target_pairs={{0,2},{1,3},{2,0},{3,1},{4,6},{5,7},{6,4},{7,5},{8,10},{9,11},{10,... | collective-permute-start | bytes 1769480 | tf_op jit(solution)/shard_map/ppermute | solution.py:463
  394.3 38.6 %collective-permute-start.9 = (bf16[576,768]{1,0:T(8,128)(2,1)}, bf16[576,768]{1,0:T(8,128)(2,1)}, u32[]{:S(2)}, u32[]{:S(2)}) collective-permute-start(bf16[576,768]{1,0:T(8,128)(2,1)} %add_convert_fusion.3), channel_id=1, source_target_pairs={{0,2},{1,3},{2,0},{3,1},{4,6},{5,7},{6,4},{7,5},{8,10},{9,11},{10,... | collective-permute-start | bytes 2654216 | tf_op jit(solution)/shard_map/ppermute | solution.py:463
  437.0 50.5 %all-to-all-start.6 = ((bf16[8,128,768]{2,1,0:T(8,128)(2,1)}), bf16[8,128,768]{2,1,0:T(8,128)(2,1)S(1)}, u32[]{:S(2)}, u32[]{:S(2)}) async-start(bf16[8,128,768]{2,1,0:T(8,128)(2,1)} %pad_maximum_fusion), calls=%async_computation.7 | async-start | bytes 3145728 | tf_op jit(solution)/shard_map/all_to_all | solution.py:982
  492.6 39.3 %all-to-all-start.7 = ((bf16[8,96,768]{2,1,0:T(8,128)(2,1)}), bf16[8,96,768]{2,1,0:T(8,128)(2,1)S(1)}, u32[]{:S(2)}, u32[]{:S(2)}) async-start(bf16[8,96,768]{2,1,0:T(8,128)(2,1)} %bitcast.53), calls=%async_computation.10 | async-start | bytes 2359296 | tf_op jit(solution)/shard_map/all_to_all | solution.py:998
  496.2 103.5 %all-gather.17.cloned.1.call-start = ((), (), s32[]{:S(2)}) async-start(), calls=%async_computation.18 | async-start | bytes 4313088 | tf_op jit(solution)/shard_map/all_gather | solution.py:1020
  507.8 13.0 %collective-permute-start.22 = (f32[8,128]{1,0:T(8,128)S(1)}, f32[8,128]{1,0:T(8,128)S(1)}, u32[]{:S(2)}, u32[]{:S(2)}) collective-permute-start(f32[8,128]{1,0:T(8,128)S(1)} %add_add_fusion.2), channel_id=1, source_target_pairs={{0,28},{4,24},{8,20},{12,16},{16,12},{20,8},{24,4},{28,0},{1,29},{... | collective-permute-start | bytes 12296 | tf_op jit(solution)/shard_map/ppermute | solution.py:463
  512.5 14.4 %collective-permute-start.21 = (f32[8,128]{1,0:T(8,128)S(1)}, f32[8,128]{1,0:T(8,128)S(1)}, u32[]{:S(2)}, u32[]{:S(2)}) collective-permute-start(f32[8,128]{1,0:T(8,128)S(1)} %add_add_fusion.2), channel_id=1, source_target_pairs={{0,24},{4,28},{8,16},{12,20},{16,8},{20,12},{24,0},{28,4},{1,25},{... | collective-permute-start | bytes 12296 | tf_op jit(solution)/shard_map/ppermute | solution.py:463
  513.1 15.5 %collective-permute-start.20 = (f32[8,128]{1,0:T(8,128)S(1)}, f32[8,128]{1,0:T(8,128)S(1)}, u32[]{:S(2)}, u32[]{:S(2)}) collective-permute-start(f32[8,128]{1,0:T(8,128)S(1)} %add_add_fusion.2), channel_id=1, source_target_pairs={{0,20},{4,16},{8,28},{12,24},{16,4},{20,0},{24,12},{28,8},{1,21},{... | collective-permute-start | bytes 12296 | tf_op jit(solution)/shard_map/ppermute | solution.py:463
  513.7 14.9 %collective-permute-start.19 = (f32[8,128]{1,0:T(8,128)S(1)}, f32[8,128]{1,0:T(8,128)S(1)}, u32[]{:S(2)}, u32[]{:S(2)}) collective-permute-start(f32[8,128]{1,0:T(8,128)S(1)} %add_add_fusion.2), channel_id=1, source_target_pairs={{0,16},{4,20},{8,24},{12,28},{16,0},{20,4},{24,8},{28,12},{1,17},{... | collective-permute-start | bytes 12296 | tf_op jit(solution)/shard_map/ppermute | solution.py:463
  515.6 13.0 %collective-permute-start.18 = (f32[8,128]{1,0:T(8,128)S(1)}, f32[8,128]{1,0:T(8,128)S(1)}, u32[]{:S(2)}, u32[]{:S(2)}) collective-permute-start(f32[8,128]{1,0:T(8,128)S(1)} %add_add_fusion.2), channel_id=1, source_target_pairs={{0,12},{4,8},{8,4},{12,0},{16,28},{20,24},{24,20},{28,16},{1,13},{... | collective-permute-start | bytes 12296 | tf_op jit(solution)/shard_map/ppermute | solution.py:463
  528.3 149.8 %all-gather.19.cloned.1.call-start = ((), (), s32[]{:S(2)}) async-start(), calls=%async_computation.19 | async-start | bytes 5308416 | tf_op jit(solution)/shard_map/all_gather | solution.py:1027
  538.3 19.6 %collective-permute-start.24 = (f32[256,768]{1,0:T(8,128)S(1)}, f32[256,768]{1,0:T(8,128)S(1)}, u32[]{:S(2)}, u32[]{:S(2)}) collective-permute-start(f32[256,768]{1,0:T(8,128)S(1)} %bitcast_add_fusion.5), channel_id=1, source_target_pairs={{0,2},{1,3},{2,0},{3,1},{4,6},{5,7},{6,4},{7,5},{8,10},{9,11},{10,... | collective-permute-start | bytes 2359304 | tf_op jit(solution)/shard_map/ppermute | solution.py:463
  607.1 18.3 %collective-permute-start.27 = (bf16[128,192]{0,1:T(8,128)(2,1)S(1)}, bf16[128,192]{0,1:T(8,128)(2,1)S(1)}, u32[]{:S(2)}, u32[]{:S(2)}) collective-permute-start(bf16[128,192]{0,1:T(8,128)(2,1)S(1)} %get-tuple-element.300), channel_id=1, source_target_pairs={{0,2},{1,3},{2,0},{3,1},{4,6},{5,7},{6,4},{7,5},{8,10},{9,11},{10,... | collective-permute-start | bytes 147464 | tf_op jit(solution)/shard_map/ppermute | solution.py:463
  608.7 16.8 %collective-permute-start.26 = (bf16[128,192]{0,1:T(8,128)(2,1)S(1)}, bf16[128,192]{0,1:T(8,128)(2,1)S(1)}, u32[]{:S(2)}, u32[]{:S(2)}) collective-permute-start(bf16[128,192]{0,1:T(8,128)(2,1)S(1)} %get-tuple-element.300), channel_id=1, source_target_pairs={{0,1},{1,0},{2,3},{3,2},{4,5},{5,4},{6,7},{7,6},{8,9},{9,8},{10,11... | collective-permute-start | bytes 147464 | tf_op jit(solution)/shard_map/ppermute | solution.py:463
  609.0 15.9 %collective-permute-start.29 = (f32[64,128]{1,0:T(8,128)S(1)}, f32[64,128]{1,0:T(8,128)S(1)}, u32[]{:S(2)}, u32[]{:S(2)}) collective-permute-start(f32[64,128]{1,0:T(8,128)S(1)} %dynamic-slice_bitcast_fusion.2), channel_id=1, source_target_pairs={{0,1},{1,0},{2,3},{3,2},{4,5},{5,4},{6,7},{7,6},{8,9},{9,8},{10,11... | collective-permute-start | bytes 98312 | tf_op jit(solution)/shard_map/ppermute | solution.py:463
  (83 other events, 702.8 us)
Sparse Core Ops, SparseCore 0:
  12.4 26.9 all-gather.8
  41.6 46.3 all-gather.10
  90.1 36.7 all-gather.12
  128.9 37.4 all-gather.14
  269.7 32.3 reduce-scatter.3
  307.0 72.9 reduce-scatter.5
  391.3 94.5 reduce-scatter.7
  528.4 67.8 all-gather.16
  599.8 78.2 all-gather.18

commit v4 on v3

--- a/solution.py
+++ b/solution.py
@@ -562,10 +562,6 @@
 
 def sum_everywhere(value, sizes):
     for axis, size in sizes:
-        if size <= 8:
-            swaps = [swap(value, axis, size, offset) for offset in range(1, size)]
-            value = sum(swaps, value)
-            continue
         bit = 1
         while bit < size:
             value = value + swap(value, axis, size, bit)

time: 704 us -> 699 us (level)
  starting transfers between devices: 49.9 us -> 40.4 us
    ppermute x32 -> x27, starting transfers between devices: 29.6 us -> 20.1 us  [swap(): lax.ppermute(value, axis, [(place, place ^ bit) for place in range(size)])]
    ppermute x32 -> x27, waiting for transfers between devices: 72.2 us -> 76.3 us  [swap(): lax.ppermute(value, axis, [(place, place ^ bit) for place in range(size)])]
  transfers between devices with their start and end apart: 46 -> 41, of which waited for: 19 -> 20; matrix products, arithmetic and copies ran while one was open for 28% -> 28% of each run, Pallas kernels for 15% -> 15%
where the time goes in v4:
time: 699 us; the launch traced here: 693 us
  waiting for transfers between devices  205 us (29%)
  matrix products  122 us (17%)
  Pallas kernels  110 us (16%)
  other arithmetic  104 us (15%)
  local copies, waits for them, and re-layouts  54 us (8%)
  starting transfers between devices  40.4 us (6%)
  blocking collectives  36.5 us (5%)
  between operations  21.9 us (3%)
    ppermute x27, waiting for transfers between devices, swap(): lax.ppermute(value, axis, [(place, place ^ bit) for place in range(size)])  76.3 us
    dot_general x10, matrix products, dot_nn(): lax.dot_general(left, right, (((1,), (0,)), ((), ())), preferred_element_...  54.8 us
    all_gather x1, waiting for transfers between devices, body(): ortho = lax.all_gather(ortho, 'blk', axis=0, tiled=False)  40.7 us
    pallas_call x2, Pallas kernels, newton_chain(): pl.pallas_call(chain_kernel, out_shape=jax.ShapeDtypeStruct(rows.shape, d...  40.6 us
    all_to_all x1, waiting for transfers between devices, body(): merged = lax.all_to_all(merged, 'blk', 0, 0, tiled=True)  40.3 us
    dot_general x5, matrix products, dot_nt(): lax.dot_general(left, right, (((1,), (1,)), ((), ())), preferred_element_...  36.4 us
    unnamed x146, local copies, waits for them, and re-layouts  30.6 us
    dot_general x6, matrix products, dot_tn(): lax.dot_general(left, right, (((0,), (0,)), ((), ())), preferred_element_...  29.3 us
  transfers between devices with their start and end apart: 41, of which 20 were waited for; matrix products, arithmetic and copies ran while one was open for 28% of the time, Pallas kernels for 15%

profile of v4, /device:TPU:0, one launch (start us, length us, event | category | flops | bytes accessed | tf_op | source)
XLA Modules:
  0.0 693.0 jit_solution(488719042886382944)
XLA Ops:
  19.8 14.3 %all_to_all.41 = s32[32,1,40]{2,1,0:T(1,128)S(1)} all-to-all(s32[32,1,40]{2,1,0:T(1,128)S(1)} %bitcast.228), channel_id=1, replica_groups=mesh['blk'=8,'narrow'=4] {'blk','narrow'}, dimensions={0} | all-to-all | bytes 10240 | tf_op jit(solution)/shard_map/all_to_all | solution.py:816
  64.3 24.6 %all-to-all-done.1 = bf16[32,40,768]{2,1,0:T(8,128)(2,1)} async-done(((bf16[32,40,768]{2,1,0:T(8,128)(2,1)}), bf16[32,40,768]{2,1,0:T(8,128)(2,1)}, u32[]{:S(2)}, u32[]{:S(2)}) %all-to-all-start.1) | async-done | bytes 1966112 | tf_op jit(solution)/shard_map/all_to_all | solution.py:821
  88.9 4.7 fusion.95
  98.4 9.0 %fusion.7.qkv_ref = bf16[1088,2304]{1,0:T(8,128)(2,1)} fusion(bf16[2304,768]{1,0:T(8,128)(2,1)} %all-gather.11.cloned.1.call-done, f32[2304]{0:T(1024)S(1)} %fusion.63, f32[1088,768]{1,0:T(8,128)S(1)} %subtract_multiply_fusion.4.hat_ref, f32[768]{0:T(1024)S(1)} %get-tuple-element.315, f32[768]{0:T(1024)S(1)} %get-tuple-element.316), kind=kOutput, calls=%fused_computation.13 | convolution fusion | flops 3857891328 | bytes 11910144 | tf_op jit(solution)/shard_map/dot_general | solution.py:49
  107.4 23.6 %shard_map.399 = (bf16[1088,768]{1,0:T(8,128)(2,1)S(1)}, f32[1088,128]{1,0:T(8,128)S(1)}) custom-call(s32[2]{0:T(128)S(1)} %bitcast.193, bf16[1088,2304]{1,0:T(8,128)(2,1)} %fusion.7.qkv_ref), custom_call_target="tpu_custom_call" | custom-call | flops 3221225472 | bytes 6684672 | tf_op jit(solution)/shard_map/pallas_call | solution.py:128
  137.1 9.4 %convolution_add_fusion.1 = f32[1088,3072]{1,0:T(8,128)S(1)} fusion(bf16[3072,768]{0,1:T(8,128)(2,1)} %all-gather.13.cloned.1.call-done, f32[3072]{0:T(1024)S(1)} %slice.219, f32[1088,768]{1,0:T(8,128)} %get-tuple-element.322, f32[768]{0:T(1024)S(1)} %get-tuple-element.310, f32[768]{0:T(1024)S(1)} %get-tuple-element.311, f32[1088]{0:T(1024)S(1)} %add_rsqrt_fusion.2, ...), kind=kOutput, calls=%fused_computation.2 | convolution fusion | flops 5141348352 | bytes 21457408 | tf_op jit(solution)/shard_map/dot_general | solution.py:49
  146.5 8.4 %fusion.4 = (bf16[1088,3072]{1,0:T(8,128)(2,1)}, bf16[1088,3072]{1,0:T(8,128)(2,1)}) fusion(f32[1088,3072]{1,0:T(8,128)S(1)} %convolution_add_fusion.1), kind=kLoop, calls=%fused_computation.7 | loop fusion | flops 36765696 | bytes 26738688 | tf_op jit(solution)/shard_map/convert_element_type | solution.py:57
  154.9 11.5 %all-gather.15.cloned.1.call-done = bf16[3072,768]{0,1:T(8,128)(2,1)} async-done(((bf16[768,768]{0,1:T(8,128)(2,1)}), bf16[3072,768]{0,1:T(8,128)(2,1)}) %all-gather.15.cloned.1.call-update) | async-done | bytes 4718608 | tf_op jit(solution)/shard_map/all_gather | solution.py:786
  166.4 11.1 %fusion.94 = (f32[1088]{0:T(1024)S(1)}, f32[1088,768]{1,0:T(8,128)S(1)}) fusion(f32[768]{0:T(1024)S(1)} %get-tuple-element.309, bf16[1088,3072]{1,0:T(8,128)(2,1)} %get-tuple-element.95, bf16[3072,768]{0,1:T(8,128)(2,1)} %all-gather.15.cloned.1.call-done, f32[768]{0:T(1024)S(1)} %get-tuple-element.310, f32[768]{0:T(1024)S(1)} %get-tuple-element.311, ...), kind=kOutput, calls=%fused_computation.278 | convolution fusion | flops 5139676160 | bytes 18110208 | tf_op jit(solution)/shard_map/dot_general | solution.py:45
  181.0 12.7 %all_to_all.42.cycle_ref = bf16[8,64,128]{2,1,0:T(8,128)(2,1)S(1)} all-to-all(bf16[8,64,128]{2,1,0:T(8,128)(2,1)S(1)} %broadcast_in_dim.131), channel_id=1, replica_groups=mesh['blk'=8,'narrow'=4] {'blk'}, dimensions={0} | all-to-all | bytes 262144 | tf_op jit(solution)/shard_map/all_to_all | solution.py:459
  195.1 9.6 %all_to_all.43.every_ref = f32[8,16,128]{2,1,0:T(8,128)S(1)} all-to-all(f32[8,16,128]{2,1,0:T(8,128)S(1)} %broadcast_in_dim.133), channel_id=1, replica_groups=mesh['blk'=8,'narrow'=4] {'blk'}, dimensions={0} | all-to-all | bytes 131072 | tf_op jit(solution)/shard_map/all_to_all | solution.py:459
  210.8 7.4 %all-to-all-done.4 = f32[8,64,128]{2,1,0:T(8,128)} async-done(((f32[8,64,128]{2,1,0:T(8,128)}), f32[8,64,128]{2,1,0:T(8,128)}, u32[]{:S(2)}, u32[]{:S(2)}) %all-to-all-start.4) | async-done | bytes 262176 | tf_op jit(solution)/shard_map/all_to_all | solution.py:882
  227.8 6.4 fusion.96
  239.4 11.1 %fusion.5 = (f32[3072]{0:T(1024)S(1)}, bf16[1088,3072]{1,0:T(8,128)(2,1)}) fusion(bf16[1088,3072]{1,0:T(8,128)(2,1)} %get-tuple-element.104, bf16[1088,768]{1,0:T(8,128)(2,1)} %copy-done.43, bf16[3072,768]{0,1:T(8,128)(2,1)} %all-gather.15.cloned.1.call-done), kind=kOutput, calls=%fused_computation.11 | convolution fusion | flops 5153879040 | bytes 19771392 | tf_op jit(solution)/shard_map/dot_general | solution.py:49
  250.4 4.4 fusion.13
  254.8 10.4 %fusion.80 = f32[3072,768]{1,0:T(8,128)S(1)} fusion(bf16[1088,3072]{1,0:T(8,128)(2,1)} %get-tuple-element.116, f32[1088,768]{1,0:T(8,128)} %get-tuple-element.322, f32[768]{0:T(1024)S(1)} %get-tuple-element.310, f32[768]{0:T(1024)S(1)} %get-tuple-element.311, f32[1088]{0:T(1024)S(1)} %add_rsqrt_fusion.2, f32[1088]{0:T(1024)S(1)} %broadcast_multiply_fusion.7), kind=kOutput, calls=%fused_computation.271 | convolution fusion | flops 5138006016 | bytes 19479040 | tf_op jit(solution)/shard_map/dot_general | solution.py:53
  270.0 4.1 collective-permute-done.2
  274.1 4.2 add.484
  281.5 10.0 %multiply_reduce_fusion = (f32[768]{0:T(1024)S(1)}, f32[1088]{0:T(1024)S(1)}, f32[1088]{0:T(1024)S(1)}, f32[768]{0:T(1024)S(1)}, f32[1088,768]{1,0:T(8,128)S(1)}) fusion(f32[1088,768]{1,0:T(8,128)} %get-tuple-element.322, f32[1088]{0:T(1024)S(1)} %add_rsqrt_fusion.2, f32[1088]{0:T(1024)S(1)} %broadcast_multiply_fusion.7, f32[768]{0:T(1024)S(1)} %get-tuple-element.311, ...), kind=kOutput, calls=%fused_computation.58 | convolution fusion | flops 5143851008 | bytes 21456896 | tf_op jit(solution)/shard_map/dot_general | solution.py:45
  314.7 29.1 %shard_map.402.qkv_ref = bf16[1088,2304]{1,0:T(8,128)(2,1)} custom-call(s32[2]{0:T(128)S(1)} %bitcast.195, bf16[1088,2304]{1,0:T(8,128)(2,1)} %fusion.7.qkv_ref, bf16[1088,768]{1,0:T(8,128)(2,1)S(1)} %convolution_convert_fusion.5.grad_ref, f32[2,16,544]{2,1,0:T(8,128)S(1)} %pad_maximum_fusion.5.norm_ref, f32[2,16,544]{2,1,0:T(8,128)S(1)} %pad_maximum_fusion.6.inner_ref), custom_call_target="tpu_custom_call" | custom-call | flops 8053063680 | bytes 11698176 | tf_op jit(solution)/shard_map/pallas_call | solution.py:245
  346.9 9.3 %multiply_reduce_fusion.7 = (f32[1088]{0:T(1024)S(1)}, f32[1088]{0:T(1024)S(1)}, f32[1088,768]{1,0:T(8,128)S(1)}) fusion(f32[768]{0:T(1024)S(1)} %get-tuple-element.316, f32[1088,768]{1,0:T(8,128)S(1)} %copy-done.13, f32[1088,768]{1,0:T(8,128)} %copy-done.24, bf16[1088,2304]{1,0:T(8,128)(2,1)} %shard_map.402.qkv_ref, ...), kind=kOutput, calls=%fused_computation.83 | convolution fusion | flops 3856218112 | bytes 18591232 | tf_op jit(solution)/shard_map/dot_general | solution.py:45
  363.3 4.7 all-to-all-start.5
  368.1 7.8 %fusion.49 = f32[2304,768]{1,0:T(8,128)S(1)} fusion(bf16[1088,2304]{1,0:T(8,128)(2,1)} %shard_map.402.qkv_ref, f32[1088,768]{1,0:T(8,128)} %copy-done.11, f32[768]{0:T(1024)S(1)} %copy-done.61, f32[768]{0:T(1024)S(1)} %get-tuple-element.316), kind=kOutput, calls=%fused_computation.136 | convolution fusion | flops 3852877824 | bytes 15439872 | tf_op jit(solution)/shard_map/dot_general | solution.py:53
  380.0 5.6 shard_map.403
  396.1 15.4 %collective-permute-done.12 = f32[192,768]{1,0:T(8,128)} collective-permute-done((f32[192,768]{1,0:T(8,128)}, f32[192,768]{1,0:T(8,128)}, u32[]{:S(2)}, u32[]{:S(2)}) %collective-permute-start.12) | collective-permute-done | bytes 589856 | tf_op jit(solution)/shard_map/ppermute | solution.py:463
  413.4 19.6 %collective-permute-done.9 = bf16[576,768]{1,0:T(8,128)(2,1)} collective-permute-done((bf16[576,768]{1,0:T(8,128)(2,1)}, bf16[576,768]{1,0:T(8,128)(2,1)}, u32[]{:S(2)}, u32[]{:S(2)}) %collective-permute-start.9) | collective-permute-done | bytes 884768 | tf_op jit(solution)/shard_map/ppermute | solution.py:463
  440.6 6.6 multiply_reduce_fusion.6
  447.2 40.3 %all-to-all-done.6 = bf16[8,128,768]{2,1,0:T(8,128)(2,1)S(1)} async-done(((bf16[8,128,768]{2,1,0:T(8,128)(2,1)}), bf16[8,128,768]{2,1,0:T(8,128)(2,1)S(1)}, u32[]{:S(2)}, u32[]{:S(2)}) %all-to-all-start.6) | async-done | bytes 1572896 | tf_op jit(solution)/shard_map/all_to_all | solution.py:978
  534.6 18.1 %collective-permute-done.19 = f32[256,768]{1,0:T(8,128)S(1)} collective-permute-done((f32[256,768]{1,0:T(8,128)S(1)}, f32[256,768]{1,0:T(8,128)S(1)}, u32[]{:S(2)}, u32[]{:S(2)}) %collective-permute-start.19) | collective-permute-done | bytes 786464 | tf_op jit(solution)/shard_map/ppermute | solution.py:463
  557.7 36.7 %shard_map.405 = bf16[384,768]{1,0:T(8,128)(2,1)} custom-call(f32[512,768]{1,0:T(8,128)} %pad_maximum_fusion.1.gram_in, f32[384,768]{1,0:T(8,128)} %constant_dynamic-slice_fusion.rows_in), custom_call_target="tpu_custom_call" | custom-call | flops 35106324480 | bytes 3145728 | tf_op jit(solution)/shard_map/pallas_call | solution.py:716
  594.5 7.3 %multiply_subtract_fusion = (f32[960,768]{1,0:T(8,128)}, f32[960,768]{1,0:T(8,128)}, f32[960,768]{1,0:T(8,128)}) fusion(f32[960,768]{1,0:T(8,128)S(1)} %copy-done.36, f32[960,768]{1,0:T(8,128)} %get-tuple-element.331, f32[]{:T(128)} %min.3, f32[960,768]{1,0:T(8,128)} %param.30, f32[960,768]{1,0:T(8,128)} %param.31), kind=kLoop, calls=%fused_computation.78 | loop fusion | flops 11796480 | bytes 20643844 | tf_op jit(solution)/shard_map/sub | solution.py:602
  632.7 40.7 %all-gather.19.cloned.1.call-done = bf16[3072,768]{1,0:T(8,128)(2,1)} async-done(((bf16[384,768]{1,0:T(8,128)(2,1)}), bf16[3072,768]{1,0:T(8,128)(2,1)}) %all-gather.19.cloned.1.call-update) | async-done | bytes 4718608 | tf_op jit(solution)/shard_map/all_gather | solution.py:1023
  (438 shorter events, 233.2 us)
Async XLA Ops:
  7.2 54.1 %all-gather.9.cloned.1.call-start = ((), (), s32[]{:S(2)}) async-start(), calls=%async_computation.11 | async-start | bytes 2949120 | tf_op jit(solution)/shard_map/all_gather | solution.py:786
  12.3 86.0 %all-gather.11.cloned.1.call-start = ((), (), s32[]{:S(2)}) async-start(), calls=%async_computation.12 | async-start | bytes 4423680 | tf_op jit(solution)/shard_map/all_gather | solution.py:786
  14.9 122.3 %all-gather.13.cloned.1.call-start = ((), (), s32[]{:S(2)}) async-start(), calls=%async_computation.13 | async-start | bytes 5898240 | tf_op jit(solution)/shard_map/all_gather | solution.py:786
  39.4 49.5 %all-to-all-start.1 = ((bf16[32,40,768]{2,1,0:T(8,128)(2,1)}), bf16[32,40,768]{2,1,0:T(8,128)(2,1)}, u32[]{:S(2)}, u32[]{:S(2)}) async-start(bf16[32,40,768]{2,1,0:T(8,128)(2,1)} %bitcast.215), calls=%async_computation.1 | async-start | bytes 3932160 | tf_op jit(solution)/shard_map/all_to_all | solution.py:821
  43.0 123.4 %all-gather.15.cloned.1.call-start = ((), (), s32[]{:S(2)}) async-start(), calls=%async_computation.14 | async-start | bytes 5898240 | tf_op jit(solution)/shard_map/all_gather | solution.py:786
  206.0 12.3 %all-to-all-start.4 = ((f32[8,64,128]{2,1,0:T(8,128)}), f32[8,64,128]{2,1,0:T(8,128)}, u32[]{:S(2)}, u32[]{:S(2)}) async-start(f32[8,64,128]{2,1,0:T(8,128)} %get-tuple-element.101), calls=%async_computation.4 | async-start | bytes 524288 | tf_op jit(solution)/shard_map/all_to_all | solution.py:882
  210.0 92.1 %reduce-scatter.4.cloned.1.call-start = ((), (), s32[]{:S(2)}) async-start(), calls=%async_computation.15 | async-start | bytes 3538944 | tf_op jit(solution)/shard_map/reduce_scatter | solution.py:917
  239.4 11.1 %collective-permute-start = (f32[2,768,768]{2,1,0:T(8,128)}, f32[2,768,768]{2,1,0:T(8,128)}, u32[]{:S(2)}, u32[]{:S(2)}) collective-permute-start(f32[2,768,768]{2,1,0:T(8,128)} %dynamic-slice_bitcast_fusion), channel_id=1, source_target_pairs={{0,1},{1,0},{2,3},{3,2},{4,5},{5,4},{6,7},{7,6},{8,9},{9,8},{10,11... | collective-permute-start | bytes 14155784 | tf_op jit(solution)/shard_map/ppermute | solution.py:463
  269.1 5.0 collective-permute-start.2
  269.6 8.7 %collective-permute-start.1 = (f32[768,768]{1,0:T(8,128)}, f32[768,768]{1,0:T(8,128)}, u32[]{:S(2)}, u32[]{:S(2)}) collective-permute-start(f32[768,768]{1,0:T(8,128)} %get-tuple-element.113), channel_id=1, source_target_pairs={{0,1},{1,0},{2,3},{3,2},{4,5},{5,4},{6,7},{7,6},{8,9},{9,8},{10,11... | collective-permute-start | bytes 7077896 | tf_op jit(solution)/shard_map/ppermute | solution.py:463
  269.6 218.2 %reduce-scatter.6.cloned.1.call-start = ((), (), s32[]{:S(2)}) async-start(), calls=%async_computation.16 | async-start | bytes 2654208 | tf_op jit(solution)/shard_map/reduce_scatter | solution.py:934
  302.1 8.0 %collective-permute-start.3 = (f32[192,768]{1,0:T(8,128)}, f32[192,768]{1,0:T(8,128)}, u32[]{:S(2)}, u32[]{:S(2)}) collective-permute-start(f32[192,768]{1,0:T(8,128)} %get-tuple-element.119), channel_id=1, source_target_pairs={{0,1},{1,0},{2,3},{3,2},{4,5},{5,4},{6,7},{7,6},{8,9},{9,8},{10,11... | collective-permute-start | bytes 1769480 | tf_op jit(solution)/shard_map/ppermute | solution.py:463
  302.2 8.0 %collective-permute-start.4 = (f32[192,768]{1,0:T(8,128)}, f32[192,768]{1,0:T(8,128)}, u32[]{:S(2)}, u32[]{:S(2)}) collective-permute-start(f32[192,768]{1,0:T(8,128)} %get-tuple-element.120), channel_id=1, source_target_pairs={{0,1},{1,0},{2,3},{3,2},{4,5},{5,4},{6,7},{7,6},{8,9},{9,8},{10,11... | collective-permute-start | bytes 1769480 | tf_op jit(solution)/shard_map/ppermute | solution.py:463
  305.0 38.7 %collective-permute-start.5 = (bf16[768,768]{1,0:T(8,128)(2,1)}, bf16[768,768]{1,0:T(8,128)(2,1)}, u32[]{:S(2)}, u32[]{:S(2)}) collective-permute-start(bf16[768,768]{1,0:T(8,128)(2,1)} %add_convert_fusion.1), channel_id=1, source_target_pairs={{0,2},{1,3},{2,0},{3,1},{4,6},{5,7},{6,4},{7,5},{8,10},{9,11},{10,... | collective-permute-start | bytes 3538952 | tf_op jit(solution)/shard_map/ppermute | solution.py:463
  312.9 30.9 %collective-permute-start.6 = (bf16[192,768]{1,0:T(8,128)(2,1)S(1)}, bf16[192,768]{1,0:T(8,128)(2,1)}, u32[]{:S(2)}, u32[]{:S(2)}) collective-permute-start(bf16[192,768]{1,0:T(8,128)(2,1)S(1)} %add_convert_fusion.5), channel_id=1, source_target_pairs={{0,2},{1,3},{2,0},{3,1},{4,6},{5,7},{6,4},{7,5},{8,10},{9,11},{10,... | collective-permute-start | bytes 884744 | tf_op jit(solution)/shard_map/ppermute | solution.py:463
  363.3 73.8 %all-to-all-start.5 = ((bf16[32,40,768]{2,1,0:T(8,128)(2,1)}), bf16[32,40,768]{2,1,0:T(8,128)(2,1)}, u32[]{:S(2)}, u32[]{:S(2)}) async-start(bf16[32,40,768]{2,1,0:T(8,128)(2,1)} %bitcast.214), calls=%async_computation.6 | async-start | bytes 3932160 | tf_op jit(solution)/shard_map/all_to_all | solution.py:959
  368.0 119.9 %reduce-scatter.8.cloned.1.call-start = ((), (), s32[]{:S(2)}) async-start(), calls=%async_computation.17 | async-start | bytes 2654208 | tf_op jit(solution)/shard_map/reduce_scatter | solution.py:953
  379.7 11.5 %collective-permute-start.8 = (f32[576,768]{1,0:T(8,128)}, f32[576,768]{1,0:T(8,128)}, u32[]{:S(2)}, u32[]{:S(2)}) collective-permute-start(f32[576,768]{1,0:T(8,128)} %get-tuple-element.133), channel_id=1, source_target_pairs={{0,1},{1,0},{2,3},{3,2},{4,5},{5,4},{6,7},{7,6},{8,9},{9,8},{10,11... | collective-permute-start | bytes 5308424 | tf_op jit(solution)/shard_map/ppermute | solution.py:463
  387.0 26.4 %collective-permute-start.7 = (f32[576,768]{1,0:T(8,128)}, f32[576,768]{1,0:T(8,128)S(1)}, u32[]{:S(2)}, u32[]{:S(2)}) collective-permute-start(f32[576,768]{1,0:T(8,128)} %get-tuple-element.132), channel_id=1, source_target_pairs={{0,1},{1,0},{2,3},{3,2},{4,5},{5,4},{6,7},{7,6},{8,9},{9,8},{10,11... | collective-permute-start | bytes 5308424 | tf_op jit(solution)/shard_map/ppermute | solution.py:463
  387.2 8.9 %collective-permute-start.10 = (f32[192,768]{1,0:T(8,128)}, f32[192,768]{1,0:T(8,128)S(1)}, u32[]{:S(2)}, u32[]{:S(2)}) collective-permute-start(f32[192,768]{1,0:T(8,128)} %get-tuple-element.293), channel_id=1, source_target_pairs={{0,1},{1,0},{2,3},{3,2},{4,5},{5,4},{6,7},{7,6},{8,9},{9,8},{10,11... | collective-permute-start | bytes 1769480 | tf_op jit(solution)/shard_map/ppermute | solution.py:463
  389.5 22.0 %collective-permute-start.12 = (f32[192,768]{1,0:T(8,128)}, f32[192,768]{1,0:T(8,128)}, u32[]{:S(2)}, u32[]{:S(2)}) collective-permute-start(f32[192,768]{1,0:T(8,128)} %dynamic-slice_add_fusion), channel_id=1, source_target_pairs={{0,2},{1,3},{2,0},{3,1},{4,6},{5,7},{6,4},{7,5},{8,10},{9,11},{10,... | collective-permute-start | bytes 1769480 | tf_op jit(solution)/shard_map/ppermute | solution.py:463
  394.4 38.6 %collective-permute-start.9 = (bf16[576,768]{1,0:T(8,128)(2,1)}, bf16[576,768]{1,0:T(8,128)(2,1)}, u32[]{:S(2)}, u32[]{:S(2)}) collective-permute-start(bf16[576,768]{1,0:T(8,128)(2,1)} %add_convert_fusion.3), channel_id=1, source_target_pairs={{0,2},{1,3},{2,0},{3,1},{4,6},{5,7},{6,4},{7,5},{8,10},{9,11},{10,... | collective-permute-start | bytes 2654216 | tf_op jit(solution)/shard_map/ppermute | solution.py:463
  437.0 50.5 %all-to-all-start.6 = ((bf16[8,128,768]{2,1,0:T(8,128)(2,1)}), bf16[8,128,768]{2,1,0:T(8,128)(2,1)S(1)}, u32[]{:S(2)}, u32[]{:S(2)}) async-start(bf16[8,128,768]{2,1,0:T(8,128)(2,1)} %pad_maximum_fusion), calls=%async_computation.7 | async-start | bytes 3145728 | tf_op jit(solution)/shard_map/all_to_all | solution.py:978
  492.6 33.8 %all-to-all-start.7 = ((bf16[8,96,768]{2,1,0:T(8,128)(2,1)}), bf16[8,96,768]{2,1,0:T(8,128)(2,1)S(1)}, u32[]{:S(2)}, u32[]{:S(2)}) async-start(bf16[8,96,768]{2,1,0:T(8,128)(2,1)} %bitcast.53), calls=%async_computation.10 | async-start | bytes 2359296 | tf_op jit(solution)/shard_map/all_to_all | solution.py:994
  496.2 98.2 %all-gather.17.cloned.1.call-start = ((), (), s32[]{:S(2)}) async-start(), calls=%async_computation.18 | async-start | bytes 4313088 | tf_op jit(solution)/shard_map/all_gather | solution.py:1016
  511.7 4.6 collective-permute-start.16
  516.3 8.8 %collective-permute-start.17 = (f32[8,128]{1,0:T(8,128)S(1)}, f32[8,128]{1,0:T(8,128)S(1)}, u32[]{:S(2)}, u32[]{:S(2)}) collective-permute-start(f32[8,128]{1,0:T(8,128)S(1)} %add.514), channel_id=1, source_target_pairs={{0,16},{4,20},{8,24},{12,28},{16,0},{20,4},{24,8},{28,12},{1,17},{... | collective-permute-start | bytes 12296 | tf_op jit(solution)/shard_map/ppermute | solution.py:463
  521.0 152.3 %all-gather.19.cloned.1.call-start = ((), (), s32[]{:S(2)}) async-start(), calls=%async_computation.19 | async-start | bytes 5308416 | tf_op jit(solution)/shard_map/all_gather | solution.py:1023
  533.0 19.6 %collective-permute-start.19 = (f32[256,768]{1,0:T(8,128)S(1)}, f32[256,768]{1,0:T(8,128)S(1)}, u32[]{:S(2)}, u32[]{:S(2)}) collective-permute-start(f32[256,768]{1,0:T(8,128)S(1)} %bitcast_add_fusion.5), channel_id=1, source_target_pairs={{0,2},{1,3},{2,0},{3,1},{4,6},{5,7},{6,4},{7,5},{8,10},{9,11},{10,... | collective-permute-start | bytes 2359304 | tf_op jit(solution)/shard_map/ppermute | solution.py:463
  601.9 18.4 %collective-permute-start.22 = (bf16[128,192]{0,1:T(8,128)(2,1)S(1)}, bf16[128,192]{0,1:T(8,128)(2,1)S(1)}, u32[]{:S(2)}, u32[]{:S(2)}) collective-permute-start(bf16[128,192]{0,1:T(8,128)(2,1)S(1)} %get-tuple-element.300), channel_id=1, source_target_pairs={{0,2},{1,3},{2,0},{3,1},{4,6},{5,7},{6,4},{7,5},{8,10},{9,11},{10,... | collective-permute-start | bytes 147464 | tf_op jit(solution)/shard_map/ppermute | solution.py:463
  603.5 16.8 %collective-permute-start.21 = (bf16[128,192]{0,1:T(8,128)(2,1)S(1)}, bf16[128,192]{0,1:T(8,128)(2,1)S(1)}, u32[]{:S(2)}, u32[]{:S(2)}) collective-permute-start(bf16[128,192]{0,1:T(8,128)(2,1)S(1)} %get-tuple-element.300), channel_id=1, source_target_pairs={{0,1},{1,0},{2,3},{3,2},{4,5},{5,4},{6,7},{7,6},{8,9},{9,8},{10,11... | collective-permute-start | bytes 147464 | tf_op jit(solution)/shard_map/ppermute | solution.py:463
  603.8 15.9 %collective-permute-start.24 = (f32[64,128]{1,0:T(8,128)S(1)}, f32[64,128]{1,0:T(8,128)S(1)}, u32[]{:S(2)}, u32[]{:S(2)}) collective-permute-start(f32[64,128]{1,0:T(8,128)S(1)} %dynamic-slice_bitcast_fusion.2), channel_id=1, source_target_pairs={{0,1},{1,0},{2,3},{3,2},{4,5},{5,4},{6,7},{7,6},{8,9},{9,8},{10,11... | collective-permute-start | bytes 98312 | tf_op jit(solution)/shard_map/ppermute | solution.py:463
  (78 other events, 675.4 us)
Sparse Core Ops, SparseCore 0:
  12.4 26.9 all-gather.8
  41.6 46.3 all-gather.10
  90.1 36.7 all-gather.12
  128.9 37.4 all-gather.14
  269.7 32.3 reduce-scatter.3
  307.1 72.9 reduce-scatter.5
  391.4 94.5 reduce-scatter.7
  521.2 66.9 all-gather.16
  594.5 78.7 all-gather.18
